TPU v7x, 128 devices: a whole 4x4x4 slice. The times are simulated.
128 devices in a mesh: dp: 16 (over x, y), row: 2 (over z_hi), col: 4 (over z_lo, core).
Axes of the slice: x: 4, y: 4, z: 4 (z_hi: 2, z_lo: 2; z = z_hi * 2 + z_lo), core: 2. Of those that a mesh axis runs over, the one named last changes fastest.
Arguments:
- tokens: bfloat16 [16384, 2048], P(('dp', 'row'), 'col'), may hold values from -6 to 6
- norm1_gain: float32 [2048], P('col'), may hold values from 0.5 to 1.5
- w_qkv: bfloat16 [2048, 8, 512], P('col', 'row'), may hold values from -0.125 to 0.125
- q_gain: float32 [128], replicated, may hold values from 0.1 to 1.9
- k_gain: float32 [128], replicated, may hold values from 0.1 to 1.9
- w_out: bfloat16 [2048, 2048], P('row', 'col'), may hold values from -0.5 to 0.5
- norm2_gain: float32 [2048], P('col'), may hold values from 0.5 to 1.5
- w_gate_up: bfloat16 [2048, 2, 6144], P('col', None, 'row'), may hold values from -0.125 to 0.125
- w_down: bfloat16 [6144, 2048], P('row', 'col'), may hold values from -0.078125 to 0.078125
- out_grad: bfloat16 [16384, 2048], P(('dp', 'row'), 'col'), may hold values from -6 to 6
- seq_lengths: int32 [64], replicated, may hold values from 1 to 1021, as said below
- seq_group: int32 [64], replicated, may hold values from 0 to 15, as said below
- seq_start: int32 [64], replicated, may hold values from 0 to 1023, as said below
Outputs:
- layer_out: bfloat16 [16384, 2048], P(('dp', 'row'), 'col')
- grad_tokens: float32 [16384, 2048], P(('dp', 'row'), 'col')
- grad_norm1_gain: float32 [2048], replicated
- grad_w_qkv: float32 [2048, 8, 512], P('col', 'row')
- grad_q_gain: float32 [128], replicated
- grad_k_gain: float32 [128], replicated
- grad_w_out: float32 [2048, 2048], P('row', 'col')
- grad_norm2_gain: float32 [2048], replicated
- grad_w_gate_up: float32 [2048, 2, 6144], P('col', None, 'row')
- grad_w_down: float32 [6144, 2048], P('row', 'col')
Inputs may be any that keep to these rules, and one draw needn't show every extreme that they name: `seq_lengths`: the lengths of the 4 sequences of one group sum to 1024. `seq_group`: each group holds 4 sequences. `seq_start`: the sequences of one group lie end to end over its slots 0 to 1023 without gaps, in some order.
All inputs are finite; a program needn't handle non-finite values.
Results may differ from a plain program's by a relative error of at most 0.02.
Values may be sent and summed in bfloat16 or wider, within the bound.
A program may use at most 192 MiB of HBM per device.

v0:
```python
import math

import jax
import jax.numpy as jnp
from jax import lax
from jax.sharding import PartitionSpec as P

EPS = 1e-06
THETA = 1000000.0


def rms_norm(value, gain):
    return value * lax.rsqrt(jnp.mean(value * value, axis=-1, keepdims=True) + EPS) * gain


def rotate(value, cosine, sine):
    half = value.shape[-1] // 2
    first = value[..., :half]
    second = value[..., half:]
    return jnp.concatenate(
        [first * cosine - second * sine, second * cosine + first * sine], axis=-1
    )


def layout(seq_lengths, seq_group, seq_start, group_index, slots_count):
    slots = jnp.arange(slots_count, dtype=jnp.int32)
    inside = (
        (seq_group[None, :] == group_index)
        & (seq_start[None, :] <= slots[:, None])
        & (slots[:, None] < (seq_start + seq_lengths)[None, :])
    )
    labels = jnp.arange(1, seq_lengths.shape[0] + 1, dtype=jnp.int32)
    segment = jnp.sum(jnp.where(inside, labels[None, :], 0), axis=1)
    offset = jnp.sum(jnp.where(inside, seq_start[None, :], 0), axis=1)
    return (segment, slots, slots - offset)


def angles(position, head):
    half = head // 2
    freq = THETA ** (-(jnp.arange(half, dtype=jnp.float32) * 2.0 / head))
    angle = position.astype(jnp.float32)[:, None] * freq[None, :]
    return (jnp.cos(angle), jnp.sin(angle))


def col_total(value):
    return lax.psum(value, "col")


def norm_forward(value, gain, width):
    total = col_total(jnp.sum(value * value, axis=1))
    scale = lax.rsqrt(total / width + EPS)
    return (value * scale[:, None] * gain, scale)


def norm_backward(grad, value, scale, gain, width):
    inner = col_total(jnp.sum(grad * gain * value, axis=1))
    gain_grad = jnp.sum(grad * value * scale[:, None], axis=0)
    back = scale[:, None] * gain * grad - value * (scale * scale * scale * inner / width)[:, None]
    return (back, gain_grad)


def row_gather(value):
    return lax.all_gather(value, "row", axis=0, tiled=True)


def col_gather(value):
    return lax.all_gather(value, "col", axis=0, tiled=True)


def product(block, weight, flip):
    if flip:
        return lax.dot_general(
            block, weight, (((1,), (1,)), ((), ())), preferred_element_type=jnp.float32
        )
    return jnp.dot(block, weight, preferred_element_type=jnp.float32)


def contract_rows(left, right):
    return lax.dot_general(
        left, right, (((0,), (0,)), ((), ())), preferred_element_type=jnp.float32
    )


def col_sum(gathered, weight, flip):
    return lax.psum_scatter(product(gathered, weight, flip), "col", scatter_dimension=0, tiled=True)


def row_sum(gathered, weight, flip):
    return lax.psum_scatter(
        product(gathered, weight, flip).astype(jnp.bfloat16), "row", scatter_dimension=0, tiled=True
    ).astype(jnp.float32)


def to_heads(value):
    return lax.all_to_all(value, "col", split_axis=1, concat_axis=0, tiled=True)


def to_tokens(value):
    return lax.all_to_all(value, "col", split_axis=0, concat_axis=1, tiled=True)


def masked_scores(query, keys, seg_q, seg_k, slot_q, slot_k):
    scale = 1.0 / math.sqrt(query.shape[-1])
    score = jnp.einsum("qhd,kd->qhk", query, keys, preferred_element_type=jnp.float32) * scale
    allowed = (seg_q[:, None] == seg_k[None, :]) & (slot_k[None, :] <= slot_q[:, None])
    return jnp.where(allowed[:, None, :], score, -1e30)


def attend_forward(query, keys, values, segment, slots):
    block = query.shape[0] // 2
    outputs = []
    totals = []
    for part_index in range(2):
        begin = part_index * block
        score = masked_scores(
            query[begin : begin + block],
            keys,
            segment[begin : begin + block],
            segment,
            slots[begin : begin + block],
            slots,
        )
        peak = jnp.max(score, axis=-1, keepdims=True)
        weight = jnp.exp(score - peak)
        total = jnp.sum(weight, axis=-1, keepdims=True)
        prob = weight / total
        outputs.append(
            jnp.einsum(
                "qhk,kd->qhd", prob.astype(jnp.bfloat16), values, preferred_element_type=jnp.float32
            )
        )
        totals.append((peak + jnp.log(total))[..., 0])
    return (jnp.concatenate(outputs, axis=0), jnp.concatenate(totals, axis=0))


def attend_backward(query, keys, values, segment, slots, log_total, grad_out):
    block = query.shape[0] // 2
    scale = 1.0 / math.sqrt(query.shape[-1])
    key_grad = jnp.zeros(keys.shape, jnp.float32)
    value_grad = jnp.zeros(values.shape, jnp.float32)
    query_grads = []
    for part_index in range(2):
        begin = part_index * block
        query_part = query[begin : begin + block]
        grad_part = grad_out[begin : begin + block]
        score = masked_scores(
            query_part,
            keys,
            segment[begin : begin + block],
            segment,
            slots[begin : begin + block],
            slots,
        )
        prob = jnp.exp(score - log_total[begin : begin + block][:, :, None])
        prob_grad = jnp.einsum("qhd,kd->qhk", grad_part, values, preferred_element_type=jnp.float32)
        delta = jnp.sum(prob_grad * prob, axis=-1, keepdims=True)
        score_grad = (prob * (prob_grad - delta)).astype(jnp.bfloat16)
        query_grads.append(
            jnp.einsum("qhk,kd->qhd", score_grad, keys, preferred_element_type=jnp.float32) * scale
        )
        key_grad = (
            key_grad
            + jnp.einsum("qhk,qhd->kd", score_grad, query_part, preferred_element_type=jnp.float32)
            * scale
        )
        value_grad = value_grad + jnp.einsum(
            "qhk,qhd->kd", prob.astype(jnp.bfloat16), grad_part, preferred_element_type=jnp.float32
        )
    return (jnp.concatenate(query_grads, axis=0), key_grad, value_grad)


def body(
    tokens,
    norm1_gain,
    w_qkv,
    q_gain,
    k_gain,
    w_out,
    norm2_gain,
    w_gate_up,
    w_down,
    out_grad,
    seq_lengths,
    seq_group,
    seq_start,
):
    half_rows, col_width = tokens.shape
    group = half_rows * lax.axis_size("row")
    width = col_width * lax.axis_size("col")
    head = q_gain.shape[0]
    units_half = w_down.shape[0]
    segment, slots, position = layout(
        seq_lengths, seq_group, seq_start, lax.axis_index("dp"), group
    )
    cosine, sine = angles(position, head)
    stream = tokens.astype(jnp.float32)
    weight_qkv = w_qkv.reshape(col_width, -1)
    weight_gate_up = w_gate_up.reshape(col_width, -1)
    normed, scale_one = norm_forward(stream, norm1_gain, width)
    normed_low = normed.astype(jnp.bfloat16)
    normed_all = row_gather(normed_low)
    mixed = col_sum(normed_all, weight_qkv, False)
    heads_low = to_heads(mixed.astype(jnp.bfloat16)).reshape(group, 4, head)

    def prepare(heads_float, gain_q, gain_k):
        query = rotate(rms_norm(heads_float[:, 0:2], gain_q), cosine[:, None], sine[:, None])
        keys = rotate(rms_norm(heads_float[:, 2], gain_k), cosine, sine)
        return (query, keys)

    (query_float, key_float), prepare_back = jax.vjp(
        prepare, heads_low.astype(jnp.float32), q_gain, k_gain
    )
    query_low = query_float.astype(jnp.bfloat16)
    key_low = key_float.astype(jnp.bfloat16)
    value_low = heads_low[:, 3]
    attended, log_total = attend_forward(query_low, key_low, value_low, segment, slots)
    attended_low = attended.astype(jnp.bfloat16).reshape(group, 2 * head)
    attended_tok = to_tokens(attended_low)
    attended_all = col_gather(attended_tok)
    branch = row_sum(attended_all, w_out, False)
    middle = stream + branch
    normed_two, scale_two = norm_forward(middle, norm2_gain, width)
    normed_two_low = normed_two.astype(jnp.bfloat16)
    normed_two_all = row_gather(normed_two_low)
    gate_up = col_sum(normed_two_all, weight_gate_up, False)

    def swiglu(pair):
        return jax.nn.silu(pair[:, :units_half]) * pair[:, units_half:]

    hidden, swiglu_back = jax.vjp(swiglu, gate_up)
    hidden_low = hidden.astype(jnp.bfloat16)
    hidden_all = col_gather(hidden_low)
    result = middle + row_sum(hidden_all, w_down, False)
    incoming = out_grad.astype(jnp.float32)
    incoming_all = row_gather(incoming.astype(jnp.bfloat16))
    grad_down = contract_rows(hidden_all, incoming_all)
    hidden_grad = col_sum(incoming_all, w_down, True)
    (pair_grad,) = swiglu_back(hidden_grad)
    pair_grad_all = col_gather(pair_grad.astype(jnp.bfloat16))
    grad_gate_up = contract_rows(normed_two_all, pair_grad_all)
    normed_two_grad = row_sum(pair_grad_all, weight_gate_up, True)
    middle_norm_grad, gain_two_grad = norm_backward(
        normed_two_grad, middle, scale_two, norm2_gain, width
    )
    middle_grad = incoming + middle_norm_grad
    middle_all = row_gather(middle_grad.astype(jnp.bfloat16))
    grad_out = contract_rows(attended_all, middle_all)
    attended_grad = col_sum(middle_all, w_out, True)
    head_grad = to_heads(attended_grad.astype(jnp.bfloat16)).reshape(group, 2, head)
    query_grad, key_grad, value_grad = attend_backward(
        query_low, key_low, value_low, segment, slots, log_total, head_grad
    )
    heads_grad, gain_q_grad, gain_k_grad = prepare_back((query_grad, key_grad))
    heads_grad = jnp.concatenate([heads_grad[:, :3], value_grad[:, None]], axis=1)
    heads_tok = to_tokens(heads_grad.astype(jnp.bfloat16).reshape(group, 4 * head))
    heads_all = col_gather(heads_tok)
    grad_qkv = contract_rows(normed_all, heads_all)
    normed_grad = row_sum(heads_all, weight_qkv, True)
    stream_norm_grad, gain_one_grad = norm_backward(
        normed_grad, stream, scale_one, norm1_gain, width
    )
    stream_grad = middle_grad + stream_norm_grad
    col_ids = jnp.arange(lax.axis_size("col"), dtype=jnp.int32)
    here = (col_ids == lax.axis_index("col"))[None, :, None]
    spread = jnp.where(here, jnp.stack([gain_one_grad, gain_two_grad])[:, None, :], 0.0)
    norm_sums, head_sums = lax.psum(
        (spread, jnp.stack([gain_q_grad, gain_k_grad])), ("dp", "row", "col")
    )
    grad_qkv, grad_out, grad_gate_up, grad_down = (
        lax.psum(grad_qkv.astype(jnp.bfloat16), "dp").astype(jnp.float32),
        lax.psum(grad_out.astype(jnp.bfloat16), "dp").astype(jnp.float32),
        lax.psum(grad_gate_up.astype(jnp.bfloat16), "dp").astype(jnp.float32),
        lax.psum(grad_down.astype(jnp.bfloat16), "dp").astype(jnp.float32),
    )
    return (
        result.astype(jnp.bfloat16),
        stream_grad,
        norm_sums[0].reshape(-1),
        grad_qkv.reshape(w_qkv.shape),
        head_sums[0],
        head_sums[1],
        grad_out,
        norm_sums[1].reshape(-1),
        grad_gate_up.reshape(w_gate_up.shape),
        grad_down,
    )


def solution(mesh):
    in_specs = (
        P(("dp", "row"), "col"),
        P("col"),
        P("col", "row", None),
        P(),
        P(),
        P("row", "col"),
        P("col"),
        P("col", None, "row"),
        P("row", "col"),
        P(("dp", "row"), "col"),
        P(),
        P(),
        P(),
    )
    out_specs = (
        P(("dp", "row"), "col"),
        P(("dp", "row"), "col"),
        P(),
        P("col", "row", None),
        P(),
        P(),
        P("row", "col"),
        P(),
        P("col", None, "row"),
        P("row", "col"),
    )
    return jax.shard_map(body, mesh=mesh, in_specs=in_specs, out_specs=out_specs, check_vma=False)
```

profile of v0, /device:TPU:0, one launch (start us, length us, event | category | flops | bytes accessed | tf_op | source)
XLA Modules:
  0.0 1338.1 jit_solution(1859835301627462793)
XLA Ops:
  8.6 7.4 psum.70
  22.2 24.0 %all-gather.9.cloned.1.call-done = bf16[1024,512]{1,0:T(8,128)(2,1)} async-done(((bf16[512,512]{1,0:T(8,128)(2,1)}), bf16[1024,512]{1,0:T(8,128)(2,1)}) %all-gather.9.cloned.1.call-update) | async-done | bytes 1048592 | tf_op jit(solution)/shard_map/all_gather | solution.py:63
  46.2 7.7 fusion.93
  54.8 77.6 %reduce-scatter.9.cloned.1.call-done = f32[256,2048]{1,0:T(8,128)} async-done(((f32[1024,2048]{1,0:T(8,128)}), f32[256,2048]{1,0:T(8,128)}) %reduce-scatter.9.cloned.1.call-update) | async-done | bytes 2097168 | tf_op jit(solution)/shard_map/reduce_scatter | solution.py:85
  141.8 12.2 all-to-all-done
  183.5 11.9 all_to_all.64
  198.1 28.7 %all-gather.11.cloned.1.call-done = bf16[1024,1024]{0,1:T(8,128)(2,1)} async-done(((bf16[256,1024]{0,1:T(8,128)(2,1)}), bf16[1024,1024]{0,1:T(8,128)(2,1)}) %all-gather.11.cloned.1.call-update) | async-done | bytes 2097168 | tf_op jit(solution)/shard_map/all_gather | solution.py:67
  231.6 25.8 %reduce-scatter.11.cloned.1.call-done = bf16[512,512]{1,0:T(8,128)(2,1)} async-done(((bf16[1024,512]{1,0:T(8,128)(2,1)}), bf16[512,512]{1,0:T(8,128)(2,1)}) %reduce-scatter.11.cloned.1.call-update) | async-done | bytes 524304 | tf_op jit(solution)/shard_map/reduce_scatter | solution.py:89
  267.1 16.5 %all-gather.17.cloned.1.call-done = bf16[1024,512]{1,0:T(8,128)(2,1)} async-done(((bf16[512,512]{1,0:T(8,128)(2,1)}), bf16[1024,512]{1,0:T(8,128)(2,1)}) %all-gather.17.cloned.1.call-update) | async-done | bytes 1048592 | tf_op jit(solution)/shard_map/all_gather | solution.py:63
  283.7 7.8 fusion.95
  291.6 7.4 copy.107
  299.0 11.6 all-gather.13.cloned.1.call-done
  310.6 14.7 %fusion.94 = f32[1024,6144]{1,0:T(8,128)} fusion(bf16[1024,512]{1,0:T(8,128)(2,1)} %all-gather.13.cloned.1.call-done, bf16[512,6144]{1,0:T(8,128)(2,1)} %bitcast.123), kind=kOutput, calls=%fused_computation.181 | convolution fusion | flops 6442450944 | bytes 32505856 | tf_op jit(solution)/shard_map/dot_general | solution.py:75
  325.4 100.7 %reduce-scatter.17.cloned.1.call-done = f32[256,3072]{1,0:T(8,128)} async-done(((f32[1024,3072]{1,0:T(8,128)}), f32[256,3072]{1,0:T(8,128)}) %reduce-scatter.17.cloned.1.call-update) | async-done | bytes 3145744 | tf_op jit(solution)/shard_map/reduce_scatter | solution.py:85
  426.1 217.8 %reduce-scatter.13.cloned.1.call-done = f32[256,6144]{1,0:T(8,128)} async-done(((f32[1024,6144]{1,0:T(8,128)}), f32[256,6144]{1,0:T(8,128)}) %reduce-scatter.13.cloned.1.call-update) | async-done | bytes 6291472 | tf_op jit(solution)/shard_map/reduce_scatter | solution.py:85
  651.6 115.6 %all-gather.19.cloned.1.call-done = bf16[1024,6144]{1,0:T(8,128)(2,1)} async-done(((bf16[256,6144]{1,0:T(8,128)(2,1)}), bf16[1024,6144]{1,0:T(8,128)(2,1)}) %all-gather.19.cloned.1.call-update) | async-done | bytes 12582928 | tf_op jit(solution)/shard_map/all_gather | solution.py:67
  767.2 12.3 convolution_convert_fusion.3
  779.7 27.2 %reduce-scatter.19.cloned.1.call-done = bf16[512,512]{1,0:T(8,128)(2,1)} async-done(((bf16[1024,512]{1,0:T(8,128)(2,1)}), bf16[512,512]{1,0:T(8,128)(2,1)}) %reduce-scatter.19.cloned.1.call-update) | async-done | bytes 524304 | tf_op jit(solution)/shard_map/reduce_scatter | solution.py:89
  817.6 25.6 %all-gather.21.cloned.1.call-done = bf16[1024,512]{1,0:T(8,128)(2,1)} async-done(((bf16[512,512]{1,0:T(8,128)(2,1)}), bf16[1024,512]{1,0:T(8,128)(2,1)}) %all-gather.21.cloned.1.call-update) | async-done | bytes 1048592 | tf_op jit(solution)/shard_map/all_gather | solution.py:63
  848.0 44.8 %reduce-scatter.21.cloned.1.call-done = f32[256,1024]{1,0:T(8,128)} async-done(((f32[1024,1024]{1,0:T(8,128)}), f32[256,1024]{1,0:T(8,128)}) %reduce-scatter.21.cloned.1.call-update) | async-done | bytes 1048592 | tf_op jit(solution)/shard_map/reduce_scatter | solution.py:85
  899.2 8.8 all-to-all-done.2
  939.8 18.8 %all_to_all.65 = bf16[4,256,512]{2,1,0:T(8,128)(2,1)} all-to-all(bf16[4,256,512]{2,1,0:T(8,128)(2,1)} %convert_element_type.142), channel_id=1, replica_groups=mesh['dp'=16,'row'=2,'col'=4] {'col'}, dimensions={0} | all-to-all | bytes 2097152 | tf_op jit(solution)/shard_map/all_to_all | solution.py:99
  961.5 46.5 %all-gather.23.cloned.1.call-done = bf16[1024,2048]{0,1:T(8,128)(2,1)} async-done(((bf16[256,2048]{0,1:T(8,128)(2,1)}), bf16[1024,2048]{0,1:T(8,128)(2,1)}) %all-gather.23.cloned.1.call-update) | async-done | bytes 4194320 | tf_op jit(solution)/shard_map/all_gather | solution.py:67
  1007.9 6.2 convolution_convert_fusion.6
  1014.2 59.8 %all-gather.15.cloned.1.call-done = bf16[1024,3072]{1,0:T(8,128)(2,1)} async-done(((bf16[256,3072]{1,0:T(8,128)(2,1)}), bf16[1024,3072]{1,0:T(8,128)(2,1)}) %all-gather.15.cloned.1.call-update) | async-done | bytes 6291472 | tf_op jit(solution)/shard_map/all_gather | solution.py:67
  1074.0 7.2 convolution_convert_fusion.7
  1081.7 8.3 convolution_convert_fusion.1
  1090.0 13.2 convolution_convert_fusion
  1103.2 14.6 %reshape.299 = bf16[512,2,3072]{2,1,0:T(2,128)(2,1)} reshape(bf16[512,6144]{1,0:T(8,128)(2,1)} %convolution_convert_fusion) | data formatting | bytes 12582912 | tf_op jit(solution)/shard_map/reshape | solution.py:284
  1132.8 70.8 %all-reduce.8 = (f32[2,4,512]{2,1,0:T(4,128)S(1)}, f32[2,128]{1,0:T(2,128)S(1)}) all-reduce(f32[2,4,512]{2,1,0:T(4,128)S(1)} %broadcast_select_fusion, f32[2,128]{1,0:T(2,128)S(1)} %pad_maximum_fusion.5), channel_id=1, replica_groups=mesh['dp'=16,'row'=2,'col'=4] {'dp','row','col'}, use_global_device_ids=true, to_apply=%region_30.31 | all-reduce | flops 4352 | bytes 34816 | tf_op jit(solution)/shard_map/psum | solution.py:266
  1215.2 99.2 %all-reduce.12.cloned.1.call-done = (bf16[512,4,512]{2,1,0:T(4,128)(2,1)}, bf16[1024,512]{1,0:T(8,128)(2,1)}, bf16[512,2,3072]{2,1,0:T(2,128)(2,1)}, bf16[3072,512]{1,0:T(8,128)(2,1)}) async-done(((bf16[512,4,512]{2,1,0:T(4,128)(2,1)}, bf16[1024,512]{1,0:T(8,128)(2,1)}, bf16[512,2,3072]{2,1,0:T(2,128)(2,1)}, bf16[3072,512]{1,0:T(8,128)(2,1)}), (bf16[512,4,512]{2,1,0:T(4,128)(2,1)}, ...) | async-done | bytes 12582928 | tf_op jit(solution)/shard_map/psum | solution.py:270
  1314.4 9.2 reshape.300
  (224 shorter events, 163.5 us)
Async XLA Ops:
  7.2 276.5 %copy-start = (bf16[3072,512]{1,0:T(8,128)(2,1)S(1)}, bf16[3072,512]{1,0:T(8,128)(2,1)}, u32[]{:S(2)}) copy-start(bf16[3072,512]{1,0:T(8,128)(2,1)} %param.21) | copy-start | bytes 9437188
  7.2 39.0 %all-gather.9.cloned.1.call-start = ((), (), s32[]{:S(2)}) async-start(), calls=%async_computation.12 | async-start | bytes 1572864 | tf_op jit(solution)/shard_map/all_gather | solution.py:63
  16.0 37.9 %copy-start.32 = (f32[512]{0:T(512)}, f32[512]{0:T(512)S(1)}, u32[]{:S(2)}) copy-start(f32[512]{0:T(512)S(1)} %psum.70) | copy-start | bytes 6148
  18.7 113.7 %reduce-scatter.9.cloned.1.call-start = ((), (), s32[]{:S(2)}) async-start(), calls=%async_computation.13 | async-start | bytes 10485760 | tf_op jit(solution)/shard_map/reduce_scatter | solution.py:85
  135.2 18.8 %all-to-all-start = ((bf16[256,4,512]{2,0,1:T(8,128)(2,1)}), bf16[256,4,512]{2,0,1:T(8,128)(2,1)}, u32[]{:S(2)}, u32[]{:S(2)}) async-start(bf16[256,4,512]{2,0,1:T(8,128)(2,1)} %bitcast.126), calls=%async_computation.1 | async-start | bytes 2097152 | tf_op jit(solution)/shard_map/all_to_all | solution.py:95
  139.4 87.4 %all-gather.11.cloned.1.call-start = ((), (), s32[]{:S(2)}) async-start(), calls=%async_computation.14 | async-start | bytes 2621440 | tf_op jit(solution)/shard_map/all_gather | solution.py:67
  154.0 8.6 copy-start.34
  156.1 7.7 copy-start.35
  165.4 4.0 copy-start.24
  197.5 67.3 %copy-start.30 = (f32[512]{0:T(512)S(1)}, f32[512]{0:T(512)}, u32[]{:S(2)}) copy-start(f32[512]{0:T(512)} %param.19) | copy-start | bytes 6148
  197.5 59.8 %reduce-scatter.11.cloned.1.call-start = ((), (), s32[]{:S(2)}) async-start(), calls=%async_computation.15 | async-start | bytes 1572864 | tf_op jit(solution)/shard_map/reduce_scatter | solution.py:89
  230.9 52.7 %all-gather.17.cloned.1.call-start = ((), (), s32[]{:S(2)}) async-start(), calls=%async_computation.20 | async-start | bytes 1572864 | tf_op jit(solution)/shard_map/all_gather | solution.py:63
  231.5 79.1 %all-gather.13.cloned.1.call-start = ((), (), s32[]{:S(2)}) async-start(), calls=%async_computation.16 | async-start | bytes 1572864 | tf_op jit(solution)/shard_map/all_gather | solution.py:63
  267.1 159.0 %reduce-scatter.17.cloned.1.call-start = ((), (), s32[]{:S(2)}) async-start(), calls=%async_computation.21 | async-start | bytes 15728640 | tf_op jit(solution)/shard_map/reduce_scatter | solution.py:85
  291.5 352.4 %reduce-scatter.13.cloned.1.call-start = ((), (), s32[]{:S(2)}) async-start(), calls=%async_computation.17 | async-start | bytes 31457280 | tf_op jit(solution)/shard_map/reduce_scatter | solution.py:85
  325.3 441.8 %all-gather.19.cloned.1.call-start = ((), (), s32[]{:S(2)}) async-start(), calls=%async_computation.22 | async-start | bytes 15728640 | tf_op jit(solution)/shard_map/all_gather | solution.py:67
  651.5 155.3 %reduce-scatter.19.cloned.1.call-start = ((), (), s32[]{:S(2)}) async-start(), calls=%async_computation.23 | async-start | bytes 1572864 | tf_op jit(solution)/shard_map/reduce_scatter | solution.py:89
  779.5 63.7 %all-gather.21.cloned.1.call-start = ((), (), s32[]{:S(2)}) async-start(), calls=%async_computation.24 | async-start | bytes 1572864 | tf_op jit(solution)/shard_map/all_gather | solution.py:63
  817.5 75.3 %reduce-scatter.21.cloned.1.call-start = ((), (), s32[]{:S(2)}) async-start(), calls=%async_computation.25 | async-start | bytes 5242880 | tf_op jit(solution)/shard_map/reduce_scatter | solution.py:85
  894.9 13.1 all-to-all-start.2
  899.1 108.8 %all-gather.23.cloned.1.call-start = ((), (), s32[]{:S(2)}) async-start(), calls=%async_computation.26 | async-start | bytes 5242880 | tf_op jit(solution)/shard_map/all_gather | solution.py:67
  920.9 3.6 copy-start.22
  960.8 113.2 %all-gather.15.cloned.1.call-start = ((), (), s32[]{:S(2)}) async-start(), calls=%async_computation.18 | async-start | bytes 7864320 | tf_op jit(solution)/shard_map/all_gather | solution.py:67
  961.4 169.0 %reduce-scatter.23.cloned.1.call-start = ((), (), s32[]{:S(2)}) async-start(), calls=%async_computation.27 | async-start | bytes 1572864 | tf_op jit(solution)/shard_map/reduce_scatter | solution.py:89
  1014.2 197.3 %reduce-scatter.15.cloned.1.call-start = ((), (), s32[]{:S(2)}) async-start(), calls=%async_computation.19 | async-start | bytes 1572864 | tf_op jit(solution)/shard_map/reduce_scatter | solution.py:89
  1081.3 233.1 %all-reduce.12.cloned.1.call-start = ((), (), s32[]{:S(2)}) async-start(), calls=%async_computation.28 | async-start | bytes 25165824 | tf_op jit(solution)/shard_map/psum | solution.py:270
  1081.7 8.3 copy-start.39
  1117.8 4.3 copy-start.37
  1117.8 4.3 copy-start.38
  1130.3 81.1 %copy-start.33 = (f32[512]{0:T(512)S(1)}, f32[512]{0:T(512)}, u32[]{:S(2)}) copy-start(f32[512]{0:T(512)} %copy-done.32) | copy-start | bytes 6148
  1314.4 9.2 copy-start.18
  1323.5 3.6 copy-start.23
  (29 other events, 63.1 us)
Sparse Core Ops, SparseCore 0:
  18.8 27.4 all-gather.8
  54.0 78.2 reduce-scatter.8
  197.6 29.1 all-gather.10
  231.1 26.2 reduce-scatter.10
  258.9 24.6 all-gather.16
  285.9 24.6 all-gather.12
  313.8 112.2 reduce-scatter.16
  428.7 215.1 reduce-scatter.12
  651.7 115.4 all-gather.18
  779.6 27.2 reduce-scatter.18
  817.6 25.5 all-gather.20
  848.2 44.6 reduce-scatter.20
  960.9 46.9 all-gather.22
  1009.4 64.5 all-gather.14
  1076.8 26.2 reduce-scatter.22
  1105.4 23.6 reduce-scatter.14
  1134.2 180.1 all-reduce.11
where the time goes:
time: 1340 us
  waiting for transfers between devices  944 us (70%)
  blocking collectives  127 us (9%)
  matrix products  115 us (9%)
  other arithmetic  66.9 us (5%)
  local copies, waits for them, and re-layouts  59.9 us (4%)
  between operations  14.8 us (1%)
    reduce_scatter x4, waiting for transfers between devices, col_sum(): lax.psum_scatter(product(gathered, weight, flip), 'col', scatter_dimensio...  441 us
    all_gather x4, waiting for transfers between devices, col_gather(): return lax.all_gather(value, 'col', axis=0, tiled=True)  251 us
    psum x1, waiting for transfers between devices, body(): lax.psum(grad_qkv.astype(jnp.bfloat16), 'dp').astype(jnp.float32)  99.2 us
    all_gather x4, waiting for transfers between devices, row_gather(): return lax.all_gather(value, 'row', axis=0, tiled=True)  77.7 us
    psum x1, blocking collectives, body(): lax.psum((spread, jnp.stack([gain_q_grad, gain_k_grad])), ('dp', 'row', '...  70.8 us
    reduce_scatter x4, waiting for transfers between devices, row_sum(): lax.psum_scatter(product(gathered, weight, flip).astype(jnp.bfloat16), 'r...  53 us
    dot_general x4, matrix products, product(): return jnp.dot(block, weight, preferred_element_type=jnp.float32)  33.7 us
    dot_general x4, matrix products, product(): lax.dot_general(block, weight, (((1,), (1,)), ((), ())), preferred_elemen...  31.2 us
  transfers between devices with their start and end apart: 19, of which 17 were waited for; matrix products, arithmetic and copies ran while one was open for 8% of the time, Pallas kernels for 0%

commit v1 on v0

v1 whole, which is shorter than its diff:
```python
import math

import jax
import jax.numpy as jnp
from jax import lax
from jax.experimental import pallas as pl
from jax.experimental.pallas import tpu as pltpu
from jax.sharding import PartitionSpec as P

EPS = 1e-06
THETA = 1000000.0
BF = jnp.bfloat16
F32 = jnp.float32
Z = ("row", "col")
MESH = pl.DeviceIdType.MESH
VMEM_LIMIT = 60 * 1024 * 1024

GROUP, WIDTH, TILE, UNITS, HEAD = 1024, 2048, 512, 768, 128
OWN = GROUP // 8
DP = 16


def dot(left, right, dims):
    return lax.dot_general(left, right, (dims, ((), ())), preferred_element_type=F32)


def mm(left, right):
    return dot(left, right, ((1,), (0,)))


def mm_t(left, right):
    return dot(left, right, ((1,), (1,)))


def t_mm(left, right):
    return dot(left, right, ((0,), (0,)))


def place():
    row, col = lax.axis_index("row"), lax.axis_index("col")
    j = 4 * row + col
    return lax.axis_index("dp"), row, col, j // 2, j % 2


def on_ring(z, k):
    j = 2 * z + k
    return {"row": j // 4, "col": j % 4}


def remote(src, dst, send, recv, device):
    return pltpu.make_async_remote_copy(
        src_ref=src, dst_ref=dst, send_sem=send, recv_sem=recv, device_id=device, device_id_type=MESH
    )


def meet(devices):
    barrier = pltpu.get_barrier_semaphore()
    for device in devices:
        pl.semaphore_signal(barrier, inc=1, device_id=device, device_id_type=MESH)
    pl.semaphore_wait(barrier, len(devices))


def ring_friends():
    _, _, _, z, k = place()
    other = z + 1 - 2 * (z % 2)
    return [
        on_ring((z + 1) % 4, k),
        on_ring((z + 3) % 4, k),
        on_ring(z, 1 - k),
        on_ring(other, 1 - k),
    ]


def dp_friends():
    p = lax.axis_index("dp")
    return [{"dp": (p + o) % DP} for o in range(1, DP)]


def tile_at(buf):
    def loc(j, half=None):
        row, col = j // 4, j % 4
        first = pl.multiple_of(row * TILE, TILE)
        rows = pl.ds(first, TILE)
        if half is not None:
            rows = pl.ds(first + half * (TILE // 2), TILE // 2)
        return buf.at[rows, pl.ds(pl.multiple_of(col * TILE, TILE), TILE)]

    return loc


def rows_at(buf):
    def loc(j, half=None):
        first = pl.multiple_of(j * OWN, OWN)
        rows = pl.ds(first, OWN)
        if half is not None:
            rows = pl.ds(first + half * (OWN // 2), OWN // 2)
        return buf.at[rows]

    return loc


class Gather:
    def __init__(self, loc, send, recv, own=None):
        _, _, _, z, k = place()
        up, down, far = (z + 1) % 4, (z + 3) % 4, (z + 2) % 4
        to_up, to_down, peer = on_ring(up, k), on_ring(down, k), on_ring(z, 1 - k)

        def out(slot, src, dst, device):
            return remote(src, dst, send.at[slot], recv.at[slot], device)

        def into(slot, dst):
            return remote(dst, dst, send.at[slot], recv.at[slot], peer)

        mine = loc(2 * z + k)
        own = mine if own is None else own
        left, right, across = 2 * down + k, 2 * up + k, 2 * far + k
        self.first = [out(0, own, mine, to_up), out(1, own, mine, to_down), out(4, own, mine, peer)]
        self.from_left = [
            out(2, loc(left, 0), loc(left, 0), to_up),
            out(5, loc(left), loc(left), peer),
        ]
        self.from_right = [
            out(3, loc(right, 1), loc(right, 1), to_down),
            out(6, loc(right), loc(right), peer),
        ]
        self.from_far = [
            out(7, loc(across, 0), loc(across, 0), peer),
            out(8, loc(across, 1), loc(across, 1), peer),
        ]
        theirs = [2 * z + 1 - k, 2 * down + 1 - k, 2 * up + 1 - k, 2 * far + 1 - k]
        self.arrivals = {
            0: into(0, loc(left)),
            1: into(1, loc(right)),
            2: into(2, loc(across, 0)),
            3: into(3, loc(across, 1)),
            4: into(4, loc(theirs[0])),
            5: into(5, loc(theirs[1])),
            6: into(6, loc(theirs[2])),
            7: into(7, loc(theirs[3], 0)),
            8: into(8, loc(theirs[3], 1)),
        }

    def start(self):
        for copy in self.first:
            copy.start()

    def forward(self):
        self.arrivals[0].wait_recv()
        for copy in self.from_left:
            copy.start()
        self.arrivals[1].wait_recv()
        for copy in self.from_right:
            copy.start()

    def share(self):
        for half in range(2):
            self.arrivals[2 + half].wait_recv()
            self.from_far[half].start()

    def finish(self):
        for slot in range(4, 9):
            self.arrivals[slot].wait_recv()

    def drain(self):
        for copy in self.first + self.from_left + self.from_right + self.from_far:
            copy.wait_send()


GATHER_SEMS = [pltpu.SemaphoreType.DMA((9,)), pltpu.SemaphoreType.DMA((9,))]


class Scatter:
    def __init__(self, parts, theirs, sums, near, full, send, recv):
        _, _, _, z, k = place()
        self.parts, self.theirs, self.sums, self.near, self.full = parts, theirs, sums, near, full
        self.k = k
        to_up, to_down = on_ring((z + 1) % 4, k), on_ring((z + 3) % 4, k)
        peer = on_ring(z, 1 - k)
        half = OWN // 2
        other = pl.ds(pl.multiple_of((1 - k) * OWN, OWN), OWN)

        def copy(slot, src, dst, device):
            return remote(src, dst, send.at[slot], recv.at[slot], device)

        self.copies = [copy(d, parts.at[d, other], theirs.at[d], peer) for d in range(4)] + [
            copy(4, sums.at[0, pl.ds(0, half)], near.at[0], to_up),
            copy(5, sums.at[0, pl.ds(half, half)], near.at[1], to_down),
            copy(6, sums.at[1], full.at[0], to_up),
            copy(7, sums.at[2], full.at[1], to_down),
        ]

    def put(self, d):
        self.copies[d].start()

    def own(self, d, rows, count):
        first = pl.multiple_of(self.k * OWN + rows, count)
        return self.parts[d, pl.ds(first, count)].astype(F32) + self.theirs[
            d, pl.ds(rows, count)
        ].astype(F32)

    def across(self):
        self.copies[2].wait_recv()

        @pl.loop(0, OWN // 16)
        def _(i):
            rows = pl.multiple_of(i * 16, 16)
            self.sums[0, pl.ds(rows, 16)] = self.own(2, rows, 16).astype(BF)

        self.copies[4].start()
        self.copies[5].start()

    def beside(self, side):
        d, half = (1, 3)[side], OWN // 2
        self.copies[d].wait_recv()
        self.copies[4 + side].wait_recv()

        @pl.loop(0, half // 16)
        def _(i):
            rows = pl.multiple_of(i * 16, 16)
            here = pl.multiple_of(rows + side * half, 16)
            there = pl.multiple_of(rows + (1 - side) * half, 16)
            added = self.own(d, here, 16) + self.near[side, pl.ds(rows, 16)].astype(F32)
            self.sums[1 + side, pl.ds(here, 16)] = added.astype(BF)
            self.sums[1 + side, pl.ds(there, 16)] = self.own(d, there, 16).astype(BF)

        self.copies[6 + side].start()

    def arrive(self):
        self.copies[0].wait_recv()
        self.copies[6].wait_recv()
        self.copies[7].wait_recv()

    def total(self, rows, count):
        return (
            self.own(0, rows, count)
            + self.full[0, pl.ds(rows, count)].astype(F32)
            + self.full[1, pl.ds(rows, count)].astype(F32)
        )

    def drain(self):
        for copy in self.copies:
            copy.wait_send()


def scatter_scratch():
    return [
        pltpu.VMEM((4, 2 * OWN, WIDTH), BF),
        pltpu.VMEM((4, OWN, WIDTH), BF),
        pltpu.VMEM((3, OWN, WIDTH), BF),
        pltpu.VMEM((2, OWN // 2, WIDTH), BF),
        pltpu.VMEM((2, OWN, WIDTH), BF),
        pltpu.SemaphoreType.DMA((8,)),
        pltpu.SemaphoreType.DMA((8,)),
    ]


def head_norm(value):
    return lax.rsqrt(jnp.mean(value * value, axis=1, keepdims=True) + EPS)


def turn(value, cosine, sine):
    return value * cosine + pltpu.roll(value, HEAD // 2, 1) * sine


def turn_back(value, cosine, sine):
    return value * cosine - pltpu.roll(value, HEAD // 2, 1) * sine


LOG2 = math.log2(math.e)
SCALE = 1.0 / math.sqrt(HEAD)
QROWS = 256


def allowed_keys(start, first, keys):
    slots = lax.broadcasted_iota(jnp.int32, (QROWS, keys), 1)
    query = lax.broadcasted_iota(jnp.int32, (QROWS, keys), 0) + first
    return (slots >= start) & (slots <= query)


def forward_kernel(
    tok, og, gains, q_gain, k_gain, start, cosine, sine, wq_pair, wq_part, wg_pair, wg_part, w_out, w_down,
    h2_o, g_o, wq_o, wo_o, wg_o, wd_o, h1_o, raw_o, q_o, k_o, att_o, lse_o, mid_o, gain_o, x_o,
    x, h1, h2, g, wq, wo, raw, qs, ks, att, lse, mid, gain,
    xs, xr, gs, gr, hs, hr,
    parts, theirs, sums, near, full, rs_s, rs_r,
    zs, zr, ps, pr, ys, yr, ns, nr, loc_s, out_s,
):
    p, row, col, z, k = place()
    me = 2 * z + k
    lo = z % 2
    other = z + 1 - 2 * lo
    peer = on_ring(z, 1 - k)
    meet(ring_friends() + dp_friends())

    gain[col] = gains[...]
    gain_copies = [
        remote(gains, gain.at[col], ns.at[i], nr.at[col], device)
        for i, device in enumerate([peer, on_ring(other, k), on_ring(other, 1 - k)])
    ]
    for copy in gain_copies:
        copy.start()

    def part(weight, rows, index):
        return weight.at[:, pl.ds(pl.multiple_of(index * rows, 16), rows)]

    rows_of = [32, 16, 32, 48]
    weights = [wq, wo, wg_o, wd_o]

    def crossing(a, kk):
        target = 2 * (1 - lo) + kk
        src = [
            wq_part.at[kk],
            w_out.at[pl.ds(pl.multiple_of(target * 256 + p * 16, 16), 16)],
            wg_part.at[kk],
            w_down.at[pl.ds(pl.multiple_of(target * UNITS + p * 48, 16), 48)],
        ][a]
        dst = weights[a].at[col, pl.ds(pl.multiple_of(p * rows_of[a], 16), rows_of[a])]
        return remote(src, dst, zs.at[a, kk], zr.at[a, k], on_ring(other, kk))

    def crossed(a, kk):
        source = 2 * (1 - lo) + kk
        dst = weights[a].at[source, pl.ds(pl.multiple_of(p * rows_of[a], 16), rows_of[a])]
        return remote(dst, dst, zs.at[a, kk], zr.at[a, kk], peer)

    def beside(a):
        src = [
            lambda c, kk: wq_pair.at[kk],
            lambda c, kk: w_out.at[pl.ds(pl.multiple_of(c * 256, 256), 256)],
            lambda c, kk: wg_pair.at[kk],
            lambda c, kk: w_down.at[pl.ds(pl.multiple_of(c * UNITS, 256), UNITS)],
        ][a]
        there = 2 * lo + 1 - k
        keep = pltpu.make_async_copy(src(col, k), weights[a].at[col], loc_s.at[a])
        give = remote(src(there, 1 - k), weights[a].at[col], ps.at[a], pr.at[a], peer)
        take = remote(weights[a].at[there], weights[a].at[there], ps.at[a], pr.at[a], peer)
        return keep, give, take

    def spread(a, o):
        q = (p + o) % DP
        pair = pl.ds(2 * (1 - lo), 2)
        rows = rows_of[a]
        mine = weights[a].at[pair, pl.ds(pl.multiple_of(p * rows, 16), rows)]
        arriving = weights[a].at[pair, pl.ds(pl.multiple_of(q * rows, 16), rows)]
        send = remote(mine, mine, ys.at[a, q], yr.at[a, p], {"dp": q})
        take = remote(arriving, arriving, ys.at[a, q], yr.at[a, q], {"dp": q})
        return send, take

    def spread_start(a):
        @pl.loop(1, DP)
        def _(o):
            spread(a, o)[0].start()

    def spread_wait(a):
        @pl.loop(1, DP)
        def _(o):
            send, take = spread(a, o)
            take.wait_recv()
            send.wait_send()

    for a in (0, 1):
        for kk in range(2):
            crossing(a, kk).start()
    x_gather = Gather(tile_at(x), xs, xr, tok)
    x_gather.start()
    for a in range(2):
        beside(a)[0].start()
        beside(a)[1].start()
    keep_x = pltpu.make_async_copy(tok, tile_at(x)(me), loc_s.at[4])
    keep_x.start()
    keep_g = pltpu.make_async_copy(og, tile_at(g)(me), loc_s.at[5])
    keep_g.start()
    for a in (0, 1):
        for kk in range(2):
            crossed(a, kk).wait_recv()
        spread_start(a)
    for a in (2, 3):
        beside(a)[0].start()
        beside(a)[1].start()
    x_gather.forward()
    for a in (2, 3):
        for kk in range(2):
            crossing(a, kk).start()
    x_gather.share()
    g_gather = Gather(tile_at(g), gs, gr, og)
    g_gather.start()
    for c in range(4):

        @pl.when(c != col)
        def _():
            remote(gain.at[c], gain.at[c], ns.at[0], nr.at[c], peer).wait_recv()

    keep_x.wait()
    x_gather.finish()
    for a in (2, 3):
        for kk in range(2):
            crossed(a, kk).wait_recv()
        spread_start(a)

    def gain_row(which):
        return jnp.concatenate([gain[c, which : which + 1] for c in range(4)], axis=1)

    gain_one = gain_row(0)

    @pl.loop(0, GROUP // 64)
    def _(i):
        rows = pl.ds(pl.multiple_of(i * 64, 64), 64)
        value = x[rows].astype(F32)
        h1[rows] = (value * head_norm(value) * gain_one).astype(BF)

    for a in range(2):
        keep, _, take = beside(a)
        keep.wait()
        take.wait_recv()
        spread_wait(a)

    @pl.loop(0, GROUP // 256)
    def _(i):
        rows = pl.ds(pl.multiple_of(i * 256, 256), 256)
        mixed = mm(h1[rows], wq[...].reshape(WIDTH, 4 * HEAD)).astype(BF)
        raw[rows] = mixed
        cos_rows, sin_rows = cosine[rows], sine[rows]
        for piece in range(3):
            value = mixed[:, piece * HEAD : (piece + 1) * HEAD].astype(F32)
            by = q_gain[...] if piece < 2 else k_gain[...]
            turned = turn(value * head_norm(value) * by, cos_rows, sin_rows).astype(BF)
            if piece < 2:
                qs[piece, rows] = turned
            else:
                ks[rows] = turned

    g_gather.forward()
    saves = [
        pltpu.make_async_copy(src, dst, out_s.at[i])
        for i, (src, dst) in enumerate(
            [
                (h1, h1_o), (wq, wq_o), (raw, raw_o), (qs, q_o), (ks, k_o), (gain, gain_o),
                (x.at[pl.ds(pl.multiple_of(me * OWN, OWN), OWN)], x_o), (wo, wo_o),
                (att, att_o), (lse, lse_o), (g, g_o), (mid, mid_o), (h2, h2_o),
            ]
        )
    ]
    for i in range(8):
        saves[i].start()

    for block in range(GROUP // QROWS):
        first, keys = block * QROWS, (block + 1) * QROWS
        rows = pl.ds(first, QROWS)
        allowed = allowed_keys(start[rows], first, keys)

        @pl.loop(0, 2)
        def _(h):
            score = mm_t(qs[h, rows], ks[:keys]) * (SCALE * LOG2)
            score = jnp.where(allowed, score, -1e30)
            peak = jnp.max(score, axis=1, keepdims=True)
            weight = jnp.exp2(score - peak)
            total = jnp.sum(weight, axis=1, keepdims=True)
            out = mm(weight.astype(BF), raw[:keys, 3 * HEAD :]) / total
            att[h, rows] = out.astype(BF)
            lse[h, rows] = jnp.broadcast_to(peak + jnp.log2(total), (QROWS, HEAD))

    saves[8].start()
    saves[9].start()
    g_gather.share()

    scatter = Scatter(parts, theirs, sums, near, full, rs_s, rs_r)

    def project(d):
        rows = pl.ds(pl.multiple_of((z + d) % 4 * 256, 256), 256)
        left = jnp.concatenate([att[0, rows], att[1, rows]], axis=1)
        for c in range(4):
            parts[d, :, c * TILE : (c + 1) * TILE] = mm(left, wo[c]).astype(BF)
        scatter.put(d)

    project(2)
    project(1)
    scatter.across()
    project(3)
    project(0)
    scatter.beside(0)
    scatter.beside(1)
    g_gather.finish()
    keep_g.wait()
    saves[10].start()
    scatter.arrive()
    gain_two = gain_row(1)

    @pl.loop(0, OWN // 16)
    def _(i):
        first = pl.multiple_of(i * 16, 16)
        there = pl.ds(pl.multiple_of(me * OWN + first, 16), 16)
        value = x[there].astype(F32) + scatter.total(first, 16)
        mid[pl.ds(first, 16)] = value
        h2[there] = (value * head_norm(value) * gain_two).astype(BF)

    saves[11].start()
    h2_gather = Gather(rows_at(h2), hs, hr)
    h2_gather.start()
    h2_gather.forward()
    for a in (2, 3):
        keep, _, take = beside(a)
        keep.wait()
        take.wait_recv()
        spread_wait(a)
    h2_gather.share()
    h2_gather.finish()
    saves[12].start()
    for copy in gain_copies:
        copy.wait_send()
    for a in range(4):
        beside(a)[1].wait_send()
        for kk in range(2):
            crossing(a, kk).wait_send()
    x_gather.drain()
    g_gather.drain()
    h2_gather.drain()
    scatter.drain()
    for copy in saves:
        copy.wait()


def forward_call(tok, og, gains, q_gain, k_gain, start, cosine, sine, wq_pair, wq_part, wg_pair, wg_part, w_out, w_down):
    hbm = pl.BlockSpec(memory_space=pl.ANY)
    vmem = pl.BlockSpec(memory_space=pltpu.VMEM)
    dma = pltpu.SemaphoreType.DMA

    def out(shape, dtype=BF):
        return jax.ShapeDtypeStruct(shape, dtype)

    wide = (GROUP, WIDTH)
    return pl.pallas_call(
        forward_kernel,
        out_shape=[
            out(wide), out(wide), out((4, TILE, 512)), out((4, 256, TILE)), out((4, TILE, 2 * UNITS)),
            out((4, UNITS, TILE)), out(wide), out((GROUP, 512)), out((2, GROUP, HEAD)), out((GROUP, HEAD)),
            out((2, GROUP, HEAD)), out((2, GROUP, HEAD), F32), out((OWN, WIDTH), F32), out((4, 8, TILE), F32),
            out((OWN, WIDTH)),
        ],
        in_specs=[vmem] * 8 + [hbm] * 6,
        out_specs=[hbm] * 15,
        scratch_shapes=[
            pltpu.VMEM(wide, BF), pltpu.VMEM(wide, BF), pltpu.VMEM(wide, BF), pltpu.VMEM(wide, BF),
            pltpu.VMEM((4, TILE, 512), BF), pltpu.VMEM((4, 256, TILE), BF), pltpu.VMEM((GROUP, 512), BF),
            pltpu.VMEM((2, GROUP, HEAD), BF), pltpu.VMEM((GROUP, HEAD), BF), pltpu.VMEM((2, GROUP, HEAD), BF),
            pltpu.VMEM((2, GROUP, HEAD), F32), pltpu.VMEM((OWN, WIDTH), F32), pltpu.VMEM((4, 8, TILE), F32),
        ]
        + GATHER_SEMS * 3
        + scatter_scratch()
        + [dma((4, 2)), dma((4, 2)), dma((4,)), dma((4,)), dma((4, DP)), dma((4, DP)), dma((3,)), dma((4,)), dma((6,)), dma((13,))],
        compiler_params=pltpu.CompilerParams(
            collective_id=1, has_side_effects=True, vmem_limit_bytes=VMEM_LIMIT
        ),
        cost_estimate=pl.CostEstimate(flops=4_000_000_000, bytes_accessed=60_000_000, transcendentals=2_000_000),
        name="forward",
    )(tok, og, gains, q_gain, k_gain, start, cosine, sine, wq_pair, wq_part, wg_pair, wg_part, w_out, w_down)


def middle_kernel(h2, g, wg, wd, grads, ggu, hid, h2_t):
    @pl.when(pl.program_id(0) == 0)
    def _():
        @pl.loop(0, 8)
        def _(i):
            cols = pl.ds(pl.multiple_of(i * 256, 256), 256)
            h2_t[cols] = h2[:, cols].T

    @pl.loop(0, GROUP // 256)
    def _(i):
        rows = pl.ds(pl.multiple_of(i * 256, 256), 256)
        pair = mm(h2[rows], wg[...].reshape(WIDTH, 512))
        back = mm_t(g[rows, :TILE], wd[0])
        for c in range(1, 4):
            back += mm_t(g[rows, c * TILE : (c + 1) * TILE], wd[c])
        gate, up = pair[:, :256], pair[:, 256:]
        sig = 1.0 / (1.0 + jnp.exp(-gate))
        silu = gate * sig
        hid[rows] = (silu * up).astype(BF)
        ggu[rows, :256] = (back * up * sig * (1.0 + gate * (1.0 - sig))).astype(BF)
        ggu[rows, 256:] = (back * silu).astype(BF)

    hid_t = hid[...].T

    @pl.loop(0, 4)
    def _(c):
        cols = pl.ds(pl.multiple_of(c * TILE, TILE), TILE)
        up_grad = mm(h2_t[cols], ggu[...]).astype(BF).reshape(DP, 1, 32, 512)
        down_grad = mm(hid_t, g[:, cols]).astype(BF).reshape(DP, 1, 16, 512)
        grads[:, 0, pl.ds(c, 1), :32] = up_grad
        grads[:, 0, pl.ds(c, 1), 32:] = down_grad


def middle_call(h2, g, wg, wd):
    once = pl.Buffered(1)
    wide = pl.BlockSpec((GROUP, WIDTH), lambda u: (0, 0), pipeline_mode=once)
    return pl.pallas_call(
        middle_kernel,
        grid=(3,),
        out_shape=[
            jax.ShapeDtypeStruct((DP, 3, 4, 48, 512), BF),
            jax.ShapeDtypeStruct((GROUP, 2 * UNITS), BF),
            jax.ShapeDtypeStruct((GROUP, UNITS), BF),
        ],
        in_specs=[
            wide,
            wide,
            pl.BlockSpec((4, TILE, 512), lambda u: (0, 0, u)),
            pl.BlockSpec((4, 256, TILE), lambda u: (0, u, 0)),
        ],
        out_specs=[
            pl.BlockSpec((DP, 1, 4, 48, 512), lambda u: (0, u, 0, 0, 0)),
            pl.BlockSpec((GROUP, 512), lambda u: (0, u)),
            pl.BlockSpec((GROUP, 256), lambda u: (0, u)),
        ],
        scratch_shapes=[pltpu.VMEM((WIDTH, GROUP), BF)],
        compiler_params=pltpu.CompilerParams(vmem_limit_bytes=VMEM_LIMIT),
        cost_estimate=pl.CostEstimate(flops=19_000_000_000, bytes_accessed=32_000_000, transcendentals=800_000),
        name="feed_forward",
    )(h2, g, wg, wd)


def starts_of(seq_lengths, seq_group, seq_start, group_index):
    slots = jnp.arange(GROUP, dtype=jnp.int32)
    inside = (
        (seq_group[None, :] == group_index)
        & (seq_start[None, :] <= slots[:, None])
        & (slots[:, None] < (seq_start + seq_lengths)[None, :])
    )
    return (jnp.sum(jnp.where(inside, seq_start[None, :], 0), axis=1), slots)


def angles(position):
    half = HEAD // 2
    freq = THETA ** (-(jnp.arange(half, dtype=F32) * 2.0 / HEAD))
    angle = position.astype(F32)[:, None] * freq[None, :]
    return (jnp.cos(angle), jnp.sin(angle))


def exchange(piece):
    return lax.all_to_all(piece, "col", split_axis=0, concat_axis=0, tiled=True)


def scatter_rows(partial):
    return lax.psum_scatter(partial.astype(BF), Z, scatter_dimension=0, tiled=True).astype(F32)


def gather_rows(block):
    return lax.all_gather(block, Z, axis=0, tiled=True)


def rows_to_tile(block):
    return lax.all_to_all(block, "col", split_axis=1, concat_axis=0, tiled=True)


def norm_backward(grad, value, scale, gain):
    inner = jnp.sum(grad * gain * value, axis=1, keepdims=True)
    gain_grad = jnp.sum(grad * value * scale, axis=0)
    back = scale * gain * grad - value * (scale * scale * scale * inner / value.shape[1])
    return (back, gain_grad)


def head_backward(grad, value, gain, cosine, sine):
    half = HEAD // 2
    first, second = grad[:, :half], grad[:, half:]
    grad = jnp.concatenate([first * cosine + second * sine, second * cosine - first * sine], axis=1)
    scale = lax.rsqrt(jnp.mean(value * value, axis=1, keepdims=True) + EPS)
    return norm_backward(grad, value, scale, gain)


def body(
    tokens, norm1_gain, w_qkv, q_gain, k_gain, w_out, norm2_gain, w_gate_up, w_down, out_grad,
    seq_lengths, seq_group, seq_start,
):
    me = lax.axis_index("row") * 4 + lax.axis_index("col")
    p = lax.axis_index("dp")
    lo = lax.axis_index("col") // 2
    start, slots = starts_of(seq_lengths, seq_group, seq_start, p)
    cosine, sine = angles(slots - start)
    cos_wide = jnp.concatenate([cosine, cosine], axis=1)
    sin_wide = jnp.concatenate([-sine, sine], axis=1)
    gains = jnp.concatenate([norm1_gain[None], norm2_gain[None], jnp.zeros((6, TILE), F32)])

    def pair(weight, index, cut):
        return lax.dynamic_index_in_dim(weight, index, cut, keepdims=False)

    wq5 = w_qkv.reshape(TILE, 2, 2, 512)
    wq_pair = pair(wq5, lo, 1).transpose(1, 0, 2)
    wq_part = pair(lax.dynamic_slice_in_dim(wq5, p * 32, 32, 0), 1 - lo, 1).transpose(1, 0, 2)
    wg7 = w_gate_up.reshape(TILE, 2, 2, 2, 3, 256)

    def order(block):
        return block.transpose(2, 0, 3, 1, 4).reshape(2, -1, 2 * UNITS)

    wg_pair = order(pair(wg7, lo, 2))
    wg_part = order(pair(lax.dynamic_slice_in_dim(wg7, p * 32, 32, 0), 1 - lo, 2))

    (h2, g, wq, wo, wg, wd, h1, raw, qs, ks, att, lse, middle, gain, x_own) = forward_call(
        tokens, out_grad, gains, q_gain[None], k_gain[None], start[:, None], cos_wide, sin_wide,
        wq_pair, wq_part, wg_pair, wg_part, w_out, w_down,
    )
    gain_one = gain[:, 0].reshape(1, WIDTH)
    gain_two = gain[:, 1].reshape(1, WIDTH)
    big, ggu, hid = middle_call(h2, g, wg, wd)
    big = lax.psum_scatter(big, "dp", scatter_dimension=0, tiled=False)

    wd2 = wd.transpose(1, 0, 2).reshape(UNITS, WIDTH)
    wo2 = wo.transpose(1, 0, 2).reshape(256, WIDTH)
    result = rows_to_tile((middle + scatter_rows(mm(hid, wd2))).astype(BF))
    scale_two = lax.rsqrt(jnp.mean(middle * middle, axis=1, keepdims=True) + EPS)
    back, gain_two_grad = norm_backward(
        scatter_rows(mm_t(ggu, wg.reshape(WIDTH, 2 * UNITS))), middle, scale_two, gain_two
    )
    middle_grad = lax.dynamic_slice_in_dim(g, me * OWN, OWN, 0).astype(F32) + back
    middle_all = gather_rows(middle_grad.astype(BF))
    att2 = jnp.concatenate([att[0], att[1]], axis=1)
    g_out = t_mm(att2, middle_all).astype(BF)
    head_grad = mm_t(middle_all, wo2).astype(BF).reshape(GROUP, 2, HEAD).transpose(1, 0, 2)
    value_low = raw[:, 3 * HEAD :]
    allowed = (slots[None, :] >= start[:, None]) & (slots[None, :] <= slots[:, None])
    key_grad, value_grad, pieces, gain_q_grad = 0.0, 0.0, [], 0.0
    for h in range(2):
        score = jnp.where(allowed, mm_t(qs[h], ks) * (SCALE * LOG2), -1e30)
        prob = jnp.exp2(score - lse[h, :, :1])
        prob_grad = mm_t(head_grad[h], value_low)
        delta = jnp.sum(prob_grad * prob, axis=-1, keepdims=True)
        score_grad = (prob * (prob_grad - delta)).astype(BF)
        key_grad += t_mm(score_grad, qs[h]) * SCALE
        value_grad += t_mm(prob.astype(BF), head_grad[h])
        piece, gain_grad = head_backward(
            mm(score_grad, ks) * SCALE, raw[:, h * HEAD : (h + 1) * HEAD].astype(F32), q_gain, cosine, sine
        )
        gain_q_grad += gain_grad
        pieces.append(piece)
    piece, gain_k_grad = head_backward(
        key_grad, raw[:, 2 * HEAD : 3 * HEAD].astype(F32), k_gain, cosine, sine
    )
    heads_grad = jnp.concatenate(pieces + [piece, value_grad], axis=1).astype(BF)
    g_qkv = t_mm(h1, heads_grad).astype(BF)
    small = jnp.concatenate(
        [
            g_qkv.reshape(4, DP, 32, 512).transpose(1, 0, 2, 3),
            g_out.reshape(DP, 16, 4, 512).transpose(0, 2, 1, 3),
        ],
        axis=2,
    )
    small = lax.psum_scatter(small, "dp", scatter_dimension=0, tiled=False)
    x_float = x_own.astype(F32)
    scale_one = lax.rsqrt(jnp.mean(x_float * x_float, axis=1, keepdims=True) + EPS)
    back, gain_one_grad = norm_backward(
        scatter_rows(mm_t(heads_grad, wq.reshape(WIDTH, 512))), x_float, scale_one, gain_one
    )
    stream_grad = rows_to_tile(middle_grad + back)
    totals = lax.psum(
        jnp.concatenate([gain_one_grad, gain_two_grad, gain_q_grad, gain_k_grad]),
        ("dp", "row", "col"),
    )
    big = lax.all_gather(exchange(big.transpose(1, 0, 2, 3)), "dp", axis=0)
    small = lax.all_gather(exchange(small), "dp", axis=0)
    g_gate_up = big[:, :, :, :32].reshape(DP, 4, 3, 32, 2, 256).transpose(0, 3, 4, 1, 2, 5)
    g_down = big[:, :, :, 32:].transpose(1, 2, 0, 3, 4)
    g_qkv = small[:, :, :32].transpose(0, 2, 1, 3)
    g_out = small[:, :, 32:].transpose(1, 0, 2, 3)
    return (
        result,
        stream_grad,
        totals[:WIDTH],
        g_qkv.reshape(w_qkv.shape).astype(F32),
        totals[2 * WIDTH : 2 * WIDTH + HEAD],
        totals[2 * WIDTH + HEAD :],
        g_out.reshape(w_out.shape).astype(F32),
        totals[WIDTH : 2 * WIDTH],
        g_gate_up.reshape(w_gate_up.shape).astype(F32),
        g_down.reshape(w_down.shape).astype(F32),
    )


def solution(mesh):
    in_specs = (
        P(("dp", "row"), "col"),
        P("col"),
        P("col", "row", None),
        P(),
        P(),
        P("row", "col"),
        P("col"),
        P("col", None, "row"),
        P("row", "col"),
        P(("dp", "row"), "col"),
        P(),
        P(),
        P(),
    )
    out_specs = (
        P(("dp", "row"), "col"),
        P(("dp", "row"), "col"),
        P(),
        P("col", "row", None),
        P(),
        P(),
        P("row", "col"),
        P(),
        P("col", None, "row"),
        P("row", "col"),
    )
    return jax.shard_map(body, mesh=mesh, in_specs=in_specs, out_specs=out_specs, check_vma=False)
```

time: 1340 us -> 827 us (0.62)
  waiting for transfers between devices: 944 us -> 325 us
  Pallas kernels: 0 us -> 155 us
  local copies, waits for them, and re-layouts: 59.9 us -> 135 us
  matrix products: 115 us -> 47 us
  blocking collectives: 127 us -> 93.9 us
  other arithmetic: 66.9 us -> 42.3 us
    reduce_scatter x8 -> x3, waiting for transfers between devices: 494 us -> 119 us  [scatter_rows(): lax.psum_scatter(partial.astype(BF), Z, scatter_dimension=0, tiled=True)]
    all_gather x8 -> x3, waiting for transfers between devices: 328 us -> 43 us  [the longest x1 24.3 us: body(): big = lax.all_gather(exchange(big.transpose(1, 0, 2, 3)), 'dp', axis=0)]
    pallas_call x0 -> x2, Pallas kernels: none -> 155 us  [the longest x1 111 us: forward_call(): pl.pallas_call(forward_kernel, out_shape=[out(wide), out(wide), out((4, T...]
    unnamed x17 -> x10, waiting for transfers between devices: 1.3 us -> 156 us
    psum x1 -> x0, waiting for transfers between devices: 99.2 us -> none  [body(): lax.psum(grad_qkv.astype(jnp.bfloat16), 'dp').astype(jnp.float32)]
    dot_general x24 -> x16, matrix products: 115 us -> 47 us  [dot(): lax.dot_general(left, right, (dims, ((), ())), preferred_element_type=F32)]
    unnamed x90 -> x62, local copies, waits for them, and re-layouts: 17.8 us -> 63.9 us
    convert_element_type x1 -> x4, local copies, waits for them, and re-layouts: 2.24 us -> 28.5 us  [the longest x1 15.2 us: body(): g_gate_up.reshape(w_gate_up.shape).astype(F32)]
  transfers between devices with their start and end apart: 19 -> 10, of which waited for: 17 -> 8; matrix products, arithmetic and copies ran while one was open for 8% -> 6% of each run, Pallas kernels for 0% -> 0%
where the time goes in v1:
time: 827 us; the launch traced here: 821 us
  waiting for transfers between devices  325 us (39%)
  Pallas kernels  155 us (19%)
  local copies, waits for them, and re-layouts  135 us (16%)
  blocking collectives  93.9 us (11%)
  matrix products  47 us (6%)
  other arithmetic  42.3 us (5%)
  between operations  14.9 us (2%)
    unnamed x10, waiting for transfers between devices  156 us
    reduce_scatter x3, waiting for transfers between devices, scatter_rows(): lax.psum_scatter(partial.astype(BF), Z, scatter_dimension=0, tiled=True)  119 us
    pallas_call x1, Pallas kernels, forward_call(): pl.pallas_call(forward_kernel, out_shape=[out(wide), out(wide), out((4, T...  111 us
    psum x1, blocking collectives, body(): lax.psum(jnp.concatenate([gain_one_grad, gain_two_grad, gain_q_grad, gain...  72.2 us
    unnamed x62, local copies, waits for them, and re-layouts  63.9 us
    dot_general x16, matrix products, dot(): lax.dot_general(left, right, (dims, ((), ())), preferred_element_type=F32)  47 us
    pallas_call x1, Pallas kernels, middle_call(): pl.pallas_call(middle_kernel, grid=(3,), out_shape=[jax.ShapeDtypeStruct(...  44.4 us
    all_gather x1, waiting for transfers between devices, body(): big = lax.all_gather(exchange(big.transpose(1, 0, 2, 3)), 'dp', axis=0)  24.3 us
  transfers between devices with their start and end apart: 10, of which 8 were waited for; matrix products, arithmetic and copies ran while one was open for 6% of the time, Pallas kernels for 0%

profile of v1, /device:TPU:0, one launch (start us, length us, event | category | flops | bytes accessed | tf_op | source)
XLA Modules:
  0.0 821.1 jit_solution(5964941621192210007)
XLA Ops:
  9.3 16.3 %copy.136 = bf16[512,2,3072]{0,2,1:T(8,128)(2,1)} copy(bf16[512,2,3072]{2,1,0:T(2,128)(2,1)} %param.20) | data formatting | bytes 12582912 | tf_op args[7]
  34.4 5.5 copy.138
  39.9 8.0 reshape.202.wg_pair
  53.0 111.0 %forward.1 = (bf16[1024,2048]{1,0:T(8,128)(2,1)}, bf16[1024,2048]{1,0:T(8,128)(2,1)}, bf16[4,512,512]{2,1,0:T(8,128)(2,1)}, bf16[4,256,512]{2,1,0:T(8,128)(2,1)}...) custom-call(bf16[512,512]{1,0:T(8,128)(2,1)} %tok.1, ...), custom_call_target="tpu_custom_call" | custom-call | flops 4000000000 | bytes 60000000 | tf_op jit(solution)/shard_map/forward/pallas_call | solution.py:530
  164.0 44.4 %feed_forward.1 = (bf16[16,3,4,48,512]{4,3,2,1,0:T(8,128)(2,1)}, bf16[1024,1536]{1,0:T(8,128)(2,1)}, bf16[1024,768]{1,0:T(8,128)(2,1)}) custom-call(bf16[1024,2048]{1,0:T(8,128)(2,1)} %get-tuple-element.29.h2, bf16[1024,2048]{1,0:T(8,128)(2,1)} %get-tuple-element.30.g, bf16[4,512,1536]{2,1,0:T(8,128)(2,1)} %get-tuple-element.31.wg, ...), custom_call_target="tpu_custom_call" | custom-call | flops 19000000512 | bytes 32000000 | tf_op jit(solution)/shard_map/feed_forward/pallas_call | solution.py:593
  208.4 11.1 %convolution_convert_fusion = bf16[1024,2048]{1,0:T(8,128)(2,1)} fusion(bf16[1024,1536]{1,0:T(8,128)(2,1)} %get-tuple-element.35, bf16[2048,1536]{1,0:T(8,128)(2,1)} %bitcast.160), kind=kOutput, calls=%fused_computation.12 | convolution fusion | flops 6444548096 | bytes 13631488 | tf_op jit(solution)/shard_map/dot_general | solution.py:24
  221.8 54.3 %reduce-scatter.12.cloned.1.call-done = bf16[128,2048]{1,0:T(8,128)(2,1)} async-done(((bf16[1024,2048]{1,0:T(8,128)(2,1)}), bf16[128,2048]{1,0:T(8,128)(2,1)}) %reduce-scatter.12.cloned.1.call-update) | async-done | bytes 524304 | tf_op jit(solution)/shard_map/reduce_scatter | solution.py:641
  284.9 4.4 multiply_exponential_fusion
  292.6 18.7 %all-gather.6.cloned.1.call-done = bf16[1024,2048]{1,0:T(8,128)(2,1)} async-done(((bf16[128,2048]{1,0:T(8,128)(2,1)}), bf16[1024,2048]{1,0:T(8,128)(2,1)}) %all-gather.6.cloned.1.call-update) | async-done | bytes 4194320 | tf_op jit(solution)/shard_map/all_gather | solution.py:645
  311.3 3.6 convolution_convert_fusion.5
  334.4 4.8 convolution_convert_fusion.3
  342.3 6.0 convolution_convert_fusion.1
  348.4 5.0 copy.142
  353.4 6.9 convolution_convert_fusion.2
  361.5 75.2 %all-reduce.4.cloned.1.call-done = bf16[16,4,48,512]{3,2,0,1:T(8,128)(2,1)} async-done(((bf16[16,4,48,512]{3,2,0,1:T(8,128)(2,1)}), bf16[16,4,48,512]{3,2,0,1:T(8,128)(2,1)}) %all-reduce.4.cloned.1.call-update) | async-done | bytes 3145744
  438.3 8.4 %all_to_all.48 = bf16[4,48,512]{2,1,0:T(8,128)(2,1)} all-to-all(bf16[4,48,512]{2,1,0:T(8,128)(2,1)S(1)} %dynamic-slice_bitcast_fusion.3), channel_id=1, replica_groups=mesh['dp'=16,'row'=2,'col'=4] {'col'}, dimensions={0} | all-to-all | bytes 393216 | tf_op jit(solution)/shard_map/all_to_all | solution.py:637
  446.7 80.3 %reduce-scatter.16.cloned.1.call-done = bf16[1,3,4,48,512]{4,3,2,1,0:T(8,128)(2,1)} async-done(((bf16[16,3,4,48,512]{4,3,2,1,0:T(8,128)(2,1)}), bf16[1,3,4,48,512]{4,3,2,1,0:T(8,128)(2,1)}) %reduce-scatter.16.cloned.1.call-update) | async-done | bytes 589840
  528.2 13.3 %all_to_all.49 = bf16[4,3,48,512]{3,2,1,0:T(8,128)(2,1)} all-to-all(bf16[4,3,48,512]{3,2,1,0:T(8,128)(2,1)S(1)} %copy.155), channel_id=1, replica_groups=mesh['dp'=16,'row'=2,'col'=4] {'col'}, dimensions={0} | all-to-all | bytes 1179648 | tf_op jit(solution)/shard_map/all_to_all | solution.py:637
  541.7 25.5 %reduce-scatter.14.cloned.1.call-done = bf16[128,2048]{1,0:T(8,128)(2,1)} async-done(((bf16[1024,2048]{1,0:T(8,128)(2,1)}), bf16[128,2048]{1,0:T(8,128)(2,1)}) %reduce-scatter.14.cloned.1.call-update) | async-done | bytes 524304 | tf_op jit(solution)/shard_map/reduce_scatter | solution.py:641
  568.6 38.7 %reduce-scatter.10.cloned.1.call-done = bf16[128,2048]{1,0:T(8,128)(2,1)} async-done(((bf16[1024,2048]{1,0:T(8,128)(2,1)}), bf16[128,2048]{1,0:T(8,128)(2,1)}) %reduce-scatter.10.cloned.1.call-update) | async-done | bytes 524304 | tf_op jit(solution)/shard_map/reduce_scatter | solution.py:641
  610.2 3.5 all-to-all-start
  614.8 7.8 all-to-all-done
  622.5 3.5 all-to-all-start.1
  626.1 72.2 %psum.7 = f32[4352]{0:T(1024)S(1)} all-reduce(f32[4352]{0:T(1024)S(1)} %pad_maximum_fusion.9), channel_id=1, replica_groups=mesh['dp'=16,'row'=2,'col'=4] {'dp','row','col'}, use_global_device_ids=true, to_apply=%region_21.22 | all-reduce | flops 4352 | bytes 34816 | tf_op jit(solution)/shard_map/psum | solution.py:750
  701.7 4.8 copy.153
  709.7 24.3 %all-gather.10.cloned.1.call-done = bf16[64,3,48,512]{3,2,1,0:T(8,128)(2,1)} async-done(((bf16[4,3,48,512]{3,2,1,0:T(8,128)(2,1)}), bf16[64,3,48,512]{3,2,1,0:T(8,128)(2,1)}) %all-gather.10.cloned.1.call-update) | async-done | bytes 9437200 | tf_op jit(solution)/shard_map/all_gather | solution.py:754
  734.0 9.4 %slice_convert_fusion = f32[16,4,3,32,512]{4,3,2,1,0:T(8,128)} fusion(bf16[16,4,3,48,512]{4,3,2,1,0:T(8,128)(2,1)} %bitcast.126), kind=kLoop, calls=%fused_computation | loop fusion | flops 3145728 | bytes 18874368 | tf_op jit(solution)/shard_map/convert_element_type | solution.py:769
  743.4 5.4 convert_bitcast_fusion
  748.9 15.2 %reshape.215 = f32[16,4,3,32,2,256]{5,4,3,2,1,0:T(2,128)} reshape(f32[16,4,3,32,512]{4,3,2,1,0:T(8,128)} %slice_convert_fusion) | data formatting | bytes 25165824 | tf_op jit(solution)/shard_map/convert_element_type | solution.py:769
  764.0 18.1 %copy.167 = f32[16,32,2,4,3,256]{5,4,3,2,1,0:T(4,128)} copy(f32[16,32,2,4,3,256]{5,2,1,4,3,0:T(2,128)} %bitcast.123) | data formatting | bytes 25165824
  782.1 23.4 %reshape.218 = f32[512,2,3072]{2,1,0:T(2,128)} reshape(f32[16,32,2,4,3,256]{5,4,3,2,1,0:T(4,128)} %copy.167) | data formatting | bytes 25165824
  805.5 6.9 copy.157
  (146 shorter events, 70.4 us)
Async XLA Ops:
  7.2 269.0 %reduce-scatter.12.cloned.1.call-start = ((), (), s32[]{:S(2)}) async-start(), calls=%async_computation.9 | async-start | bytes 4718592 | tf_op jit(solution)/shard_map/reduce_scatter | solution.py:641
  9.3 16.4 %copy-start.4 = (bf16[512,4,512]{2,0,1:T(8,128)(2,1)}, bf16[512,4,512]{2,0,1:T(8,128)(2,1)S(1)}, u32[]{:S(2)}) copy-start(bf16[512,4,512]{2,0,1:T(8,128)(2,1)S(1)} %copy.170) | copy-start | bytes 6291460
  26.7 6.5 copy-start.24
  26.7 6.5 copy-start.22
  26.7 6.5 copy-start.25
  39.9 8.0 copy-start.7
  39.9 11.1 %copy-start.18 = (f32[512]{0:T(512)S(1)}, f32[512]{0:T(512)}, u32[]{:S(2)}) copy-start(f32[512]{0:T(512)} %param.19) | copy-start | bytes 6148
  39.9 11.1 %copy-start.19 = (f32[512]{0:T(512)S(1)}, f32[512]{0:T(512)}, u32[]{:S(2)}) copy-start(f32[512]{0:T(512)} %param.14) | copy-start | bytes 6148
  219.5 62.9 %copy-start.9 = (f32[2,1024,128]{2,1,0:T(8,128)S(1)}, f32[2,1024,128]{2,1,0:T(8,128)}, u32[]{:S(2)}) copy-start(f32[2,1024,128]{2,1,0:T(8,128)} %get-tuple-element.40) | copy-start | bytes 3145732
  219.5 91.8 %all-gather.6.cloned.1.call-start = ((), (), s32[]{:S(2)}) async-start(), calls=%async_computation.10 | async-start | bytes 4718592 | tf_op jit(solution)/shard_map/all_gather | solution.py:645
  220.8 61.8 %copy-start.3 = (bf16[1024,512]{1,0:T(8,128)(2,1)S(1)}, bf16[1024,512]{1,0:T(8,128)(2,1)}, u32[]{:S(2)}) copy-start(bf16[1024,512]{1,0:T(8,128)(2,1)} %get-tuple-element.37) | copy-start | bytes 3145732
  277.6 7.4 copy-start.8
  280.0 156.7 %all-reduce.4.cloned.1.call-start = ((), (), s32[]{:S(2)}) async-start(), calls=%async_computation.14 | async-start | bytes 6291456
  284.9 4.4 copy-start.11
  289.3 22.0 %copy-start.10 = (bf16[256,4,512]{0,2,1:T(8,128)(2,1)S(1)}, bf16[256,4,512]{0,2,1:T(8,128)(2,1)}, u32[]{:S(2)}) copy-start(bf16[256,4,512]{0,2,1:T(8,128)(2,1)} %copy.144) | copy-start | bytes 3145732
  311.3 3.6 copy-start
  315.7 2.2 copy-start.1
  323.9 3.7 copy-start.20
  324.6 4.1 copy-start.21
  327.6 4.4 copy-start.13
  327.6 4.4 copy-start.14
  327.6 4.4 copy-start.23
  341.1 185.9 %reduce-scatter.16.cloned.1.call-start = ((), (), s32[]{:S(2)}) async-start(), calls=%async_computation.15 | async-start | bytes 10027008
  341.7 225.5 %reduce-scatter.14.cloned.1.call-start = ((), (), s32[]{:S(2)}) async-start(), calls=%async_computation.11 | async-start | bytes 4718592 | tf_op jit(solution)/shard_map/reduce_scatter | solution.py:641
  348.3 5.1 copy-start.27
  348.3 259.1 %reduce-scatter.10.cloned.1.call-start = ((), (), s32[]{:S(2)}) async-start(), calls=%async_computation.8 | async-start | bytes 4718592 | tf_op jit(solution)/shard_map/reduce_scatter | solution.py:641
  360.3 181.2 %copy-start.5 = (bf16[128,2048]{1,0:T(8,128)(2,1)S(1)}, bf16[128,2048]{1,0:T(8,128)(2,1)}, u32[]{:S(2)}) copy-start(bf16[128,2048]{1,0:T(8,128)(2,1)} %get-tuple-element.36) | copy-start | bytes 1572868
  360.3 247.1 %copy-start.6 = (bf16[128,2048]{1,0:T(8,128)(2,1)S(1)}, bf16[128,2048]{1,0:T(8,128)(2,1)}, u32[]{:S(2)}) copy-start(bf16[128,2048]{1,0:T(8,128)(2,1)} %reduce-scatter.12.cloned.1.call-done) | copy-start | bytes 1572868
  360.3 339.1 %all-gather.8.cloned.1.call-start = ((), (), s32[]{:S(2)}) async-start(), calls=%async_computation.12 | async-start | bytes 3342336 | tf_op jit(solution)/shard_map/all_gather | solution.py:755
  446.7 287.3 %all-gather.10.cloned.1.call-start = ((), (), s32[]{:S(2)}) async-start(), calls=%async_computation.13 | async-start | bytes 10027008 | tf_op jit(solution)/shard_map/all_gather | solution.py:754
  610.2 12.3 %all-to-all-start = ((bf16[128,4,512]{2,0,1:T(8,128)(2,1)}), bf16[128,4,512]{2,0,1:T(8,128)(2,1)S(1)}, u32[]{:S(2)}, u32[]{:S(2)}) async-start(bf16[128,4,512]{2,0,1:T(8,128)(2,1)} %bitcast.122), calls=%async_computation.1 | async-start | bytes 1048576 | tf_op jit(solution)/shard_map/all_to_all | solution.py:649
  622.5 76.9 %all-to-all-start.1 = ((f32[128,4,512]{2,0,1:T(8,128)}), f32[128,4,512]{2,0,1:T(8,128)S(1)}, u32[]{:S(2)}, u32[]{:S(2)}) async-start(f32[128,4,512]{2,0,1:T(8,128)} %bitcast.120), calls=%async_computation.4 | async-start | bytes 2097152 | tf_op jit(solution)/shard_map/all_to_all | solution.py:649
  (6 other events, 6.1 us)
Sparse Core Ops, SparseCore 0:
  219.6 56.5 reduce-scatter.11
  280.1 31.1 all-gather.5
  341.3 95.3 all-reduce.3
  440.6 86.4 reduce-scatter.15
  530.0 37.1 reduce-scatter.13
  570.2 37.1 reduce-scatter.9
  609.8 47.1 all-gather.7
  659.4 74.5 all-gather.9

commit v2 on v1

--- a/solution.py
+++ b/solution.py
@@ -279,8 +279,8 @@
 
 def forward_kernel(
     tok, og, gains, q_gain, k_gain, start, cosine, sine, wq_pair, wq_part, wg_pair, wg_part, w_out, w_down,
-    h2_o, g_o, wq_o, wo_o, wg_o, wd_o, h1_o, raw_o, q_o, k_o, att_o, lse_o, mid_o, gain_o, x_o,
-    x, h1, h2, g, wq, wo, raw, qs, ks, att, lse, mid, gain,
+    h2_o, g_o, wq_o, wo_o, wg_o, wd_o, h1t_o, raw_o, q_o, k_o, att_o, lse_o, mid_o, gain_o, x_o,
+    x, h1, h1t, h2, g, wq, wo, raw, qs, ks, att, lse, mid, gain,
     xs, xr, gs, gr, hs, hr,
     parts, theirs, sums, near, full, rs_s, rs_r,
     zs, zr, ps, pr, ys, yr, ns, nr, loc_s, out_s,
@@ -433,13 +433,13 @@
         pltpu.make_async_copy(src, dst, out_s.at[i])
         for i, (src, dst) in enumerate(
             [
-                (h1, h1_o), (wq, wq_o), (raw, raw_o), (qs, q_o), (ks, k_o), (gain, gain_o),
+                (wq, wq_o), (raw, raw_o), (qs, q_o), (ks, k_o), (gain, gain_o),
                 (x.at[pl.ds(pl.multiple_of(me * OWN, OWN), OWN)], x_o), (wo, wo_o),
-                (att, att_o), (lse, lse_o), (g, g_o), (mid, mid_o), (h2, h2_o),
+                (att, att_o), (lse, lse_o), (g, g_o), (mid, mid_o), (h2, h2_o), (h1t, h1t_o),
             ]
         )
     ]
-    for i in range(8):
+    for i in range(7):
         saves[i].start()
 
     for block in range(GROUP // QROWS):
@@ -458,8 +458,8 @@
             att[h, rows] = out.astype(BF)
             lse[h, rows] = jnp.broadcast_to(peak + jnp.log2(total), (QROWS, HEAD))
 
+    saves[7].start()
     saves[8].start()
-    saves[9].start()
     g_gather.share()
 
     scatter = Scatter(parts, theirs, sums, near, full, rs_s, rs_r)
@@ -478,9 +478,16 @@
     project(0)
     scatter.beside(0)
     scatter.beside(1)
+
+    @pl.loop(0, 8)
+    def _(i):
+        cols = pl.ds(pl.multiple_of(i * 256, 256), 256)
+        h1t[cols] = h1[:, cols].T
+
+    saves[12].start()
     g_gather.finish()
     keep_g.wait()
-    saves[10].start()
+    saves[9].start()
     scatter.arrive()
     gain_two = gain_row(1)
 
@@ -492,7 +499,7 @@
         mid[pl.ds(first, 16)] = value
         h2[there] = (value * head_norm(value) * gain_two).astype(BF)
 
-    saves[11].start()
+    saves[10].start()
     h2_gather = Gather(rows_at(h2), hs, hr)
     h2_gather.start()
     h2_gather.forward()
@@ -503,7 +510,7 @@
         spread_wait(a)
     h2_gather.share()
     h2_gather.finish()
-    saves[12].start()
+    saves[11].start()
     for copy in gain_copies:
         copy.wait_send()
     for a in range(4):
@@ -531,14 +538,14 @@
         forward_kernel,
         out_shape=[
             out(wide), out(wide), out((4, TILE, 512)), out((4, 256, TILE)), out((4, TILE, 2 * UNITS)),
-            out((4, UNITS, TILE)), out(wide), out((GROUP, 512)), out((2, GROUP, HEAD)), out((GROUP, HEAD)),
+            out((4, UNITS, TILE)), out((WIDTH, GROUP)), out((GROUP, 512)), out((2, GROUP, HEAD)), out((GROUP, HEAD)),
             out((2, GROUP, HEAD)), out((2, GROUP, HEAD), F32), out((OWN, WIDTH), F32), out((4, 8, TILE), F32),
             out((OWN, WIDTH)),
         ],
         in_specs=[vmem] * 8 + [hbm] * 6,
         out_specs=[hbm] * 15,
         scratch_shapes=[
-            pltpu.VMEM(wide, BF), pltpu.VMEM(wide, BF), pltpu.VMEM(wide, BF), pltpu.VMEM(wide, BF),
+            pltpu.VMEM(wide, BF), pltpu.VMEM(wide, BF), pltpu.VMEM((WIDTH, GROUP), BF), pltpu.VMEM(wide, BF), pltpu.VMEM(wide, BF),
             pltpu.VMEM((4, TILE, 512), BF), pltpu.VMEM((4, 256, TILE), BF), pltpu.VMEM((GROUP, 512), BF),
             pltpu.VMEM((2, GROUP, HEAD), BF), pltpu.VMEM((GROUP, HEAD), BF), pltpu.VMEM((2, GROUP, HEAD), BF),
             pltpu.VMEM((2, GROUP, HEAD), F32), pltpu.VMEM((OWN, WIDTH), F32), pltpu.VMEM((4, 8, TILE), F32),
@@ -616,6 +623,556 @@
     )(h2, g, wg, wd)
 
 
+def dp_place():
+    p = lax.axis_index("dp")
+    return p // 4, p % 4
+
+
+def along(axis, o):
+    px, py = dp_place()
+    return {"dp": (px + o) % 4 * 4 + py} if axis == 0 else {"dp": px * 4 + (py + o) % 4}
+
+
+def xy_friends():
+    return [along(axis, o) for axis in range(2) for o in range(1, 4)]
+
+
+class Spread:
+    def __init__(self, at, send, recv):
+        px, py = dp_place()
+        here = (px, py)
+        self.out, self.into = {}, {}
+        for half in range(2):
+            for phase in range(2):
+                axis = half ^ phase
+                for o in range(1, 4):
+                    came = [px, py]
+                    came[axis] = (here[axis] - o + 4) % 4
+                    mine = [px, py]
+                    if phase:
+                        mine[1 - axis] = came[1 - axis] = None
+                    src, dst = at(half, *mine), at(half, *came)
+                    sems = (send.at[half, phase, o - 1], recv.at[half, phase, o - 1])
+                    self.out[half, phase, o] = remote(src, src, *sems, along(axis, o))
+                    self.into[half, phase, o] = remote(dst, dst, *sems, along(axis, o))
+
+    def start(self, phase):
+        for half in range(2):
+            for o in range(1, 4):
+                self.out[half, phase, o].start()
+
+    def wait(self, phase):
+        for half in range(2):
+            for o in range(1, 4):
+                self.into[half, phase, o].wait_recv()
+
+    def drain(self):
+        for copy in self.out.values():
+            copy.wait_send()
+
+
+class Collapse:
+    def __init__(self, src, got, sums, got2, done, send, recv, own):
+        px, py = dp_place()
+        here = (px, py)
+        self.got, self.sums, self.got2, self.done, self.here = got, sums, got2, done, here
+        self.units = src.shape[2]
+
+        def cut(axis, index, half):
+            pair = pl.ds(2 * half, 2)
+            return src.at[index, :, :, pair] if axis == 0 else src.at[:, index, :, pair]
+
+        self.keep, self.copies = [], {}
+        for half in range(2):
+            axis = half
+            self.keep.append(pltpu.make_async_copy(cut(axis, here[axis], half), sums.at[half], own.at[half]))
+            for o in range(1, 4):
+                there = (here[axis] + o) % 4
+                self.copies[half, 0, o] = remote(
+                    cut(axis, there, half), got.at[half, o - 1],
+                    send.at[half, 0, o - 1], recv.at[half, 0, o - 1], along(axis, o),
+                )
+                there = (here[1 - axis] + o) % 4
+                self.copies[half, 1, o] = remote(
+                    sums.at[half, there], got2.at[half, o - 1],
+                    send.at[half, 1, o - 1], recv.at[half, 1, o - 1], along(1 - axis, o),
+                )
+
+    def start(self):
+        for half in range(2):
+            for o in range(1, 4):
+                self.copies[half, 0, o].start()
+            self.keep[half].start()
+
+    def first(self):
+        units = self.units
+        for half in range(2):
+            self.keep[half].wait()
+            for o in range(1, 4):
+                self.copies[half, 0, o].wait_recv()
+
+            @pl.loop(0, 4 * units)
+            def _(i):
+                a, u = i // units, i % units
+                for c in range(2):
+                    total = self.sums[half, a, u, c].astype(F32)
+                    for o in range(3):
+                        total += self.got[half, o, a, u, c].astype(F32)
+                    self.sums[half, a, u, c] = total.astype(BF)
+
+            for o in range(1, 4):
+                self.copies[half, 1, o].start()
+
+    def second(self):
+        for half in range(2):
+            for o in range(1, 4):
+                self.copies[half, 1, o].wait_recv()
+
+            @pl.loop(0, self.units)
+            def _(u):
+                for c in range(2):
+                    total = self.sums[half, self.here[1 - half], u, c].astype(F32)
+                    for o in range(3):
+                        total += self.got2[half, o, u, c].astype(F32)
+                    self.done[2 * half + c, u] = total.astype(BF)
+
+    def drain(self):
+        for copy in self.copies.values():
+            copy.wait_send()
+
+
+def collapse_scratch(units):
+    dma = pltpu.SemaphoreType.DMA
+    return [
+        pltpu.VMEM((2, 3, 4, units, 2, 48, 512), BF),
+        pltpu.VMEM((2, 4, units, 2, 48, 512), BF),
+        pltpu.VMEM((2, 3, units, 2, 48, 512), BF),
+        pltpu.VMEM((4, units, 48, 512), BF),
+        dma((2, 2, 3)), dma((2, 2, 3)), dma((2,)),
+        dma((3,)), dma((4,)), dma((2, 2, 3)), dma((2, 2, 3)),
+    ]
+
+
+class Trade:
+    def __init__(self, block, slot, send, recv):
+        _, row, col, z, k = place()
+        self.col, self.peer = col, on_ring(z, 1 - k)
+        self.recv, self.send, self.slot = recv, send, slot
+        self.copies = [
+            remote(block((col + o) % 4), slot(col), send.at[o - 1], recv.at[o - 1], {"col": (col + o) % 4})
+            for o in range(1, 4)
+        ]
+        self.keep = pltpu.make_async_copy(block(col), slot(col), recv.at[3])
+
+    def start(self):
+        for copy in self.copies:
+            copy.start()
+        self.keep.start()
+
+    def finish(self):
+        for o in range(1, 4):
+            dst = self.slot((self.col - o + 4) % 4)
+            remote(dst, dst, self.send.at[o - 1], self.recv.at[o - 1], self.peer).wait_recv()
+        self.keep.wait()
+
+    def drain(self):
+        for copy in self.copies:
+            copy.wait_send()
+
+
+def norm_back(grad, value, gain):
+    scale = head_norm(value)
+    weighted = grad * gain
+    inner = jnp.mean(weighted * value, axis=1, keepdims=True)
+    return scale * weighted - value * (scale * scale * scale * inner), grad * value * scale
+
+
+def backward_kernel(
+    big, ggu_i, hid_i, g_i, wg_i, wd_i, wo_i, wq_i, h1t_i, raw_i, q_i, k_i, att_i, lse_i, mid_i, gain_i, x_i,
+    q_gain, k_gain, start, cosine, sine,
+    result_o, stream_o, big_o, small_o, sums_o,
+    m, gm, dqkv, small, mid, gain, x_own, g_own, acc, head_acc, tile_f, tile_b, totals, heard,
+    ms, mr,
+    parts, theirs, psums, near, full, rs_s, rs_r,
+    b_got, b_sums, b_got2, b_done, b_s, b_r, b_own, b_ts, b_tr, b_gs, b_gr,
+    s_got, s_sums, s_got2, s_done, s_s, s_r, s_own, s_ts, s_tr, s_gs, s_gr,
+    fs, fr, ls, lr, as_, ar, in_s, free,
+):
+    p, row, col, z, k = place()
+    px, py = dp_place()
+    me = 2 * z + k
+    up, down, peer = on_ring((z + 1) % 4, k), on_ring((z + 3) % 4, k), on_ring(z, 1 - k)
+    far = on_ring((z + 2) % 4, k)
+    meet(ring_friends() + [far] + xy_friends())
+
+    loads = {}
+
+    def load(src, dst):
+        i = len(loads)
+        copy = pltpu.make_async_copy(src, dst, in_s.at[i])
+        copy.start()
+        loads[i] = copy
+        return copy
+
+    def small_slot(units_ref):
+        return units_ref
+
+    big_sum = Collapse(big, b_got, b_sums, b_got2, b_done, b_s, b_r, b_own)
+    big_trade = Trade(lambda c: b_done.at[c], lambda c: big_o.at[px, py, c], b_ts, b_tr)
+
+    def big_at(half, x, y):
+        xs = slice(None) if x is None else x
+        ys = slice(None) if y is None else y
+        return big_o.at[xs, ys, pl.ds(2 * half, 2)]
+
+    def small_at(half, x, y):
+        xs = slice(None) if x is None else x
+        ys = slice(None) if y is None else y
+        return small_o.at[xs, ys, pl.ds(2 * half, 2)]
+
+    big_all = Spread(big_at, b_gs, b_gr)
+    small_sum = Collapse(small, s_got, s_sums, s_got2, s_done, s_s, s_r, s_own)
+    small_trade = Trade(lambda c: s_done.at[c], lambda c: small_o.at[px, py, c], s_ts, s_tr)
+    small_all = Spread(small_at, s_gs, s_gr)
+    scatter = Scatter(parts, theirs, psums, near, full, rs_s, rs_r)
+    stream_trade = Trade(
+        lambda c: tile_f.at[:, pl.ds(pl.multiple_of(c * TILE, TILE), TILE)],
+        lambda c: stream_o.at[pl.ds(pl.multiple_of(c * OWN, OWN), OWN)], fs, fr,
+    )
+    result_trade = Trade(
+        lambda c: tile_b.at[:, pl.ds(pl.multiple_of(c * TILE, TILE), TILE)],
+        lambda c: result_o.at[pl.ds(pl.multiple_of(c * OWN, OWN), OWN)], ls, lr,
+    )
+
+    def release():
+        scatter.drain()
+        for device in (up, down, peer):
+            pl.semaphore_signal(free, inc=1, device_id=device, device_id_type=MESH)
+
+    def project(d, product):
+        rows = pl.ds(pl.multiple_of((z + d) % 4 * 256, 256), 256)
+
+        @pl.loop(0, 4)
+        def _(c):
+            cols = pl.ds(pl.multiple_of(c * TILE, TILE), TILE)
+            parts[d, :, cols] = product(rows, c, cols).astype(BF)
+
+        scatter.put(d)
+
+    big_sum.start()
+    own_rows = pl.ds(pl.multiple_of(me * OWN, OWN), OWN)
+    early = [load(mid_i, mid), load(gain_i, gain), load(x_i, x_own), load(g_i.at[own_rows], g_own)]
+
+    def gain_row(which):
+        return jnp.concatenate([gain[c, which : which + 1] for c in range(4)], axis=1)
+
+    def stage_one(wg, ggu):
+        waits = [load(wg_i, wg), load(ggu_i, ggu)]
+        for copy in waits:
+            copy.wait()
+
+        def product(rows, c, cols):
+            return mm_t(ggu[rows], wg[c])
+
+        project(2, product)
+        project(1, product)
+        scatter.across()
+        project(3, product)
+        project(0, product)
+
+    pl.run_scoped(stage_one, pltpu.VMEM((4, TILE, 2 * UNITS), BF), pltpu.VMEM((GROUP, 2 * UNITS), BF))
+
+    def stage_two(wo, att, qs, ks, raw, lse, ga, dk, dv, h1t, wq, att_t):
+        l_wo, l_att = load(wo_i, wo), load(att_i, att)
+        l_heads = [load(q_i, qs), load(k_i, ks), load(raw_i, raw), load(lse_i, lse)]
+        l_last = [load(h1t_i, h1t), load(wq_i, wq)]
+        scatter.beside(0)
+        scatter.beside(1)
+        for copy in early:
+            copy.wait()
+        acc[...] = jnp.zeros_like(acc)
+        head_acc[...] = jnp.zeros_like(head_acc)
+        dk[...] = jnp.zeros_like(dk)
+        dv[...] = jnp.zeros_like(dv)
+        totals[0] = jnp.zeros((8, WIDTH), F32)
+        gain_two = gain_row(1)
+        scatter.arrive()
+
+        @pl.loop(0, OWN // 16)
+        def _(i):
+            rows = pl.ds(pl.multiple_of(i * 16, 16), 16)
+            back, gained = norm_back(scatter.total(pl.multiple_of(i * 16, 16), 16), mid[rows], gain_two)
+            acc[1] += gained
+            back = back + g_own[rows].astype(F32)
+            gm[rows] = back
+            m[pl.ds(pl.multiple_of(me * OWN + i * 16, 16), 16)] = back.astype(BF)
+
+        m_gather = Gather(rows_at(m), ms, mr)
+        m_gather.start()
+        release()
+        l_att.wait()
+        for h in range(2):
+            att_t[h * HEAD : (h + 1) * HEAD] = att[h].T
+        m_gather.forward()
+        l_wo.wait()
+        for copy in l_heads:
+            copy.wait()
+        m_gather.share()
+        m_gather.finish()
+
+        @pl.loop(0, 4)
+        def _(i):
+            rows = pl.ds(pl.multiple_of(i * 256, 256), 256)
+            back = mm_t(m[rows, :TILE], wo[0])
+            for c in range(1, 4):
+                back += mm_t(m[rows, c * TILE : (c + 1) * TILE], wo[c])
+            for h in range(2):
+                ga[h, rows] = back[:, h * HEAD : (h + 1) * HEAD].astype(BF)
+
+        @pl.loop(0, 4)
+        def _(c):
+            cols = pl.ds(pl.multiple_of(c * TILE, TILE), TILE)
+            grad = mm(att_t[...], m[:, cols]).astype(BF)
+            small[:, :, 0, pl.ds(c, 1), 32:] = grad.reshape(4, 4, 1, 16, TILE)
+
+        for block in range(GROUP // QROWS):
+            first, keys = block * QROWS, (block + 1) * QROWS
+            rows = pl.ds(first, QROWS)
+            allowed = allowed_keys(start[rows], first, keys)
+
+            @pl.loop(0, 2)
+            def _(h):
+                cols = pl.ds(pl.multiple_of(h * HEAD, HEAD), HEAD)
+                score = mm_t(qs[h, rows], ks[:keys]) * (SCALE * LOG2)
+                prob = jnp.exp2(jnp.where(allowed, score, -1e30) - lse[h, rows, :1])
+                grad = ga[h, rows]
+                delta = jnp.sum(grad.astype(F32) * att[h, rows].astype(F32), axis=1, keepdims=True)
+                prob_grad = mm_t(grad, raw[:keys, 3 * HEAD :])
+                score_grad = (prob * (prob_grad - delta)).astype(BF)
+                dk[:keys] += t_mm(score_grad, qs[h, rows])
+                dv[:keys] += t_mm(prob.astype(BF), grad)
+                back = turn_back(mm(score_grad, ks[:keys]) * SCALE, cosine[rows], sine[rows])
+                back, gained = norm_back(back, raw[rows, cols].astype(F32), q_gain[...])
+                dqkv[rows, cols] = back.astype(BF)
+                head_acc[0:1] += jnp.sum(gained, axis=0, keepdims=True)
+
+        @pl.loop(0, 4)
+        def _(i):
+            rows = pl.ds(pl.multiple_of(i * 256, 256), 256)
+            back = turn_back(dk[rows] * SCALE, cosine[rows], sine[rows])
+            back, gained = norm_back(back, raw[rows, 2 * HEAD : 3 * HEAD].astype(F32), k_gain[...])
+            dqkv[rows, 2 * HEAD : 3 * HEAD] = back.astype(BF)
+            dqkv[rows, 3 * HEAD :] = dv[rows].astype(BF)
+            head_acc[1:2] += jnp.sum(gained, axis=0, keepdims=True)
+
+        big_sum.first()
+        for copy in l_last:
+            copy.wait()
+        pl.semaphore_wait(free, 3)
+
+        def product(rows, c, cols):
+            return mm_t(dqkv[rows], wq[c])
+
+        project(2, product)
+        project(1, product)
+
+        @pl.loop(0, 4)
+        def _(c):
+            cols = pl.ds(pl.multiple_of(c * TILE, TILE), TILE)
+            small[:, :, 0, pl.ds(c, 1), :32] = mm(h1t[cols], dqkv[...]).astype(BF).reshape(4, 4, 1, 32, 512)
+
+        small_sum.start()
+        scatter.across()
+        project(3, product)
+        project(0, product)
+        m_gather.drain()
+
+    pl.run_scoped(
+        stage_two,
+        pltpu.VMEM((4, 256, TILE), BF), pltpu.VMEM((2, GROUP, HEAD), BF), pltpu.VMEM((2, GROUP, HEAD), BF),
+        pltpu.VMEM((GROUP, HEAD), BF), pltpu.VMEM((GROUP, 512), BF), pltpu.VMEM((2, GROUP, HEAD), F32),
+        pltpu.VMEM((2, GROUP, HEAD), BF), pltpu.VMEM((GROUP, HEAD), F32), pltpu.VMEM((GROUP, HEAD), F32),
+        pltpu.VMEM((WIDTH, GROUP), BF), pltpu.VMEM((4, TILE, 512), BF), pltpu.VMEM((2 * HEAD, GROUP), BF),
+    )
+
+    def stage_three(hid, wd):
+        waits = [load(hid_i, hid), load(wd_i, wd)]
+        big_sum.second()
+        big_trade.start()
+        scatter.beside(0)
+        scatter.beside(1)
+        small_sum.first()
+        big_trade.finish()
+        big_all.start(0)
+        gain_one = gain_row(0)
+        scatter.arrive()
+
+        @pl.loop(0, OWN // 16)
+        def _(i):
+            rows = pl.ds(pl.multiple_of(i * 16, 16), 16)
+            back, gained = norm_back(
+                scatter.total(pl.multiple_of(i * 16, 16), 16), x_own[rows].astype(F32), gain_one
+            )
+            acc[0] += gained
+            tile_f[rows] = gm[rows] + back
+
+        stream_trade.start()
+        release()
+        totals[0, 0:1] = jnp.sum(acc[0], axis=0, keepdims=True)
+        totals[0, 1:2] = jnp.sum(acc[1], axis=0, keepdims=True)
+        totals[0, 2:3, 0:HEAD] = head_acc[0:1]
+        totals[0, 2:3, HEAD : 2 * HEAD] = head_acc[1:2]
+        sent = []
+
+        def tell(phase, devices, slots):
+            for device, slot in zip(devices, slots):
+                copy = remote(totals.at[phase], heard.at[slot], as_.at[slot], ar.at[slot], device)
+                copy.start()
+                sent.append(copy)
+
+        def listen(phase, slots):
+            total = totals[phase]
+            for slot in slots:
+                remote(heard.at[slot], heard.at[slot], as_.at[slot], ar.at[slot], peer).wait_recv()
+                total += heard[slot]
+            totals[phase + 1] = total
+
+        tell(0, [peer], [0])
+        big_all.wait(0)
+        big_all.start(1)
+        small_sum.second()
+        small_trade.start()
+        listen(0, [0])
+        tell(1, [up, down, far], [1, 2, 3])
+        for copy in waits:
+            copy.wait()
+        pl.semaphore_wait(free, 3)
+
+        def product(rows, c, cols):
+            return mm(hid[rows], wd[c])
+
+        project(2, product)
+        project(1, product)
+        small_trade.finish()
+        small_all.start(0)
+        scatter.across()
+        project(3, product)
+        project(0, product)
+        listen(1, [1, 2, 3])
+        tell(2, [along(0, o) for o in range(1, 4)], [4, 5, 6])
+        scatter.beside(0)
+        scatter.beside(1)
+        small_all.wait(0)
+        small_all.start(1)
+        scatter.arrive()
+
+        @pl.loop(0, OWN // 16)
+        def _(i):
+            rows = pl.ds(pl.multiple_of(i * 16, 16), 16)
+            tile_b[rows] = (mid[rows] + scatter.total(pl.multiple_of(i * 16, 16), 16)).astype(BF)
+
+        result_trade.start()
+        listen(2, [4, 5, 6])
+        tell(3, [along(1, o) for o in range(1, 4)], [7, 8, 9])
+        stream_trade.finish()
+        listen(3, [7, 8, 9])
+        sums_o[...] = totals[4]
+        result_trade.finish()
+        big_all.wait(1)
+        small_all.wait(1)
+        scatter.drain()
+        for thing in (big_sum, big_trade, big_all, small_sum, small_trade, small_all, stream_trade, result_trade):
+            thing.drain()
+        for copy in sent:
+            copy.wait_send()
+
+    pl.run_scoped(stage_three, pltpu.VMEM((GROUP, UNITS), BF), pltpu.VMEM((4, UNITS, TILE), BF))
+
+
+def backward_call(*args):
+    hbm = pl.BlockSpec(memory_space=pl.ANY)
+    vmem = pl.BlockSpec(memory_space=pltpu.VMEM)
+    dma = pltpu.SemaphoreType.DMA
+    out = jax.ShapeDtypeStruct
+    return pl.pallas_call(
+        backward_kernel,
+        out_shape=[
+            out((TILE, TILE), BF), out((TILE, TILE), F32), out((4, 4, 4, 3, 48, 512), BF),
+            out((4, 4, 4, 1, 48, 512), BF), out((8, WIDTH), F32),
+        ],
+        in_specs=[hbm] * 17 + [vmem] * 5,
+        out_specs=[hbm] * 4 + [vmem],
+        scratch_shapes=[
+            pltpu.VMEM((GROUP, WIDTH), BF), pltpu.VMEM((OWN, WIDTH), F32), pltpu.VMEM((GROUP, 512), BF),
+            pltpu.VMEM((4, 4, 1, 4, 48, 512), BF), pltpu.VMEM((OWN, WIDTH), F32), pltpu.VMEM((4, 8, TILE), F32),
+            pltpu.VMEM((OWN, WIDTH), BF), pltpu.VMEM((OWN, WIDTH), BF), pltpu.VMEM((2, 16, WIDTH), F32),
+            pltpu.VMEM((8, HEAD), F32), pltpu.VMEM((OWN, WIDTH), F32), pltpu.VMEM((OWN, WIDTH), BF),
+            pltpu.VMEM((5, 8, WIDTH), F32), pltpu.VMEM((10, 8, WIDTH), F32),
+        ]
+        + GATHER_SEMS
+        + scatter_scratch()
+        + collapse_scratch(3)
+        + collapse_scratch(1)
+        + [dma((3,)), dma((4,)), dma((3,)), dma((4,)), dma((10,)), dma((10,)), dma((20,)), pltpu.SemaphoreType.REGULAR],
+        compiler_params=pltpu.CompilerParams(
+            collective_id=2, has_side_effects=True, vmem_limit_bytes=63 * 1024 * 1024
+        ),
+        cost_estimate=pl.CostEstimate(flops=15_000_000_000, bytes_accessed=100_000_000, transcendentals=2_000_000),
+        name="backward",
+    )(*args)
+
+
+def place_big_kernel(grads, gate_up, down):
+    value = grads[:, 0, 0, :32].reshape(TILE, 512).astype(F32)
+    for g in range(2):
+        gate_up[:, g, :] = value[:, g * 256 : (g + 1) * 256]
+    down[...] = grads[:, 0, 0, 32:].reshape(256, TILE).astype(F32)
+
+
+def place_big(grads):
+    return pl.pallas_call(
+        place_big_kernel,
+        grid=(4, 3),
+        in_specs=[pl.BlockSpec((DP, 1, 1, 48, 512), lambda c, u: (0, c, u, 0, 0))],
+        out_specs=[
+            pl.BlockSpec((TILE, 2, 256), lambda c, u: (0, 0, c * 3 + u)),
+            pl.BlockSpec((256, TILE), lambda c, u: (c * 3 + u, 0)),
+        ],
+        out_shape=[
+            jax.ShapeDtypeStruct((TILE, 2, 4 * UNITS), F32),
+            jax.ShapeDtypeStruct((4 * UNITS, TILE), F32),
+        ],
+        compiler_params=pltpu.CompilerParams(vmem_limit_bytes=40 * 1024 * 1024),
+        cost_estimate=pl.CostEstimate(flops=0, bytes_accessed=29_000_000, transcendentals=0),
+        name="place_big",
+    )(grads)
+
+
+def place_small_kernel(grads, qkv, out):
+    for c in range(4):
+        qkv[:, c, :] = grads[:, c, :32].reshape(128, 512).astype(F32)
+        out[c] = grads[:, c, 32:].reshape(64, TILE).astype(F32)
+
+
+def place_small(grads):
+    return pl.pallas_call(
+        place_small_kernel,
+        grid=(4,),
+        in_specs=[pl.BlockSpec((4, 4, 48, 512), lambda i: (i, 0, 0, 0))],
+        out_specs=[
+            pl.BlockSpec((128, 4, 512), lambda i: (i, 0, 0)),
+            pl.BlockSpec((4, 64, TILE), lambda i: (0, i, 0)),
+        ],
+        out_shape=[
+            jax.ShapeDtypeStruct((TILE, 4, 512), F32),
+            jax.ShapeDtypeStruct((4, 256, TILE), F32),
+        ],
+        compiler_params=pltpu.CompilerParams(vmem_limit_bytes=40 * 1024 * 1024),
+        cost_estimate=pl.CostEstimate(flops=0, bytes_accessed=9_000_000, transcendentals=0),
+        name="place_small",
+    )(grads)
+
+
 def starts_of(seq_lengths, seq_group, seq_start, group_index):
     slots = jnp.arange(GROUP, dtype=jnp.int32)
     inside = (
@@ -631,37 +1188,6 @@
     freq = THETA ** (-(jnp.arange(half, dtype=F32) * 2.0 / HEAD))
     angle = position.astype(F32)[:, None] * freq[None, :]
     return (jnp.cos(angle), jnp.sin(angle))
-
-
-def exchange(piece):
-    return lax.all_to_all(piece, "col", split_axis=0, concat_axis=0, tiled=True)
-
-
-def scatter_rows(partial):
-    return lax.psum_scatter(partial.astype(BF), Z, scatter_dimension=0, tiled=True).astype(F32)
-
-
-def gather_rows(block):
-    return lax.all_gather(block, Z, axis=0, tiled=True)
-
-
-def rows_to_tile(block):
-    return lax.all_to_all(block, "col", split_axis=1, concat_axis=0, tiled=True)
-
-
-def norm_backward(grad, value, scale, gain):
-    inner = jnp.sum(grad * gain * value, axis=1, keepdims=True)
-    gain_grad = jnp.sum(grad * value * scale, axis=0)
-    back = scale * gain * grad - value * (scale * scale * scale * inner / value.shape[1])
-    return (back, gain_grad)
-
-
-def head_backward(grad, value, gain, cosine, sine):
-    half = HEAD // 2
-    first, second = grad[:, :half], grad[:, half:]
-    grad = jnp.concatenate([first * cosine + second * sine, second * cosine - first * sine], axis=1)
-    scale = lax.rsqrt(jnp.mean(value * value, axis=1, keepdims=True) + EPS)
-    return norm_backward(grad, value, scale, gain)
 
 
 def body(
@@ -691,83 +1217,28 @@
     wg_pair = order(pair(wg7, lo, 2))
     wg_part = order(pair(lax.dynamic_slice_in_dim(wg7, p * 32, 32, 0), 1 - lo, 2))
 
-    (h2, g, wq, wo, wg, wd, h1, raw, qs, ks, att, lse, middle, gain, x_own) = forward_call(
+    (h2, g, wq, wo, wg, wd, h1t, raw, qs, ks, att, lse, middle, gain, x_own) = forward_call(
         tokens, out_grad, gains, q_gain[None], k_gain[None], start[:, None], cos_wide, sin_wide,
         wq_pair, wq_part, wg_pair, wg_part, w_out, w_down,
     )
-    gain_one = gain[:, 0].reshape(1, WIDTH)
-    gain_two = gain[:, 1].reshape(1, WIDTH)
     big, ggu, hid = middle_call(h2, g, wg, wd)
-    big = lax.psum_scatter(big, "dp", scatter_dimension=0, tiled=False)
-
-    wd2 = wd.transpose(1, 0, 2).reshape(UNITS, WIDTH)
-    wo2 = wo.transpose(1, 0, 2).reshape(256, WIDTH)
-    result = rows_to_tile((middle + scatter_rows(mm(hid, wd2))).astype(BF))
-    scale_two = lax.rsqrt(jnp.mean(middle * middle, axis=1, keepdims=True) + EPS)
-    back, gain_two_grad = norm_backward(
-        scatter_rows(mm_t(ggu, wg.reshape(WIDTH, 2 * UNITS))), middle, scale_two, gain_two
+    result, stream_grad, big, small, totals = backward_call(
+        big.reshape(4, 4, 3, 4, 48, 512), ggu, hid, g, wg, wd, wo, wq, h1t, raw, qs, ks, att, lse, middle, gain,
+        x_own, q_gain[None], k_gain[None], start[:, None], cos_wide, sin_wide,
     )
-    middle_grad = lax.dynamic_slice_in_dim(g, me * OWN, OWN, 0).astype(F32) + back
-    middle_all = gather_rows(middle_grad.astype(BF))
-    att2 = jnp.concatenate([att[0], att[1]], axis=1)
-    g_out = t_mm(att2, middle_all).astype(BF)
-    head_grad = mm_t(middle_all, wo2).astype(BF).reshape(GROUP, 2, HEAD).transpose(1, 0, 2)
-    value_low = raw[:, 3 * HEAD :]
-    allowed = (slots[None, :] >= start[:, None]) & (slots[None, :] <= slots[:, None])
-    key_grad, value_grad, pieces, gain_q_grad = 0.0, 0.0, [], 0.0
-    for h in range(2):
-        score = jnp.where(allowed, mm_t(qs[h], ks) * (SCALE * LOG2), -1e30)
-        prob = jnp.exp2(score - lse[h, :, :1])
-        prob_grad = mm_t(head_grad[h], value_low)
-        delta = jnp.sum(prob_grad * prob, axis=-1, keepdims=True)
-        score_grad = (prob * (prob_grad - delta)).astype(BF)
-        key_grad += t_mm(score_grad, qs[h]) * SCALE
-        value_grad += t_mm(prob.astype(BF), head_grad[h])
-        piece, gain_grad = head_backward(
-            mm(score_grad, ks) * SCALE, raw[:, h * HEAD : (h + 1) * HEAD].astype(F32), q_gain, cosine, sine
-        )
-        gain_q_grad += gain_grad
-        pieces.append(piece)
-    piece, gain_k_grad = head_backward(
-        key_grad, raw[:, 2 * HEAD : 3 * HEAD].astype(F32), k_gain, cosine, sine
-    )
-    heads_grad = jnp.concatenate(pieces + [piece, value_grad], axis=1).astype(BF)
-    g_qkv = t_mm(h1, heads_grad).astype(BF)
-    small = jnp.concatenate(
-        [
-            g_qkv.reshape(4, DP, 32, 512).transpose(1, 0, 2, 3),
-            g_out.reshape(DP, 16, 4, 512).transpose(0, 2, 1, 3),
-        ],
-        axis=2,
-    )
-    small = lax.psum_scatter(small, "dp", scatter_dimension=0, tiled=False)
-    x_float = x_own.astype(F32)
-    scale_one = lax.rsqrt(jnp.mean(x_float * x_float, axis=1, keepdims=True) + EPS)
-    back, gain_one_grad = norm_backward(
-        scatter_rows(mm_t(heads_grad, wq.reshape(WIDTH, 512))), x_float, scale_one, gain_one
-    )
-    stream_grad = rows_to_tile(middle_grad + back)
-    totals = lax.psum(
-        jnp.concatenate([gain_one_grad, gain_two_grad, gain_q_grad, gain_k_grad]),
-        ("dp", "row", "col"),
-    )
-    big = lax.all_gather(exchange(big.transpose(1, 0, 2, 3)), "dp", axis=0)
-    small = lax.all_gather(exchange(small), "dp", axis=0)
-    g_gate_up = big[:, :, :, :32].reshape(DP, 4, 3, 32, 2, 256).transpose(0, 3, 4, 1, 2, 5)
-    g_down = big[:, :, :, 32:].transpose(1, 2, 0, 3, 4)
-    g_qkv = small[:, :, :32].transpose(0, 2, 1, 3)
-    g_out = small[:, :, 32:].transpose(1, 0, 2, 3)
+    g_gate_up, g_down = place_big(big.reshape(DP, 4, 3, 48, 512))
+    g_qkv, g_out = place_small(small.reshape(DP, 4, 48, 512))
     return (
         result,
         stream_grad,
-        totals[:WIDTH],
-        g_qkv.reshape(w_qkv.shape).astype(F32),
-        totals[2 * WIDTH : 2 * WIDTH + HEAD],
-        totals[2 * WIDTH + HEAD :],
-        g_out.reshape(w_out.shape).astype(F32),
-        totals[WIDTH : 2 * WIDTH],
-        g_gate_up.reshape(w_gate_up.shape).astype(F32),
-        g_down.reshape(w_down.shape).astype(F32),
+        totals[0],
+        g_qkv,
+        totals[2, :HEAD],
+        totals[2, HEAD : 2 * HEAD],
+        g_out.reshape(w_out.shape),
+        totals[1],
+        g_gate_up,
+        g_down,
     )
 
 

time: 827 us -> 434 us (0.52)
  waiting for transfers between devices: 325 us -> 0 us
  Pallas kernels: 155 us -> 376 us
  blocking collectives: 93.9 us -> 0 us
  local copies, waits for them, and re-layouts: 135 us -> 49.9 us
  matrix products: 47 us -> 0 us
  other arithmetic: 42.3 us -> 6.89 us
  between operations: 14.9 us -> 0.75 us
    pallas_call x0 -> x3, Pallas kernels: none -> 232 us  [the longest x1 220 us: backward_call(): pl.pallas_call(backward_kernel, out_shape=[out((TILE, TILE), BF), out((TI...]
    unnamed x10 -> x0, waiting for transfers between devices: 156 us -> none
    reduce_scatter x3 -> x0, waiting for transfers between devices: 119 us -> none  [scatter_rows(): lax.psum_scatter(partial.astype(BF), Z, scatter_dimension=0, tiled=True)]
    psum x1 -> x0, blocking collectives: 72.2 us -> none  [body(): lax.psum(jnp.concatenate([gain_one_grad, gain_two_grad, gain_q_grad, gain...]
    dot_general x16 -> x0, matrix products: 47 us -> none  [dot(): lax.dot_general(left, right, (dims, ((), ())), preferred_element_type=F32)]
    all_gather x3 -> x0, waiting for transfers between devices: 43 us -> none  [the longest x1 24.3 us: body(): big = lax.all_gather(exchange(big.transpose(1, 0, 2, 3)), 'dp', axis=0)]
    unnamed x62 -> x13, local copies, waits for them, and re-layouts: 63.9 us -> 23.4 us
    convert_element_type x4 -> x0, local copies, waits for them, and re-layouts: 28.5 us -> none  [the longest x1 15.2 us: body(): g_gate_up.reshape(w_gate_up.shape).astype(F32)]
  transfers between devices with their start and end apart: 10 -> 0, of which waited for: 8 -> 0; matrix products, arithmetic and copies ran while one was open for 6% -> 0% of each run, Pallas kernels for 0% -> 0%
where the time goes in v2:
time: 434 us; the launch traced here: 433 us
  Pallas kernels  376 us (87%)
  local copies, waits for them, and re-layouts  49.9 us (11%)
  other arithmetic  6.89 us (2%)
    pallas_call x1, Pallas kernels, backward_call(): pl.pallas_call(backward_kernel, out_shape=[out((TILE, TILE), BF), out((TI...  220 us
    pallas_call x1, Pallas kernels, forward_call(): pl.pallas_call(forward_kernel, out_shape=[out(wide), out(wide), out((4, T...  111 us
    pallas_call x1, Pallas kernels, middle_call(): pl.pallas_call(middle_kernel, grid=(3,), out_shape=[jax.ShapeDtypeStruct(...  32.6 us
    unnamed x13, local copies, waits for them, and re-layouts  23.4 us
    transpose x4, local copies, waits for them, and re-layouts, order(): return block.transpose(2, 0, 3, 1, 4).reshape(2, -1, 2 * UNITS)  11.8 us
    pallas_call x1, Pallas kernels, place_big(): pl.pallas_call(place_big_kernel, grid=(4, 3), in_specs=[pl.BlockSpec((DP,...  9.41 us
    reshape x2, local copies, waits for them, and re-layouts, order(): return block.transpose(2, 0, 3, 1, 4).reshape(2, -1, 2 * UNITS)  8.76 us

profile of v2, /device:TPU:0, one launch (start us, length us, event | category | flops | bytes accessed | tf_op | source)
XLA Modules:
  0.0 433.4 jit_solution(2479705274620277010)
XLA Ops:
  0.6 0.0 copy-start.2
  0.7 0.8 broadcast_compare_fusion
  1.5 0.7 add.31
  2.2 0.1 pad.6.clone
  2.2 0.8 select_reduce_fusion
  3.1 1.4 maximum_maximum_fusion.gains
  4.4 1.0 copy.48.start
  5.5 1.9 fusion.2
  7.4 1.3 pad_maximum_fusion
  8.7 0.0 copy-done.2
  8.7 0.4 copy.50
  9.1 0.7 dynamic-slice_bitcast_fusion.3.wq_part
  9.8 1.0 dynamic-slice_bitcast_fusion.1.wq_pair
  10.8 16.1 %copy.43 = bf16[512,2,3072]{0,2,1:T(8,128)(2,1)} copy(bf16[512,2,3072]{2,1,0:T(2,128)(2,1)} %param.20) | data formatting | bytes 12582912 | tf_op args[7]
  26.9 2.6 dynamic-slice_bitcast_fusion.2
  29.5 2.3 dynamic-slice_bitcast_fusion
  31.8 1.4 copy.47
  33.2 0.8 reshape.64.wg_part
  34.0 5.5 %copy.45 = bf16[2,512,3,2,256]{4,3,2,1,0:T(2,128)(2,1)} copy(bf16[2,512,3,2,256]{1,4,2,0,3:T(8,128)(2,1)S(1)} %dynamic-slice_bitcast_fusion) | data formatting | bytes 6291456 | tf_op jit(solution)/shard_map/transpose | solution.py:1215
  39.5 8.0 %reshape.63.wg_pair = bf16[2,512,1536]{2,1,0:T(8,128)(2,1)} reshape(bf16[2,512,3,2,256]{4,3,2,1,0:T(2,128)(2,1)} %copy.45) | data formatting | bytes 6291456 | tf_op jit(solution)/shard_map/reshape | solution.py:1215
  47.5 110.8 %forward.1 = (bf16[1024,2048]{1,0:T(8,128)(2,1)}, bf16[1024,2048]{1,0:T(8,128)(2,1)}, bf16[4,512,512]{2,1,0:T(8,128)(2,1)}, bf16[4,256,512]{2,1,0:T(8,128)(2,1)}...) custom-call(bf16[512,512]{1,0:T(8,128)(2,1)} %tok.1, ...), custom_call_target="tpu_custom_call" | custom-call | flops 4000000000 | bytes 60000000 | tf_op jit(solution)/shard_map/forward/pallas_call | solution.py:537
  158.3 32.6 %feed_forward.1 = (bf16[16,3,4,48,512]{4,3,2,1,0:T(8,128)(2,1)}, bf16[1024,1536]{1,0:T(8,128)(2,1)}, bf16[1024,768]{1,0:T(8,128)(2,1)}) custom-call(bf16[1024,2048]{1,0:T(8,128)(2,1)} %get-tuple-element.37.h2, bf16[1024,2048]{1,0:T(8,128)(2,1)} %get-tuple-element.38.g.g_i, bf16[4,512,1536]{2,1,0:T(8,128)(2,1)} %get-tuple-element.39.wg.wg_i, ...), custom_call_target="tpu_custom_call" | custom-call | flops 19000000512 | bytes 32000000 | tf_op jit(solution)/shard_map/feed_forward/pallas_call | solution.py:600
  190.8 219.8 %backward.1 = (bf16[512,512]{1,0:T(8,128)(2,1)}, f32[512,512]{1,0:T(8,128)}, bf16[4,4,4,3,48,512]{5,4,3,2,1,0:T(8,128)(2,1)}, bf16[4,4,4,1,48,512]{5,4,3,2,1,0:T(8,128)(2,1)}, f32[8,2048]{1,0:T(8,128)}) custom-call(bf16[4,4,3,4,48,512]{5,4,3,2,1,0:T(8,128)(2,1)} %bitcast.49, bf16[1024,1536]{1,0:T(8,128)(2,1)} %get-tuple-element.42.ggu_i, ...), custom_call_target="tpu_custom_call" | custom-call | flops 15000000512 | bytes 100000000 | tf_op jit(solution)/shard_map/backward/pallas_call | solution.py:1097
  410.7 1.2 slice_bitcast_fusion
  411.9 1.5 fusion.3
  413.4 1.9 copy-done.1
  415.3 3.2 place_small.1
  418.5 3.7 copy-done
  422.2 9.4 %place_big.1 = (f32[512,2,3072]{2,1,0:T(2,128)}, f32[3072,512]{1,0:T(8,128)}) custom-call(bf16[16,4,3,48,512]{4,3,2,1,0:T(8,128)(2,1)S(1)} %bitcast.33), custom_call_target="tpu_custom_call" | custom-call | bytes 29000000 | tf_op jit(solution)/shard_map/place_big/pallas_call | solution.py:1133
  431.6 0.0 copy-done.4
  431.6 0.8 copy.55
  432.4 1.0 copy.56
  (8 shorter events, 0.0 us)
Async XLA Ops:
  0.6 8.1 %copy-start.2 = (bf16[512,4,512]{2,1,0:T(4,128)(2,1)S(1)}, bf16[512,4,512]{2,1,0:T(4,128)(2,1)}, u32[]{:S(2)}) copy-start(bf16[512,4,512]{2,1,0:T(4,128)(2,1)} %param.15) | copy-start | bytes 6291460
  413.4 1.9 copy-start.1
  418.5 3.7 copy-start
  422.2 9.4 %copy-start.4 = (bf16[512,512]{1,0:T(8,128)(2,1)S(1)}, bf16[512,512]{1,0:T(8,128)(2,1)}, u32[]{:S(2)}) copy-start(bf16[512,512]{1,0:T(8,128)(2,1)} %get-tuple-element.83) | copy-start | bytes 1572868
  422.2 10.2 %copy-start.3 = (f32[512,512]{1,0:T(8,128)S(1)}, f32[512,512]{1,0:T(8,128)}, u32[]{:S(2)}) copy-start(f32[512,512]{1,0:T(8,128)} %get-tuple-element.84) | copy-start | bytes 3145732

commit v3 on v2

v3 whole, which is shorter than its diff:
```python
import math

import jax
import jax.numpy as jnp
import numpy as np
from jax import lax
from jax.experimental import pallas as pl
from jax.experimental.pallas import tpu as pltpu
from jax.sharding import PartitionSpec as P

EPS = 1e-06
THETA = 1000000.0
BF = jnp.bfloat16
F32 = jnp.float32
Z = ("row", "col")
MESH = pl.DeviceIdType.MESH
VMEM_LIMIT = 63 * 1024 * 1024

GROUP, WIDTH, TILE, UNITS, HEAD = 1024, 2048, 512, 768, 128
OWN = GROUP // 8
DP = 16


def dot(left, right, dims):
    return lax.dot_general(left, right, (dims, ((), ())), preferred_element_type=F32)


def mm(left, right):
    return dot(left, right, ((1,), (0,)))


def mm_t(left, right):
    return dot(left, right, ((1,), (1,)))


def t_mm(left, right):
    return dot(left, right, ((0,), (0,)))


def place():
    row, col = lax.axis_index("row"), lax.axis_index("col")
    j = 4 * row + col
    return lax.axis_index("dp"), row, col, j // 2, j % 2


def on_ring(z, k):
    j = 2 * z + k
    return {"row": j // 4, "col": j % 4}


def remote(src, dst, send, recv, device):
    return pltpu.make_async_remote_copy(
        src_ref=src, dst_ref=dst, send_sem=send, recv_sem=recv, device_id=device, device_id_type=MESH
    )


def meet(devices):
    barrier = pltpu.get_barrier_semaphore()
    for device in devices:
        pl.semaphore_signal(barrier, inc=1, device_id=device, device_id_type=MESH)
    pl.semaphore_wait(barrier, len(devices))


def ring_friends():
    _, _, _, z, k = place()
    other = z + 1 - 2 * (z % 2)
    return [
        on_ring((z + 1) % 4, k),
        on_ring((z + 3) % 4, k),
        on_ring(z, 1 - k),
        on_ring(other, 1 - k),
    ]


def dp_place():
    p = lax.axis_index("dp")
    return p // 4, p % 4


def along(axis, o):
    px, py = dp_place()
    return {"dp": (px + o) % 4 * 4 + py} if axis == 0 else {"dp": px * 4 + (py + o) % 4}


def xy_friends():
    return [along(axis, o) for axis in range(2) for o in range(1, 4)]


def tile_at(buf):
    def loc(j, half=None):
        row, col = j // 4, j % 4
        first = pl.multiple_of(row * TILE, TILE)
        rows = pl.ds(first, TILE)
        if half is not None:
            rows = pl.ds(first + half * (TILE // 2), TILE // 2)
        return buf.at[rows, pl.ds(pl.multiple_of(col * TILE, TILE), TILE)]

    return loc


def rows_at(buf):
    def loc(j, half=None):
        first = pl.multiple_of(j * OWN, OWN)
        rows = pl.ds(first, OWN)
        if half is not None:
            rows = pl.ds(first + half * (OWN // 2), OWN // 2)
        return buf.at[rows]

    return loc


class Gather:
    def __init__(self, loc, send, recv, own=None):
        _, _, _, z, k = place()
        up, down, far = (z + 1) % 4, (z + 3) % 4, (z + 2) % 4
        to_up, to_down, peer = on_ring(up, k), on_ring(down, k), on_ring(z, 1 - k)

        def out(slot, src, dst, device):
            return remote(src, dst, send.at[slot], recv.at[slot], device)

        def into(slot, dst):
            return remote(dst, dst, send.at[slot], recv.at[slot], peer)

        mine = loc(2 * z + k)
        own = mine if own is None else own
        left, right, across = 2 * down + k, 2 * up + k, 2 * far + k
        self.first = [out(0, own, mine, to_up), out(1, own, mine, to_down), out(4, own, mine, peer)]
        self.from_left = [
            out(2, loc(left, 0), loc(left, 0), to_up),
            out(5, loc(left), loc(left), peer),
        ]
        self.from_right = [
            out(3, loc(right, 1), loc(right, 1), to_down),
            out(6, loc(right), loc(right), peer),
        ]
        self.from_far = [
            out(7, loc(across, 0), loc(across, 0), peer),
            out(8, loc(across, 1), loc(across, 1), peer),
        ]
        theirs = [2 * z + 1 - k, 2 * down + 1 - k, 2 * up + 1 - k, 2 * far + 1 - k]
        self.arrivals = {
            0: into(0, loc(left)),
            1: into(1, loc(right)),
            2: into(2, loc(across, 0)),
            3: into(3, loc(across, 1)),
            4: into(4, loc(theirs[0])),
            5: into(5, loc(theirs[1])),
            6: into(6, loc(theirs[2])),
            7: into(7, loc(theirs[3], 0)),
            8: into(8, loc(theirs[3], 1)),
        }

    def start(self):
        for copy in self.first:
            copy.start()

    def forward(self):
        self.arrivals[0].wait_recv()
        for copy in self.from_left:
            copy.start()
        self.arrivals[1].wait_recv()
        for copy in self.from_right:
            copy.start()

    def share(self):
        for half in range(2):
            self.arrivals[2 + half].wait_recv()
            self.from_far[half].start()

    def finish(self):
        for slot in range(4, 9):
            self.arrivals[slot].wait_recv()

    def drain(self):
        for copy in self.first + self.from_left + self.from_right + self.from_far:
            copy.wait_send()


GATHER_SEMS = [pltpu.SemaphoreType.DMA((9,)), pltpu.SemaphoreType.DMA((9,))]


class Spread:
    def __init__(self, at, send, recv, which=()):
        px, py = dp_place()
        here = (px, py)
        self.out, self.into = {}, {}
        for half in range(2):
            for phase in range(2):
                axis = half ^ phase

                def block(o, part=None):
                    whose = [px, py]
                    whose[axis] = (here[axis] + o) % 4
                    if phase:
                        whose[1 - axis] = None
                    return at(half, *whose, part)

                def copy(slot, ref, o):
                    index = (*which, half, phase, slot)
                    sems = (send.at[index], recv.at[index])
                    return remote(ref, ref, *sems, along(axis, o))

                self.out[half, phase] = [
                    copy(0, block(0), 1), copy(1, block(0), 3),
                    copy(2, block(3, 0), 1), copy(3, block(1, 1), 3),
                ]
                self.into[half, phase] = [
                    copy(0, block(3), 1), copy(1, block(1), 3),
                    copy(2, block(2, 0), 1), copy(3, block(2, 1), 3),
                ]

    def start(self, phase):
        for half in range(2):
            for slot in range(2):
                self.out[half, phase][slot].start()

    def pass_on(self, phase):
        for half in range(2):
            for slot in range(2):
                self.into[half, phase][slot].wait_recv()
                self.out[half, phase][2 + slot].start()

    def wait(self, phase):
        for half in range(2):
            for slot in range(2, 4):
                self.into[half, phase][slot].wait_recv()

    def drain(self):
        for copies in self.out.values():
            for copy in copies:
                copy.wait_send()


SPREAD_SEMS = [pltpu.SemaphoreType.DMA((2, 2, 4)), pltpu.SemaphoreType.DMA((2, 2, 4))]


class Scatter:
    def __init__(self, parts, theirs, sums, near, full, send, recv):
        _, _, _, z, k = place()
        self.parts, self.theirs, self.sums, self.near, self.full = parts, theirs, sums, near, full
        self.k = k
        to_up, to_down = on_ring((z + 1) % 4, k), on_ring((z + 3) % 4, k)
        peer = on_ring(z, 1 - k)
        half = OWN // 2
        other = pl.ds(pl.multiple_of((1 - k) * OWN, OWN), OWN)

        def copy(slot, src, dst, device):
            return remote(src, dst, send.at[slot], recv.at[slot], device)

        self.copies = [copy(d, parts.at[d, other], theirs.at[d], peer) for d in range(4)] + [
            copy(4, sums.at[0, pl.ds(0, half)], near.at[0], to_up),
            copy(5, sums.at[0, pl.ds(half, half)], near.at[1], to_down),
            copy(6, sums.at[1], full.at[0], to_up),
            copy(7, sums.at[2], full.at[1], to_down),
        ]

    def put(self, d):
        self.copies[d].start()

    def own(self, d, rows, count):
        first = pl.multiple_of(self.k * OWN + rows, count)
        return self.parts[d, pl.ds(first, count)].astype(F32) + self.theirs[
            d, pl.ds(rows, count)
        ].astype(F32)

    def across(self):
        self.copies[2].wait_recv()

        @pl.loop(0, OWN // 16)
        def _(i):
            rows = pl.multiple_of(i * 16, 16)
            self.sums[0, pl.ds(rows, 16)] = self.own(2, rows, 16).astype(BF)

        self.copies[4].start()
        self.copies[5].start()

    def beside(self, side):
        d, half = (1, 3)[side], OWN // 2
        self.copies[d].wait_recv()
        self.copies[4 + side].wait_recv()

        @pl.loop(0, half // 16)
        def _(i):
            rows = pl.multiple_of(i * 16, 16)
            here = pl.multiple_of(rows + side * half, 16)
            there = pl.multiple_of(rows + (1 - side) * half, 16)
            added = self.own(d, here, 16) + self.near[side, pl.ds(rows, 16)].astype(F32)
            self.sums[1 + side, pl.ds(here, 16)] = added.astype(BF)
            self.sums[1 + side, pl.ds(there, 16)] = self.own(d, there, 16).astype(BF)

        self.copies[6 + side].start()

    def arrive(self):
        self.copies[0].wait_recv()
        self.copies[6].wait_recv()
        self.copies[7].wait_recv()

    def total(self, rows, count):
        return (
            self.own(0, rows, count)
            + self.full[0, pl.ds(rows, count)].astype(F32)
            + self.full[1, pl.ds(rows, count)].astype(F32)
        )

    def drain(self):
        for copy in self.copies:
            copy.wait_send()


def scatter_scratch():
    return [
        pltpu.VMEM((4, 2 * OWN, WIDTH), BF),
        pltpu.VMEM((4, OWN, WIDTH), BF),
        pltpu.VMEM((3, OWN, WIDTH), BF),
        pltpu.VMEM((2, OWN // 2, WIDTH), BF),
        pltpu.VMEM((2, OWN, WIDTH), BF),
        pltpu.SemaphoreType.DMA((8,)),
        pltpu.SemaphoreType.DMA((8,)),
    ]


def head_norm(value):
    return lax.rsqrt(jnp.mean(value * value, axis=1, keepdims=True) + EPS)


def turn(value, cosine, sine):
    return value * cosine + pltpu.roll(value, HEAD // 2, 1) * sine


def turn_back(value, cosine, sine):
    return value * cosine - pltpu.roll(value, HEAD // 2, 1) * sine


LOG2 = math.log2(math.e)
SCALE = 1.0 / math.sqrt(HEAD)
QROWS = 256


def allowed_keys(start, first, keys):
    slots = lax.broadcasted_iota(jnp.int32, (QROWS, keys), 1)
    query = lax.broadcasted_iota(jnp.int32, (QROWS, keys), 0) + first
    return (slots >= start) & (slots <= query)


FREQ = np.tile(THETA ** (-(np.arange(HEAD // 2) * 2.0 / HEAD)), 2)[None].astype(np.float32)


def forward_kernel(
    tok, og, norm1, norm2, q_gain, k_gain, freq, lengths, groups, starts, w_qkv, w_gu, w_out, w_down,
    h2_o, g_o, wq_o, wo_o, wg_o, wd_o, h1t_o, raw_o, q_o, k_o, att_o, lse_o, mid_o, gain_o, x_o, start_o, cos_o, sin_o,
    x, h1, h1t, h2, g, wq, wo, raw, qs, ks, att, lse, mid, gain, gains, start, cosine, sine,
    q_raw, q_cut, q_raw_part, q_part, g_raw, g_cut, g_raw_part, g_part,
    xs, xr, gs, gr, hs, hr,
    parts, theirs, sums, near, full, rs_s, rs_r,
    zs, zr, ps, pr, ns, nr, loc_s, out_s, raw_s,
    y0s, y0r, y1s, y1r, y2s, y2r, y3s, y3r,
):
    p, row, col, z, k = place()
    px, py = dp_place()
    me = 2 * z + k
    lo = z % 2
    other = z + 1 - 2 * lo
    peer = on_ring(z, 1 - k)
    piece_rows = pl.ds(pl.multiple_of(p * 32, 32), 32)

    def lanes(first, count):
        return pl.ds(pl.multiple_of(first, 256), count)

    raws = [
        pltpu.make_async_copy(src, dst, raw_s.at[i])
        for i, (src, dst) in enumerate(
            [
                (w_qkv.at[piece_rows], q_raw_part),
                (w_gu.at[piece_rows, :, lanes((1 - lo) * 2 * UNITS, 2 * UNITS)], g_raw_part),
                (w_qkv, q_raw),
                (w_gu.at[:, :, lanes(lo * 2 * UNITS, 2 * UNITS)], g_raw),
            ]
        )
    ]
    for copy in raws:
        copy.start()
    gains[0:1] = norm1[...]
    gains[1:2] = norm2[...]
    raws[0].wait()
    for kk in range(2):
        q_part[kk] = jnp.where(lo == 0, q_raw_part[:, 2 + kk, :], q_raw_part[:, kk, :])
    meet(ring_friends() + xy_friends())

    gain[col] = gains[...]
    gain_copies = [
        remote(gains, gain.at[col], ns.at[i], nr.at[col], device)
        for i, device in enumerate([peer, on_ring(other, k), on_ring(other, 1 - k)])
    ]
    weights = [wq, wo, wg_o, wd_o]
    sources = [q_part, w_out, g_part, w_down]
    blocks = [q_cut, w_out, g_cut, w_down]

    def crossing(a, kk):
        target = 2 * (1 - lo) + kk
        src = sources[a].at[kk] if a % 2 == 0 else w_out.at[target, px, py] if a == 1 else w_down.at[target, px, py]
        return remote(src, weights[a].at[col, px, py], zs.at[a, kk], zr.at[a, k], on_ring(other, kk))

    def crossed(a, kk):
        dst = weights[a].at[2 * (1 - lo) + kk, px, py]
        return remote(dst, dst, zs.at[a, kk], zr.at[a, kk], peer)

    def beside(a):
        there = 2 * lo + 1 - k
        src, dst = (blocks[a].at[k], blocks[a].at[1 - k]) if a % 2 == 0 else (blocks[a].at[col], blocks[a].at[there])
        keep = pltpu.make_async_copy(src, weights[a].at[col], loc_s.at[a])
        give = remote(dst, weights[a].at[col], ps.at[a], pr.at[a], peer)
        take = remote(weights[a].at[there], weights[a].at[there], ps.at[a], pr.at[a], peer)
        return keep, give, take

    def spread_at(a):
        weight = weights[a]
        half_lanes = weight.shape[-1] // 2

        def at(half, xx, yy, part):
            xs_ = slice(None) if xx is None else xx
            ys_ = slice(None) if yy is None else yy
            cols = slice(None) if part is None else pl.ds(part * half_lanes, half_lanes)
            return weight.at[2 * (1 - lo) + half, xs_, ys_, :, cols]

        return at

    spreads = [
        Spread(spread_at(a), send, recv)
        for a, (send, recv) in enumerate([(y0s, y0r), (y1s, y1r), (y2s, y2r), (y3s, y3r)])
    ]

    for a in (0, 1):
        for kk in range(2):
            crossing(a, kk).start()
    x_gather = Gather(tile_at(x), xs, xr, tok)
    x_gather.start()
    for copy in gain_copies:
        copy.start()
    keep_x = pltpu.make_async_copy(tok, tile_at(x)(me), loc_s.at[4])
    keep_x.start()
    keep_g = pltpu.make_async_copy(og, tile_at(g)(me), loc_s.at[5])
    keep_g.start()
    raws[2].wait()

    @pl.loop(0, 16)
    def _(i):
        rows = pl.ds(pl.multiple_of(i * 32, 32), 32)
        for kk in range(2):
            q_cut[kk, i // 4, i % 4] = jnp.where(lo == 0, q_raw[rows, kk, :], q_raw[rows, 2 + kk, :])

    for a in (0, 1):
        beside(a)[0].start()
        beside(a)[1].start()
    for a in (0, 1):
        for kk in range(2):
            crossed(a, kk).wait_recv()
        spreads[a].start(0)
    for a in (1, 3):
        raws[a].wait()
    slot = (
        lax.broadcasted_iota(jnp.int32, (8, HEAD), 0) * HEAD + lax.broadcasted_iota(jnp.int32, (8, HEAD), 1)
    ).astype(F32)

    def one_sequence(i, begun):
        first = starts[i].astype(F32)
        last = first + jnp.where(groups[i] == p, lengths[i], 0).astype(F32)
        return jnp.where((slot >= first) & (slot < last), first, begun)

    begun = lax.fori_loop(0, lengths.shape[0], one_sequence, jnp.zeros((8, HEAD), F32))
    for i in range(8):
        rows = slice(i * HEAD, (i + 1) * HEAD)
        begin = jnp.broadcast_to(begun[i : i + 1], (HEAD, HEAD)).T
        there = lax.broadcasted_iota(jnp.int32, (HEAD, HEAD), 0).astype(F32) + float(i * HEAD)
        angle = (there - begin) * freq[...]
        start[rows] = begin.astype(jnp.int32)
        cosine[rows] = jnp.cos(angle)
        lane = lax.broadcasted_iota(jnp.int32, (HEAD, HEAD), 1)
        sine[rows] = jnp.where(lane < HEAD // 2, -1.0, 1.0) * jnp.sin(angle)
    for a in (0, 1):
        spreads[a].pass_on(0)
    for u in range(3):
        for half in range(2):
            into = slice(u * 512 + half * 256, u * 512 + half * 256 + 256)
            for kk in range(2):
                cols = slice(kk * UNITS + u * 256, kk * UNITS + u * 256 + 256)
                g_part[kk, :, into] = g_raw_part[:, half, cols]
    for a in (0, 1):
        spreads[a].wait(0)
        spreads[a].start(1)
    x_gather.forward()

    @pl.loop(0, 16)
    def _(i):
        rows = pl.ds(pl.multiple_of(i * 32, 32), 32)
        for u in range(3):
            for half in range(2):
                into = slice(u * 512 + half * 256, u * 512 + half * 256 + 256)
                for kk in range(2):
                    cols = slice(kk * UNITS + u * 256, kk * UNITS + u * 256 + 256)
                    g_cut[kk, i // 4, i % 4, :, into] = g_raw[rows, half, cols]

    for a in (0, 1):
        spreads[a].pass_on(1)
    x_gather.share()
    for a in (2, 3):
        for kk in range(2):
            crossing(a, kk).start()
    for a in (2, 3):
        beside(a)[0].start()
        beside(a)[1].start()
    for c in range(4):

        @pl.when(c != col)
        def _():
            remote(gain.at[c], gain.at[c], ns.at[0], nr.at[c], peer).wait_recv()

    keep_x.wait()
    x_gather.finish()
    g_gather = Gather(tile_at(g), gs, gr, og)
    g_gather.start()

    def gain_row(which):
        return jnp.concatenate([gain[c, which : which + 1] for c in range(4)], axis=1)

    gain_one = gain_row(0)

    @pl.loop(0, GROUP // 64)
    def _(i):
        rows = pl.ds(pl.multiple_of(i * 64, 64), 64)
        value = x[rows].astype(F32)
        h1[rows] = (value * head_norm(value) * gain_one).astype(BF)

    for a in (2, 3):
        for kk in range(2):
            crossed(a, kk).wait_recv()
        spreads[a].start(0)
    for a in range(2):
        keep, _, take = beside(a)
        keep.wait()
        take.wait_recv()
        spreads[a].wait(1)

    @pl.loop(0, GROUP // 256)
    def _(i):
        rows = pl.ds(pl.multiple_of(i * 256, 256), 256)
        mixed = mm(h1[rows], wq[...].reshape(WIDTH, 4 * HEAD)).astype(BF)
        raw[rows] = mixed
        cos_rows, sin_rows = cosine[rows], sine[rows]
        for piece in range(3):
            value = mixed[:, piece * HEAD : (piece + 1) * HEAD].astype(F32)
            by = q_gain[...] if piece < 2 else k_gain[...]
            turned = turn(value * head_norm(value) * by, cos_rows, sin_rows).astype(BF)
            if piece < 2:
                qs[piece, rows] = turned
            else:
                ks[rows] = turned

    for a in (2, 3):
        spreads[a].pass_on(0)
    g_gather.forward()
    saves = [
        pltpu.make_async_copy(src, dst, out_s.at[i])
        for i, (src, dst) in enumerate(
            [
                (wq, wq_o), (raw, raw_o), (qs, q_o), (ks, k_o), (gain, gain_o),
                (x.at[pl.ds(pl.multiple_of(me * OWN, OWN), OWN)], x_o), (wo, wo_o),
                (att, att_o), (lse, lse_o), (g, g_o), (mid, mid_o), (h2, h2_o), (h1t, h1t_o), (start, start_o), (cosine, cos_o), (sine, sin_o),
            ]
        )
    ]
    for i in (0, 1, 2, 3, 4, 5, 6, 13, 14, 15):
        saves[i].start()

    for block in range(GROUP // QROWS):
        first, keys = block * QROWS, (block + 1) * QROWS
        rows = pl.ds(first, QROWS)
        allowed = allowed_keys(start[rows, :1], first, keys)

        @pl.loop(0, 2)
        def _(h):
            score = mm_t(qs[h, rows], ks[:keys]) * (SCALE * LOG2)
            score = jnp.where(allowed, score, -1e30)
            peak = jnp.max(score, axis=1, keepdims=True)
            weight = jnp.exp2(score - peak)
            total = jnp.sum(weight, axis=1, keepdims=True)
            out = mm(weight.astype(BF), raw[:keys, 3 * HEAD :]) / total
            att[h, rows] = out.astype(BF)
            lse[h, rows] = jnp.broadcast_to(peak + jnp.log2(total), (QROWS, HEAD))

    for a in (2, 3):
        spreads[a].wait(0)
        spreads[a].start(1)
    saves[7].start()
    saves[8].start()
    g_gather.share()

    scatter = Scatter(parts, theirs, sums, near, full, rs_s, rs_r)

    def project(d):
        rows = pl.ds(pl.multiple_of((z + d) % 4 * 256, 256), 256)
        left = jnp.concatenate([att[0, rows], att[1, rows]], axis=1)
        for c in range(4):
            parts[d, :, c * TILE : (c + 1) * TILE] = mm(left, wo[c].reshape(256, TILE)).astype(BF)
        scatter.put(d)

    project(2)
    project(1)
    scatter.across()
    project(3)
    project(0)
    scatter.beside(0)
    scatter.beside(1)

    @pl.loop(0, 8)
    def _(i):
        cols = pl.ds(pl.multiple_of(i * 256, 256), 256)
        h1t[cols] = h1[:, cols].T

    saves[12].start()
    for a in (2, 3):
        spreads[a].pass_on(1)
    g_gather.finish()
    keep_g.wait()
    saves[9].start()
    scatter.arrive()
    gain_two = gain_row(1)

    @pl.loop(0, OWN // 16)
    def _(i):
        first = pl.multiple_of(i * 16, 16)
        there = pl.ds(pl.multiple_of(me * OWN + first, 16), 16)
        value = x[there].astype(F32) + scatter.total(first, 16)
        mid[pl.ds(first, 16)] = value
        h2[there] = (value * head_norm(value) * gain_two).astype(BF)

    saves[10].start()
    h2_gather = Gather(rows_at(h2), hs, hr)
    h2_gather.start()
    h2_gather.forward()
    for a in (2, 3):
        keep, _, take = beside(a)
        keep.wait()
        take.wait_recv()
        spreads[a].wait(1)
    h2_gather.share()
    h2_gather.finish()
    saves[11].start()
    for copy in gain_copies:
        copy.wait_send()
    for a in range(4):
        beside(a)[1].wait_send()
        for kk in range(2):
            crossing(a, kk).wait_send()
    for spread in spreads:
        spread.drain()
    x_gather.drain()
    g_gather.drain()
    h2_gather.drain()
    scatter.drain()
    for copy in saves:
        copy.wait()


def forward_call(*args):
    hbm = pl.BlockSpec(memory_space=pl.ANY)
    vmem = pl.BlockSpec(memory_space=pltpu.VMEM)
    smem = pl.BlockSpec(memory_space=pltpu.SMEM)
    dma = pltpu.SemaphoreType.DMA

    def out(shape, dtype=BF):
        return jax.ShapeDtypeStruct(shape, dtype)

    wide = (GROUP, WIDTH)
    return pl.pallas_call(
        forward_kernel,
        out_shape=[
            out(wide), out(wide), out((4, 4, 4, 32, 512)), out((4, 4, 4, 16, TILE)), out((4, 4, 4, 32, 2 * UNITS)),
            out((4, 4, 4, 48, TILE)), out((WIDTH, GROUP)), out((GROUP, 512)), out((2, GROUP, HEAD)), out((GROUP, HEAD)),
            out((2, GROUP, HEAD)), out((2, GROUP, HEAD), F32), out((OWN, WIDTH), F32), out((4, 8, TILE), F32),
            out((OWN, WIDTH)), out((GROUP, HEAD), jnp.int32), out((GROUP, HEAD), F32), out((GROUP, HEAD), F32),
        ],
        in_specs=[vmem] * 7 + [smem] * 3 + [hbm] * 4,
        out_specs=[hbm] * 18,
        scratch_shapes=[
            pltpu.VMEM(wide, BF), pltpu.VMEM(wide, BF), pltpu.VMEM((WIDTH, GROUP), BF), pltpu.VMEM(wide, BF),
            pltpu.VMEM(wide, BF), pltpu.VMEM((4, 4, 4, 32, 512), BF), pltpu.VMEM((4, 4, 4, 16, TILE), BF),
            pltpu.VMEM((GROUP, 512), BF), pltpu.VMEM((2, GROUP, HEAD), BF), pltpu.VMEM((GROUP, HEAD), BF),
            pltpu.VMEM((2, GROUP, HEAD), BF), pltpu.VMEM((2, GROUP, HEAD), F32), pltpu.VMEM((OWN, WIDTH), F32),
            pltpu.VMEM((4, 8, TILE), F32), pltpu.VMEM((8, TILE), F32), pltpu.VMEM((GROUP, HEAD), jnp.int32),
            pltpu.VMEM((GROUP, HEAD), F32), pltpu.VMEM((GROUP, HEAD), F32),
            pltpu.VMEM((TILE, 4, 512), BF), pltpu.VMEM((2, 4, 4, 32, 512), BF), pltpu.VMEM((32, 4, 512), BF),
            pltpu.VMEM((2, 32, 512), BF), pltpu.VMEM((TILE, 2, 2 * UNITS), BF), pltpu.VMEM((2, 4, 4, 32, 2 * UNITS), BF),
            pltpu.VMEM((32, 2, 2 * UNITS), BF), pltpu.VMEM((2, 32, 2 * UNITS), BF),
        ]
        + GATHER_SEMS * 3
        + scatter_scratch()
        + [dma((4, 2)), dma((4, 2)), dma((4,)), dma((4,)), dma((3,)), dma((4,)), dma((6,)), dma((16,)), dma((4,))]
        + SPREAD_SEMS * 4,
        compiler_params=pltpu.CompilerParams(
            collective_id=1, has_side_effects=True, vmem_limit_bytes=VMEM_LIMIT
        ),
        cost_estimate=pl.CostEstimate(flops=4_000_000_000, bytes_accessed=60_000_000, transcendentals=2_000_000),
        name="forward",
    )(*args)


def middle_kernel(h2, g, wg, wd, ggu, hid):
    @pl.loop(0, GROUP // 256)
    def _(i):
        rows = pl.ds(pl.multiple_of(i * 256, 256), 256)
        pair = mm(h2[rows], wg[...].reshape(WIDTH, 512))
        back = mm_t(g[rows, :TILE], wd[0])
        for c in range(1, 4):
            back += mm_t(g[rows, c * TILE : (c + 1) * TILE], wd[c])
        gate, up = pair[:, :256], pair[:, 256:]
        sig = 1.0 / (1.0 + jnp.exp(-gate))
        silu = gate * sig
        hid[rows] = (silu * up).astype(BF)
        ggu[rows, :256] = (back * up * sig * (1.0 + gate * (1.0 - sig))).astype(BF)
        ggu[rows, 256:] = (back * silu).astype(BF)


def middle_call(h2, g, wg, wd):
    wide = pl.BlockSpec((GROUP, WIDTH), lambda u: (0, 0), pipeline_mode=pl.Buffered(1))
    return pl.pallas_call(
        middle_kernel,
        grid=(3,),
        out_shape=[
            jax.ShapeDtypeStruct((GROUP, 2 * UNITS), BF),
            jax.ShapeDtypeStruct((GROUP, UNITS), BF),
        ],
        in_specs=[
            wide,
            wide,
            pl.BlockSpec((4, TILE, 512), lambda u: (0, 0, u)),
            pl.BlockSpec((4, 256, TILE), lambda u: (0, u, 0)),
        ],
        out_specs=[
            pl.BlockSpec((GROUP, 512), lambda u: (0, u)),
            pl.BlockSpec((GROUP, 256), lambda u: (0, u)),
        ],
        compiler_params=pltpu.CompilerParams(vmem_limit_bytes=VMEM_LIMIT),
        cost_estimate=pl.CostEstimate(flops=9_600_000_000, bytes_accessed=22_000_000, transcendentals=800_000),
        name="feed_forward",
    )(h2, g, wg, wd)


class Collapse:
    def __init__(self, which, src, got, sums, got2, done, send, recv, own):
        px, py = dp_place()
        here = (px, py)
        self.which = which
        self.got, self.sums, self.got2, self.done, self.here = got, sums, got2, done, here

        def cut(axis, index, half):
            pair = pl.ds(2 * half, 2)
            return src.at[which, index, :, pair] if axis == 0 else src.at[which, :, index, pair]

        self.keep, self.copies = [], {}
        for half in range(2):
            axis = half
            self.keep.append(pltpu.make_async_copy(cut(axis, here[axis], half), sums.at[which, half], own.at[which, half]))
            for o in range(1, 4):
                there = (here[axis] + o) % 4
                self.copies[half, 0, o] = remote(
                    cut(axis, there, half), got.at[which, half, o - 1],
                    send.at[which, half, 0, o - 1], recv.at[which, half, 0, o - 1], along(axis, o),
                )
                there = (here[1 - axis] + o) % 4
                self.copies[half, 1, o] = remote(
                    sums.at[which, half, there], got2.at[which, half, o - 1],
                    send.at[which, half, 1, o - 1], recv.at[which, half, 1, o - 1], along(1 - axis, o),
                )

    def start(self):
        for half in range(2):
            for o in range(1, 4):
                self.copies[half, 0, o].start()
            self.keep[half].start()

    def first(self):
        for half in range(2):
            self.keep[half].wait()
            for o in range(1, 4):
                self.copies[half, 0, o].wait_recv()

            @pl.loop(0, 8)
            def _(i):
                a, c = i // 2, i % 2
                total = self.sums[self.which, half, a, c].astype(F32)
                for o in range(3):
                    total += self.got[self.which, half, o, a, c].astype(F32)
                self.sums[self.which, half, a, c] = total.astype(BF)

            for o in range(1, 4):
                self.copies[half, 1, o].start()

    def second(self):
        for half in range(2):
            for o in range(1, 4):
                self.copies[half, 1, o].wait_recv()
            for c in range(2):
                total = self.sums[self.which, half, self.here[1 - half], c].astype(F32)
                for o in range(3):
                    total += self.got2[self.which, half, o, c].astype(F32)
                self.done[self.which, 2 * half + c] = total.astype(BF)

    def drain(self):
        for copy in self.copies.values():
            copy.wait_send()


CHUNKS = 4


def collapse_scratch():
    dma = pltpu.SemaphoreType.DMA
    return [
        pltpu.VMEM((CHUNKS, 2, 3, 4, 2, 48, 512), BF),
        pltpu.VMEM((CHUNKS, 2, 4, 2, 48, 512), BF),
        pltpu.VMEM((CHUNKS, 2, 3, 2, 48, 512), BF),
        pltpu.VMEM((CHUNKS, 4, 48, 512), BF),
        dma((CHUNKS, 2, 2, 3)), dma((CHUNKS, 2, 2, 3)), dma((CHUNKS, 2)),
        dma((CHUNKS, 3)), dma((CHUNKS, 4)), dma((CHUNKS, 2, 2, 4)), dma((CHUNKS, 2, 2, 4)),
    ]


class Trade:
    def __init__(self, block, slot, send, recv, which=()):
        _, row, col, z, k = place()
        self.col, self.peer = col, on_ring(z, 1 - k)
        self.recv, self.send, self.slot, self.which = recv, send, slot, which
        self.copies = [
            remote(block((col + o) % 4), slot(col), send.at[(*which, o - 1)], recv.at[(*which, o - 1)], {"col": (col + o) % 4})
            for o in range(1, 4)
        ]
        self.keep = pltpu.make_async_copy(block(col), slot(col), recv.at[(*which, 3)])

    def start(self):
        for copy in self.copies:
            copy.start()
        self.keep.start()

    def finish(self):
        for o in range(1, 4):
            dst = self.slot((self.col - o + 4) % 4)
            sems = (self.send.at[(*self.which, o - 1)], self.recv.at[(*self.which, o - 1)])
            remote(dst, dst, *sems, self.peer).wait_recv()
        self.keep.wait()

    def drain(self):
        for copy in self.copies:
            copy.wait_send()


def norm_back(grad, value, gain):
    scale = head_norm(value)
    weighted = grad * gain
    inner = jnp.mean(weighted * value, axis=1, keepdims=True)
    return scale * weighted - value * (scale * scale * scale * inner), grad * value * scale


def norm_back(grad, value, gain):
    scale = head_norm(value)
    weighted = grad * gain
    inner = jnp.mean(weighted * value, axis=1, keepdims=True)
    return scale * weighted - value * (scale * scale * scale * inner), grad * value * scale


def backward_kernel(
    h2_i, ggu_i, hid_i, g_i, wg_i, wd_i, wo_i, wq_i, h1t_i, raw_i, q_i, k_i, att_i, lse_i, mid_i, gain_i, x_i,
    start_i, cos_i, sin_i, q_gain, k_gain,
    result_o, stream_o, grads_o, local_o, sums_o,
    m, gm, dqkv, stage, mid, gain, x_own, g_own, acc, head_acc, tile_f, tile_b, totals, heard,
    ms, mr,
    parts, theirs, psums, near, full, rs_s, rs_r,
    got, sums, got2, done, c_s, c_r, c_own, t_s, t_r, a_s, a_r,
    fs, fr, ls, lr, as_, ar, in_s, stage_s, free,
):
    p, row, col, z, k = place()
    px, py = dp_place()
    me = 2 * z + k
    up, down, peer = on_ring((z + 1) % 4, k), on_ring((z + 3) % 4, k), on_ring(z, 1 - k)
    far = on_ring((z + 2) % 4, k)
    loads = []

    def load(src, dst):
        copy = pltpu.make_async_copy(src, dst, in_s.at[len(loads)])
        copy.start()
        loads.append(copy)
        return copy

    def wait(copies):
        for copy in copies:
            copy.wait()

    collapses, trades, spreads = [], [], []

    def chunk(i):
        def at(half, x, y, part):
            xs = slice(None) if x is None else x
            ys = slice(None) if y is None else y
            which = pl.ds(2 * half, 2) if part is None else 2 * half + part
            return grads_o.at[i, xs, ys, which]

        collapses.append(
            Collapse(
                i, local_o, got, sums, got2, done, c_s, c_r, c_own
            )
        )
        trades.append(
            Trade(lambda c: done.at[i, c], lambda c: grads_o.at[i, px, py, c], t_s, t_r, (i,))
        )
        spreads.append(Spread(at, a_s, a_r, (i,)))

    for i in range(CHUNKS):
        chunk(i)
    scatter = Scatter(parts, theirs, psums, near, full, rs_s, rs_r)
    stream_trade = Trade(
        lambda c: tile_f.at[:, pl.ds(pl.multiple_of(c * TILE, TILE), TILE)],
        lambda c: stream_o.at[pl.ds(pl.multiple_of(c * OWN, OWN), OWN)], fs, fr,
    )
    result_trade = Trade(
        lambda c: tile_b.at[:, pl.ds(pl.multiple_of(c * TILE, TILE), TILE)],
        lambda c: result_o.at[pl.ds(pl.multiple_of(c * OWN, OWN), OWN)], ls, lr,
    )

    def release():
        scatter.drain()
        for device in (up, down, peer):
            pl.semaphore_signal(free, inc=1, device_id=device, device_id_type=MESH)

    def project(d, product):
        rows = pl.ds(pl.multiple_of((z + d) % 4 * 256, 256), 256)

        @pl.loop(0, 4)
        def _(c):
            cols = pl.ds(pl.multiple_of(c * TILE, TILE), TILE)
            parts[d, :, cols] = product(rows, c, cols).astype(BF)

        scatter.put(d)

    def weight_grads(i, first, second):
        copies = [
            pltpu.make_async_copy(stage.at[c % 2], local_o.at[i, :, :, c], stage_s.at[i, c]) for c in range(4)
        ]
        for c in range(4):
            if c >= 2:
                copies[c - 2].wait()
            cols = slice(c * TILE, (c + 1) * TILE)
            stage[c % 2, :, :, :32] = first(cols).astype(BF).reshape(4, 4, 32, 512)
            stage[c % 2, :, :, 32:] = second(cols).astype(BF).reshape(4, 4, 16, 512)
            copies[c].start()
        copies[2].wait()
        copies[3].wait()
        collapses[i].start()

    def gain_row(which):
        return jnp.concatenate([gain[c, which : which + 1] for c in range(4)], axis=1)

    own_rows = pl.ds(pl.multiple_of(me * OWN, OWN), OWN)

    def stage_one(h2, g, ggu, hid, wg):
        needed = [load(ggu_i, ggu), load(h2_i, h2), load(hid_i, hid), load(g_i, g)]
        l_wg = load(wg_i, wg)
        meet(ring_friends() + [far] + xy_friends())
        wait(needed)

        def grads(u):
            weight_grads(
                u,
                lambda cols: t_mm(h2[:, cols], ggu[:, u * 512 : (u + 1) * 512]),
                lambda cols: t_mm(hid[:, u * 256 : (u + 1) * 256], g[:, cols]),
            )

        def product(rows, c, cols):
            return mm_t(ggu[rows], wg[c])

        grads(0)
        l_wg.wait()
        project(2, product)
        project(1, product)
        scatter.across()
        project(3, product)
        project(0, product)
        grads(1)
        scatter.beside(0)
        scatter.beside(1)
        grads(2)

    early = [load(mid_i, mid), load(gain_i, gain), load(x_i, x_own), load(g_i.at[own_rows], g_own)]
    pl.run_scoped(
        stage_one,
        pltpu.VMEM((GROUP, WIDTH), BF), pltpu.VMEM((GROUP, WIDTH), BF), pltpu.VMEM((GROUP, 2 * UNITS), BF),
        pltpu.VMEM((GROUP, UNITS), BF), pltpu.VMEM((4, TILE, 2 * UNITS), BF),
    )

    def stage_two(wo, att, qs, ks, raw, lse, ga, dk, dv, h1t, wq, att_t, start, cosine, sine):
        l_wo, l_att = load(wo_i, wo), load(att_i, att)
        l_heads = [
            load(q_i, qs), load(k_i, ks), load(raw_i, raw), load(lse_i, lse),
            load(start_i, start), load(cos_i, cosine), load(sin_i, sine),
        ]
        l_last = [load(h1t_i, h1t), load(wq_i, wq)]
        wait(early)
        acc[...] = jnp.zeros_like(acc)
        head_acc[...] = jnp.zeros_like(head_acc)
        dk[...] = jnp.zeros_like(dk)
        dv[...] = jnp.zeros_like(dv)
        totals[0] = jnp.zeros((8, WIDTH), F32)
        gain_two = gain_row(1)
        scatter.arrive()

        @pl.loop(0, OWN // 16)
        def _(i):
            rows = pl.ds(pl.multiple_of(i * 16, 16), 16)
            back, gained = norm_back(scatter.total(pl.multiple_of(i * 16, 16), 16), mid[rows], gain_two)
            acc[1] += gained
            back = back + g_own[rows].astype(F32)
            gm[rows] = back
            m[pl.ds(pl.multiple_of(me * OWN + i * 16, 16), 16)] = back.astype(BF)

        m_gather = Gather(rows_at(m), ms, mr)
        m_gather.start()
        release()
        collapses[0].first()
        l_att.wait()
        for h in range(2):
            att_t[h * HEAD : (h + 1) * HEAD] = att[h].T
        m_gather.forward()
        l_wo.wait()
        wait(l_heads)
        m_gather.share()
        m_gather.finish()

        @pl.loop(0, 4)
        def _(i):
            rows = pl.ds(pl.multiple_of(i * 256, 256), 256)
            back = mm_t(m[rows, :TILE], wo[0])
            for c in range(1, 4):
                back += mm_t(m[rows, c * TILE : (c + 1) * TILE], wo[c])
            for h in range(2):
                ga[h, rows] = back[:, h * HEAD : (h + 1) * HEAD].astype(BF)

        collapses[1].first()
        collapses[0].second()
        trades[0].start()
        for block in range(GROUP // QROWS):
            first, keys = block * QROWS, (block + 1) * QROWS
            rows = pl.ds(first, QROWS)
            allowed = allowed_keys(start[rows, :1], first, keys)

            @pl.loop(0, 2)
            def _(h):
                cols = pl.ds(pl.multiple_of(h * HEAD, HEAD), HEAD)
                score = mm_t(qs[h, rows], ks[:keys]) * (SCALE * LOG2)
                prob = jnp.exp2(jnp.where(allowed, score, -1e30) - lse[h, rows, :1])
                grad = ga[h, rows]
                delta = jnp.sum(grad.astype(F32) * att[h, rows].astype(F32), axis=1, keepdims=True)
                prob_grad = mm_t(grad, raw[:keys, 3 * HEAD :])
                score_grad = (prob * (prob_grad - delta)).astype(BF)
                dk[:keys] += t_mm(score_grad, qs[h, rows])
                dv[:keys] += t_mm(prob.astype(BF), grad)
                back = turn_back(mm(score_grad, ks[:keys]) * SCALE, cosine[rows], sine[rows])
                back, gained = norm_back(back, raw[rows, cols].astype(F32), q_gain[...])
                dqkv[rows, cols] = back.astype(BF)
                head_acc[0:1] += jnp.sum(gained, axis=0, keepdims=True)

            if block == 1:
                trades[0].finish()
                spreads[0].start(0)
            if block == 2:
                collapses[2].first()


        @pl.loop(0, 4)
        def _(i):
            rows = pl.ds(pl.multiple_of(i * 256, 256), 256)
            back = turn_back(dk[rows] * SCALE, cosine[rows], sine[rows])
            back, gained = norm_back(back, raw[rows, 2 * HEAD : 3 * HEAD].astype(F32), k_gain[...])
            dqkv[rows, 2 * HEAD : 3 * HEAD] = back.astype(BF)
            dqkv[rows, 3 * HEAD :] = dv[rows].astype(BF)
            head_acc[1:2] += jnp.sum(gained, axis=0, keepdims=True)

        wait(l_last)
        pl.semaphore_wait(free, 3)

        def product(rows, c, cols):
            return mm_t(dqkv[rows], wq[c])

        project(2, product)
        project(1, product)
        weight_grads(3, lambda cols: mm(h1t[cols], dqkv[...]), lambda cols: mm(att_t[...], m[:, cols]))
        spreads[0].pass_on(0)
        scatter.across()
        project(3, product)
        project(0, product)
        collapses[1].second()
        trades[1].start()
        spreads[0].wait(0)
        spreads[0].start(1)
        m_gather.drain()

    pl.run_scoped(
        stage_two,
        pltpu.VMEM((4, 256, TILE), BF), pltpu.VMEM((2, GROUP, HEAD), BF), pltpu.VMEM((2, GROUP, HEAD), BF),
        pltpu.VMEM((GROUP, HEAD), BF), pltpu.VMEM((GROUP, 512), BF), pltpu.VMEM((2, GROUP, HEAD), F32),
        pltpu.VMEM((2, GROUP, HEAD), BF), pltpu.VMEM((GROUP, HEAD), F32), pltpu.VMEM((GROUP, HEAD), F32),
        pltpu.VMEM((WIDTH, GROUP), BF), pltpu.VMEM((4, TILE, 512), BF), pltpu.VMEM((2 * HEAD, GROUP), BF),
        pltpu.VMEM((GROUP, HEAD), jnp.int32), pltpu.VMEM((GROUP, HEAD), F32), pltpu.VMEM((GROUP, HEAD), F32),
    )

    def stage_three(hid, wd):
        last = [load(hid_i, hid), load(wd_i, wd)]
        scatter.beside(0)
        scatter.beside(1)
        collapses[2].second()
        trades[2].start()
        trades[1].finish()
        spreads[1].start(0)
        gain_one = gain_row(0)
        scatter.arrive()

        @pl.loop(0, OWN // 16)
        def _(i):
            rows = pl.ds(pl.multiple_of(i * 16, 16), 16)
            back, gained = norm_back(
                scatter.total(pl.multiple_of(i * 16, 16), 16), x_own[rows].astype(F32), gain_one
            )
            acc[0] += gained
            tile_f[rows] = gm[rows] + back

        stream_trade.start()
        release()
        totals[0, 0:1] = jnp.sum(acc[0], axis=0, keepdims=True)
        totals[0, 1:2] = jnp.sum(acc[1], axis=0, keepdims=True)
        totals[0, 2:3, 0:HEAD] = head_acc[0:1]
        totals[0, 2:3, HEAD : 2 * HEAD] = head_acc[1:2]
        sent = []

        def tell(phase, devices, slots):
            for device, slot in zip(devices, slots):
                copy = remote(totals.at[phase], heard.at[slot], as_.at[slot], ar.at[slot], device)
                copy.start()
                sent.append(copy)

        def listen(phase, slots):
            total = totals[phase]
            for slot in slots:
                remote(heard.at[slot], heard.at[slot], as_.at[slot], ar.at[slot], peer).wait_recv()
                total += heard[slot]
            totals[phase + 1] = total

        tell(0, [peer], [0])
        trades[2].finish()
        spreads[2].start(0)
        collapses[3].first()
        spreads[1].pass_on(0)
        listen(0, [0])
        tell(1, [up, down, far], [1, 2, 3])
        wait(last)
        pl.semaphore_wait(free, 3)

        def product(rows, c, cols):
            return mm(hid[rows], wd[c])

        project(2, product)
        project(1, product)
        spreads[0].pass_on(1)
        spreads[1].wait(0)
        spreads[1].start(1)
        spreads[2].pass_on(0)
        scatter.across()
        project(3, product)
        project(0, product)
        listen(1, [1, 2, 3])
        tell(2, [along(0, o) for o in range(1, 4)], [4, 5, 6])
        collapses[3].second()
        trades[3].start()
        scatter.beside(0)
        scatter.beside(1)
        spreads[2].wait(0)
        spreads[2].start(1)
        trades[3].finish()
        spreads[3].start(0)
        scatter.arrive()

        @pl.loop(0, OWN // 16)
        def _(i):
            rows = pl.ds(pl.multiple_of(i * 16, 16), 16)
            tile_b[rows] = (mid[rows] + scatter.total(pl.multiple_of(i * 16, 16), 16)).astype(BF)

        result_trade.start()
        spreads[1].pass_on(1)
        spreads[3].pass_on(0)
        listen(2, [4, 5, 6])
        tell(3, [along(1, o) for o in range(1, 4)], [7, 8, 9])
        spreads[3].wait(0)
        spreads[3].start(1)
        spreads[2].pass_on(1)
        stream_trade.finish()
        result_trade.finish()
        listen(3, [7, 8, 9])
        sums_o[...] = totals[4]
        spreads[3].pass_on(1)
        for spread in spreads:
            spread.wait(1)
        scatter.drain()
        for thing in collapses + trades + spreads + [stream_trade, result_trade]:
            thing.drain()
        for copy in sent:
            copy.wait_send()

    pl.run_scoped(stage_three, pltpu.VMEM((GROUP, UNITS), BF), pltpu.VMEM((4, UNITS, TILE), BF))


def backward_call(*args):
    hbm = pl.BlockSpec(memory_space=pl.ANY)
    vmem = pl.BlockSpec(memory_space=pltpu.VMEM)
    dma = pltpu.SemaphoreType.DMA
    out = jax.ShapeDtypeStruct
    grads = out((CHUNKS, 4, 4, 4, 48, 512), BF)
    return pl.pallas_call(
        backward_kernel,
        out_shape=[out((TILE, TILE), BF), out((TILE, TILE), F32), grads, grads, out((8, WIDTH), F32)],
        in_specs=[hbm] * 20 + [vmem] * 2,
        out_specs=[hbm] * 4 + [vmem],
        scratch_shapes=[
            pltpu.VMEM((GROUP, WIDTH), BF), pltpu.VMEM((OWN, WIDTH), F32), pltpu.VMEM((GROUP, 512), BF),
            pltpu.VMEM((2, 4, 4, 48, 512), BF), pltpu.VMEM((OWN, WIDTH), F32), pltpu.VMEM((4, 8, TILE), F32),
            pltpu.VMEM((OWN, WIDTH), BF), pltpu.VMEM((OWN, WIDTH), BF), pltpu.VMEM((2, 16, WIDTH), F32),
            pltpu.VMEM((8, HEAD), F32), pltpu.VMEM((OWN, WIDTH), F32), pltpu.VMEM((OWN, WIDTH), BF),
            pltpu.VMEM((5, 8, WIDTH), F32), pltpu.VMEM((10, 8, WIDTH), F32),
        ]
        + GATHER_SEMS
        + scatter_scratch()
        + collapse_scratch()
        + [
            dma((3,)), dma((4,)), dma((3,)), dma((4,)), dma((10,)), dma((10,)), dma((24,)), dma((CHUNKS, 4)),
            pltpu.SemaphoreType.REGULAR,
        ],
        compiler_params=pltpu.CompilerParams(
            collective_id=2, has_side_effects=True, vmem_limit_bytes=VMEM_LIMIT
        ),
        cost_estimate=pl.CostEstimate(flops=25_000_000_000, bytes_accessed=100_000_000, transcendentals=2_000_000),
        name="backward",
    )(*args)


def place_big_kernel(grads, result, stream, totals, gate_up, down, result_o, stream_o, one, two, head):
    value = grads[0, :, 0, :32].reshape(TILE, 512).astype(F32)
    for g in range(2):
        gate_up[:, g, :] = value[:, g * 256 : (g + 1) * 256]
    down[...] = grads[0, :, 0, 32:].reshape(256, TILE).astype(F32)
    result_o[...] = result[...]
    stream_o[...] = stream[...]
    one[...] = totals[0:1]
    two[...] = totals[1:2]
    head[...] = totals[2:3, : 2 * HEAD]


def place_big(grads, result, stream, totals):
    rows = pl.BlockSpec((OWN, TILE), lambda c, u: (c, 0))

    def whole(*shape):
        return pl.BlockSpec(shape, lambda c, u: (0, 0))

    return pl.pallas_call(
        place_big_kernel,
        grid=(4, 3),
        in_specs=[
            pl.BlockSpec((1, DP, 1, 48, 512), lambda c, u: (u, 0, c, 0, 0)), rows, rows, whole(8, WIDTH),
        ],
        out_specs=[
            pl.BlockSpec((TILE, 2, 256), lambda c, u: (0, 0, c * 3 + u)),
            pl.BlockSpec((256, TILE), lambda c, u: (c * 3 + u, 0)),
            rows, rows, whole(1, WIDTH), whole(1, WIDTH), whole(1, 2 * HEAD),
        ],
        out_shape=[
            jax.ShapeDtypeStruct((TILE, 2, 4 * UNITS), F32),
            jax.ShapeDtypeStruct((4 * UNITS, TILE), F32),
            jax.ShapeDtypeStruct((TILE, TILE), BF),
            jax.ShapeDtypeStruct((TILE, TILE), F32),
            jax.ShapeDtypeStruct((1, WIDTH), F32),
            jax.ShapeDtypeStruct((1, WIDTH), F32),
            jax.ShapeDtypeStruct((1, 2 * HEAD), F32),
        ],
        compiler_params=pltpu.CompilerParams(vmem_limit_bytes=40 * 1024 * 1024),
        cost_estimate=pl.CostEstimate(flops=0, bytes_accessed=32_000_000, transcendentals=0),
        name="place_big",
    )(grads, result, stream, totals)


def place_small_kernel(grads, qkv, out):
    for c in range(4):
        qkv[:, c, :] = grads[0, :, c, :32].reshape(128, 512).astype(F32)
        out[c] = grads[0, :, c, 32:].reshape(64, TILE).astype(F32)


def place_small(grads):
    return pl.pallas_call(
        place_small_kernel,
        grid=(4,),
        in_specs=[pl.BlockSpec((1, 4, 4, 48, 512), lambda i: (3, i, 0, 0, 0))],
        out_specs=[
            pl.BlockSpec((128, 4, 512), lambda i: (i, 0, 0)),
            pl.BlockSpec((4, 64, TILE), lambda i: (0, i, 0)),
        ],
        out_shape=[
            jax.ShapeDtypeStruct((TILE, 4, 512), F32),
            jax.ShapeDtypeStruct((4, 256, TILE), F32),
        ],
        compiler_params=pltpu.CompilerParams(vmem_limit_bytes=40 * 1024 * 1024),
        cost_estimate=pl.CostEstimate(flops=0, bytes_accessed=9_000_000, transcendentals=0),
        name="place_small",
    )(grads)


def body(
    tokens, norm1_gain, w_qkv, q_gain, k_gain, w_out, norm2_gain, w_gate_up, w_down, out_grad,
    seq_lengths, seq_group, seq_start,
):
    (h2, g, wq, wo, wg, wd, h1t, raw, qs, ks, att, lse, middle, gain, x_own, start, cosine, sine) = forward_call(
        tokens, out_grad, norm1_gain[None], norm2_gain[None], q_gain[None], k_gain[None], jnp.asarray(FREQ),
        seq_lengths, seq_group, seq_start, w_qkv, w_gate_up,
        w_out.reshape(4, 4, 4, 16, TILE), w_down.reshape(4, 4, 4, 48, TILE),
    )
    wg = wg.reshape(4, TILE, 2 * UNITS)
    wd = wd.reshape(4, UNITS, TILE)
    ggu, hid = middle_call(h2, g, wg, wd)
    result, stream, grads, _, totals = backward_call(
        h2, ggu, hid, g, wg, wd, wo.reshape(4, 256, TILE), wq.reshape(4, TILE, 512), h1t, raw, qs, ks, att, lse,
        middle, gain, x_own, start, cosine, sine, q_gain[None], k_gain[None],
    )
    grads = grads.reshape(CHUNKS, DP, 4, 48, 512)
    g_gate_up, g_down, result, stream, one, two, head = place_big(grads, result, stream, totals)
    g_qkv, g_out = place_small(grads)
    return (
        result,
        stream,
        one.reshape(WIDTH),
        g_qkv,
        head[0, :HEAD],
        head[0, HEAD:],
        g_out.reshape(w_out.shape),
        two.reshape(WIDTH),
        g_gate_up,
        g_down,
    )


def solution(mesh):
    in_specs = (
        P(("dp", "row"), "col"),
        P("col"),
        P("col", "row", None),
        P(),
        P(),
        P("row", "col"),
        P("col"),
        P("col", None, "row"),
        P("row", "col"),
        P(("dp", "row"), "col"),
        P(),
        P(),
        P(),
    )
    out_specs = (
        P(("dp", "row"), "col"),
        P(("dp", "row"), "col"),
        P(),
        P("col", "row", None),
        P(),
        P(),
        P("row", "col"),
        P(),
        P("col", None, "row"),
        P("row", "col"),
    )
    return jax.shard_map(body, mesh=mesh, in_specs=in_specs, out_specs=out_specs, check_vma=False)
```

time: 434 us -> 338 us (0.78)
  Pallas kernels: 376 us -> 327 us
  local copies, waits for them, and re-layouts: 49.9 us -> 9.67 us
  other arithmetic: 6.89 us -> 0 us
    pallas_call x1, Pallas kernels: 220 us -> 191 us  [backward_call(): pl.pallas_call(backward_kernel, out_shape=[out((TILE, TILE), BF), out((TI...]
    pallas_call x1, Pallas kernels: 32.6 us -> 17.6 us  [middle_call(): pl.pallas_call(middle_kernel, grid=(3,), out_shape=[jax.ShapeDtypeStruct(...]
    unnamed x13 -> x10, local copies, waits for them, and re-layouts: 23.4 us -> 9.15 us
    transpose x6 -> x0, local copies, waits for them, and re-layouts: 13.5 us -> none  [the longest x4 11.8 us: order(): return block.transpose(2, 0, 3, 1, 4).reshape(2, -1, 2 * UNITS)]
    reshape x3 -> x0, local copies, waits for them, and re-layouts: 9.17 us -> none  [the longest x2 8.76 us: order(): return block.transpose(2, 0, 3, 1, 4).reshape(2, -1, 2 * UNITS)]
    pallas_call x3, Pallas kernels: 123 us -> 119 us  [the longest x1 106 us: forward_call(): pl.pallas_call(forward_kernel, out_shape=[out(wide), out(wide), out((4, 4...]
where the time goes in v3:
time: 338 us
  Pallas kernels  327 us (97%)
  local copies, waits for them, and re-layouts  9.67 us (3%)
    pallas_call x1, Pallas kernels, backward_call(): pl.pallas_call(backward_kernel, out_shape=[out((TILE, TILE), BF), out((TI...  191 us
    pallas_call x1, Pallas kernels, forward_call(): pl.pallas_call(forward_kernel, out_shape=[out(wide), out(wide), out((4, 4...  106 us
    pallas_call x1, Pallas kernels, middle_call(): pl.pallas_call(middle_kernel, grid=(3,), out_shape=[jax.ShapeDtypeStruct(...  17.6 us
    pallas_call x1, Pallas kernels, place_big(): pl.pallas_call(place_big_kernel, grid=(4, 3), in_specs=[pl.BlockSpec((1,...  9.87 us
    unnamed x10, local copies, waits for them, and re-layouts  9.15 us

profile of v3, /device:TPU:0, one launch (start us, length us, event | category | flops | bytes accessed | tf_op | source)
XLA Modules:
  0.0 337.6 jit_solution(15577033923571188373)
XLA Ops:
  0.6 105.9 %forward.1 = (bf16[1024,2048]{1,0:T(8,128)(2,1)}, bf16[1024,2048]{1,0:T(8,128)(2,1)}, bf16[4,4,4,32,512]{4,3,2,1,0:T(8,128)(2,1)}, bf16[4,4,4,16,512]{4,3,2,1,0:...) custom-call(bf16[512,512]{1,0:T(8,128)(2,1)} %tok.1, ...), custom_call_target="tpu_custom_call" | custom-call | flops 4000000000 | bytes 60000000 | tf_op jit(solution)/shard_map/forward/pallas_call | solution.py:674
  106.5 17.6 %feed_forward.1 = (bf16[1024,1536]{1,0:T(8,128)(2,1)}, bf16[1024,768]{1,0:T(8,128)(2,1)}) custom-call(bf16[1024,2048]{1,0:T(8,128)(2,1)} %get-tuple-element.43.h2.h2_i, bf16[1024,2048]{1,0:T(8,128)(2,1)} %get-tuple-element.44.g.g_i, bf16[4,512,1536]{2,1,0:T(8,128)(2,1)} %bitcast.31, bf16[4,768,512]{2,1,0:T(8,128)(2,1)} %bitcast.33), custom_call_target="tpu_custom_call" | custom-call | flops 9600000000 | bytes 22000000 | tf_op jit(solution)/shard_map/feed_forward/pallas_call | solution.py:725
  124.1 190.8 %backward.1 = (bf16[512,512]{1,0:T(8,128)(2,1)}, f32[512,512]{1,0:T(8,128)}, bf16[4,4,4,4,48,512]{5,4,3,2,1,0:T(8,128)(2,1)}, bf16[4,4,4,4,48,512]{5,4,3,2,1,0:T(8,128)(2,1)}, f32[8,2048]{1,0:T(8,128)}) custom-call(bf16[1024,2048]{1,0:T(8,128)(2,1)} %get-tuple-element.43.h2.h2_i, bf16[1024,1536]{1,0:T(8,128)(2,1)} %get-tuple-element.47.ggu_i, ...), custom_call_target="tpu_custom_call" | custom-call | flops 24999999488 | bytes 100000000 | tf_op jit(solution)/shard_map/backward/pallas_call | solution.py:1223
  314.9 0.0 copy-start
  314.9 4.6 %copy-done = bf16[4,4,4,4,48,512]{5,4,3,2,1,0:T(8,128)(2,1)S(1)} copy-done((bf16[4,4,4,4,48,512]{5,4,3,2,1,0:T(8,128)(2,1)S(1)}, bf16[4,4,4,4,48,512]{5,4,3,2,1,0:T(8,128)(2,1)}, u32[]{:S(2)}) %copy-start) | copy-done | bytes 12582936
  319.4 0.0 copy-start.2
  319.4 0.0 copy-start.3
  319.4 0.0 copy-start.4
  319.4 3.2 place_small.1
  322.7 0.0 copy-done.2
  322.7 0.0 copy-done.3
  322.7 0.0 copy-done.4
  322.7 0.0 copy-start.1
  322.7 4.6 %copy-done.1 = bf16[4,4,4,4,48,512]{5,4,3,2,1,0:T(8,128)(2,1)S(1)} copy-done((bf16[4,4,4,4,48,512]{5,4,3,2,1,0:T(8,128)(2,1)S(1)}, bf16[4,4,4,4,48,512]{5,4,3,2,1,0:T(8,128)(2,1)}, u32[]{:S(2)}) %copy-start.1) | copy-done | bytes 12582936
  327.3 9.9 %place_big.1 = (f32[512,2,3072]{2,1,0:T(2,128)}, f32[3072,512]{1,0:T(8,128)}, bf16[512,512]{1,0:T(8,128)(2,1)}, f32[512,512]{1,0:T(8,128)}, f32[1,2048]{1,0:T(1,...) custom-call(bf16[4,16,4,48,512]{4,3,2,1,0:T(8,128)(2,1)S(1)} %bitcast.19, bf16[512,512]{1,0:T(8,128)(2,1)S(1)} %copy-done.3, ...), custom_call_target="tpu_custom_call" | custom-call | bytes 32000000 | tf_op jit(solution)/shard_map/place_big/pallas_call | solution.py:1268
  337.1 0.5 slice_bitcast_fusion
Async XLA Ops:
  314.9 4.6 %copy-start = (bf16[4,4,4,4,48,512]{5,4,3,2,1,0:T(8,128)(2,1)S(1)}, bf16[4,4,4,4,48,512]{5,4,3,2,1,0:T(8,128)(2,1)}, u32[]{:S(2)}) copy-start(bf16[4,4,4,4,48,512]{5,4,3,2,1,0:T(8,128)(2,1)} %get-tuple-element.63) | copy-start | bytes 37748740
  319.4 3.2 copy-start.2
  319.4 3.2 copy-start.3
  319.4 3.2 copy-start.4
  322.7 4.6 %copy-start.1 = (bf16[4,4,4,4,48,512]{5,4,3,2,1,0:T(8,128)(2,1)S(1)}, bf16[4,4,4,4,48,512]{5,4,3,2,1,0:T(8,128)(2,1)}, u32[]{:S(2)}) copy-start(bf16[4,4,4,4,48,512]{5,4,3,2,1,0:T(8,128)(2,1)} %get-tuple-element.63) | copy-start | bytes 37748740

commit v4 on v3

--- a/solution.py
+++ b/solution.py
@@ -167,8 +167,8 @@
             self.arrivals[2 + half].wait_recv()
             self.from_far[half].start()
 
-    def finish(self):
-        for slot in range(4, 9):
+    def finish(self, slots=range(4, 9)):
+        for slot in slots:
             self.arrivals[slot].wait_recv()
 
     def drain(self):
@@ -347,12 +347,12 @@
 
 def forward_kernel(
     tok, og, norm1, norm2, q_gain, k_gain, freq, lengths, groups, starts, w_qkv, w_gu, w_out, w_down,
-    h2_o, g_o, wq_o, wo_o, wg_o, wd_o, h1t_o, raw_o, q_o, k_o, att_o, lse_o, mid_o, gain_o, x_o, start_o, cos_o, sin_o,
-    x, h1, h1t, h2, g, wq, wo, raw, qs, ks, att, lse, mid, gain, gains, start, cosine, sine,
+    h2_o, g_o, wq_o, wo_o, wg_o, wd_o, h1t_o, raw_o, q_o, k_o, att_o, lse_o, mid_o, gain_o, x_o, start_o, cos_o, sin_o, ggu_o, hid_o,
+    x, h1, h1t, h2, g, wq, wo, wg, wd, raw, qs, ks, att, lse, mid, gain, gains, start, cosine, sine,
     q_raw, q_cut, q_raw_part, q_part, g_raw, g_cut, g_raw_part, g_part,
     xs, xr, gs, gr, hs, hr,
     parts, theirs, sums, near, full, rs_s, rs_r,
-    zs, zr, ps, pr, ns, nr, loc_s, out_s, raw_s,
+    zs, zr, ps, pr, ns, nr, loc_s, out_s, raw_s, row_s,
     y0s, y0r, y1s, y1r, y2s, y2r, y3s, y3r,
 ):
     p, row, col, z, k = place()
@@ -381,27 +381,32 @@
         copy.start()
     gains[0:1] = norm1[...]
     gains[1:2] = norm2[...]
+    meet(ring_friends() + xy_friends())
+
     raws[0].wait()
     for kk in range(2):
         q_part[kk] = jnp.where(lo == 0, q_raw_part[:, 2 + kk, :], q_raw_part[:, kk, :])
-    meet(ring_friends() + xy_friends())
 
     gain[col] = gains[...]
     gain_copies = [
         remote(gains, gain.at[col], ns.at[i], nr.at[col], device)
         for i, device in enumerate([peer, on_ring(other, k), on_ring(other, 1 - k)])
     ]
-    weights = [wq, wo, wg_o, wd_o]
+    weights = [wq, wo, wg, wd]
     sources = [q_part, w_out, g_part, w_down]
     blocks = [q_cut, w_out, g_cut, w_down]
 
+    def cell(weight, c, xx, yy, cols=slice(None)):
+        between = (slice(None),) * (len(weight.shape) - 5)
+        return weight.at[(c, *between, xx, yy, slice(None), cols)]
+
     def crossing(a, kk):
         target = 2 * (1 - lo) + kk
-        src = sources[a].at[kk] if a % 2 == 0 else w_out.at[target, px, py] if a == 1 else w_down.at[target, px, py]
-        return remote(src, weights[a].at[col, px, py], zs.at[a, kk], zr.at[a, k], on_ring(other, kk))
+        src = sources[a].at[kk] if a % 2 == 0 else cell(sources[a], target, px, py)
+        return remote(src, cell(weights[a], col, px, py), zs.at[a, kk], zr.at[a, k], on_ring(other, kk))
 
     def crossed(a, kk):
-        dst = weights[a].at[2 * (1 - lo) + kk, px, py]
+        dst = cell(weights[a], 2 * (1 - lo) + kk, px, py)
         return remote(dst, dst, zs.at[a, kk], zr.at[a, kk], peer)
 
     def beside(a):
@@ -420,7 +425,7 @@
             xs_ = slice(None) if xx is None else xx
             ys_ = slice(None) if yy is None else yy
             cols = slice(None) if part is None else pl.ds(part * half_lanes, half_lanes)
-            return weight.at[2 * (1 - lo) + half, xs_, ys_, :, cols]
+            return cell(weight, 2 * (1 - lo) + half, xs_, ys_, cols)
 
         return at
 
@@ -487,27 +492,9 @@
     for a in (0, 1):
         spreads[a].wait(0)
         spreads[a].start(1)
-    x_gather.forward()
-
-    @pl.loop(0, 16)
-    def _(i):
-        rows = pl.ds(pl.multiple_of(i * 32, 32), 32)
-        for u in range(3):
-            for half in range(2):
-                into = slice(u * 512 + half * 256, u * 512 + half * 256 + 256)
-                for kk in range(2):
-                    cols = slice(kk * UNITS + u * 256, kk * UNITS + u * 256 + 256)
-                    g_cut[kk, i // 4, i % 4, :, into] = g_raw[rows, half, cols]
-
     for a in (0, 1):
         spreads[a].pass_on(1)
-    x_gather.share()
-    for a in (2, 3):
-        for kk in range(2):
-            crossing(a, kk).start()
-    for a in (2, 3):
-        beside(a)[0].start()
-        beside(a)[1].start()
+    x_gather.forward()
     for c in range(4):
 
         @pl.when(c != col)
@@ -515,49 +502,54 @@
             remote(gain.at[c], gain.at[c], ns.at[0], nr.at[c], peer).wait_recv()
 
     keep_x.wait()
-    x_gather.finish()
-    g_gather = Gather(tile_at(g), gs, gr, og)
-    g_gather.start()
+    x_gather.finish([4, 5, 6])
 
     def gain_row(which):
         return jnp.concatenate([gain[c, which : which + 1] for c in range(4)], axis=1)
 
     gain_one = gain_row(0)
 
-    @pl.loop(0, GROUP // 64)
-    def _(i):
-        rows = pl.ds(pl.multiple_of(i * 64, 64), 64)
-        value = x[rows].astype(F32)
-        h1[rows] = (value * head_norm(value) * gain_one).astype(BF)
-
-    for a in (2, 3):
-        for kk in range(2):
-            crossed(a, kk).wait_recv()
-        spreads[a].start(0)
+    def norm_one(half):
+        @pl.loop(0, TILE // 64)
+        def _(i):
+            rows = pl.ds(pl.multiple_of(half * TILE + i * 64, 64), 64)
+            value = x[rows].astype(F32)
+            h1[rows] = (value * head_norm(value) * gain_one).astype(BF)
+
+    def heads(half):
+        @pl.loop(0, TILE // 256)
+        def _(i):
+            rows = pl.ds(pl.multiple_of(half * TILE + i * 256, 256), 256)
+            mixed = mm(h1[rows], wq[...].reshape(WIDTH, 4 * HEAD)).astype(BF)
+            raw[rows] = mixed
+            cos_rows, sin_rows = cosine[rows], sine[rows]
+            for piece in range(3):
+                value = mixed[:, piece * HEAD : (piece + 1) * HEAD].astype(F32)
+                by = q_gain[...] if piece < 2 else k_gain[...]
+                turned = turn(value * head_norm(value) * by, cos_rows, sin_rows).astype(BF)
+                if piece < 2:
+                    qs[piece, rows] = turned
+                else:
+                    ks[rows] = turned
+
+    norm_one(row)
     for a in range(2):
         keep, _, take = beside(a)
         keep.wait()
         take.wait_recv()
         spreads[a].wait(1)
-
-    @pl.loop(0, GROUP // 256)
-    def _(i):
-        rows = pl.ds(pl.multiple_of(i * 256, 256), 256)
-        mixed = mm(h1[rows], wq[...].reshape(WIDTH, 4 * HEAD)).astype(BF)
-        raw[rows] = mixed
-        cos_rows, sin_rows = cosine[rows], sine[rows]
-        for piece in range(3):
-            value = mixed[:, piece * HEAD : (piece + 1) * HEAD].astype(F32)
-            by = q_gain[...] if piece < 2 else k_gain[...]
-            turned = turn(value * head_norm(value) * by, cos_rows, sin_rows).astype(BF)
-            if piece < 2:
-                qs[piece, rows] = turned
-            else:
-                ks[rows] = turned
-
+    heads(row)
+    x_gather.share()
     for a in (2, 3):
-        spreads[a].pass_on(0)
-    g_gather.forward()
+        for kk in range(2):
+            crossing(a, kk).start()
+    beside(3)[0].start()
+    beside(3)[1].start()
+    x_gather.finish([7, 8])
+    norm_one(1 - row)
+    heads(1 - row)
+    g_gather = Gather(tile_at(g), gs, gr, og)
+    g_gather.start()
     saves = [
         pltpu.make_async_copy(src, dst, out_s.at[i])
         for i, (src, dst) in enumerate(
@@ -587,12 +579,12 @@
             att[h, rows] = out.astype(BF)
             lse[h, rows] = jnp.broadcast_to(peak + jnp.log2(total), (QROWS, HEAD))
 
-    for a in (2, 3):
-        spreads[a].wait(0)
-        spreads[a].start(1)
     saves[7].start()
     saves[8].start()
-    g_gather.share()
+    for a in (2, 3):
+        for kk in range(2):
+            crossed(a, kk).wait_recv()
+        spreads[a].start(0)
 
     scatter = Scatter(parts, theirs, sums, near, full, rs_s, rs_r)
 
@@ -608,8 +600,8 @@
     scatter.across()
     project(3)
     project(0)
-    scatter.beside(0)
-    scatter.beside(1)
+    for a in (2, 3):
+        spreads[a].pass_on(0)
 
     @pl.loop(0, 8)
     def _(i):
@@ -617,11 +609,29 @@
         h1t[cols] = h1[:, cols].T
 
     saves[12].start()
+    scatter.beside(0)
+    scatter.beside(1)
+    g_gather.forward()
+    for a in (2, 3):
+        spreads[a].wait(0)
+        spreads[a].start(1)
+
+
+    @pl.loop(0, 16)
+    def _(i):
+        rows = pl.ds(pl.multiple_of(i * 32, 32), 32)
+        for u in range(3):
+            for half in range(2):
+                into = slice(u * 512 + half * 256, u * 512 + half * 256 + 256)
+                for kk in range(2):
+                    cols = slice(kk * UNITS + u * 256, kk * UNITS + u * 256 + 256)
+                    g_cut[kk, i // 4, i % 4, :, into] = g_raw[rows, half, cols]
+
+    beside(2)[0].start()
+    beside(2)[1].start()
     for a in (2, 3):
         spreads[a].pass_on(1)
-    g_gather.finish()
-    keep_g.wait()
-    saves[9].start()
+    g_gather.share()
     scatter.arrive()
     gain_two = gain_row(1)
 
@@ -636,15 +646,60 @@
     saves[10].start()
     h2_gather = Gather(rows_at(h2), hs, hr)
     h2_gather.start()
-    h2_gather.forward()
+    x_gather.drain()
+    saves[5].wait()
     for a in (2, 3):
         keep, _, take = beside(a)
         keep.wait()
         take.wait_recv()
         spreads[a].wait(1)
+    weight_saves = [pltpu.make_async_copy(weights[a], (wg_o, wd_o)[a - 2], loc_s.at[a + 4]) for a in (2, 3)]
+    for copy in weight_saves:
+        copy.start()
+    row_saves = []
+
+    def feed(d):
+        rows = pl.ds(pl.multiple_of((z + d) % 4 * 256, 256), 256)
+
+        @pl.loop(0, 3)
+        def _(u):
+            wide = pl.ds(pl.multiple_of(u * 512, 512), 512)
+            gate_cols = pl.ds(pl.multiple_of(u * 512, 256), 256)
+            up_cols = pl.ds(pl.multiple_of(u * 512 + 256, 256), 256)
+            pair = mm(h2[rows], wg[:, :, :, :, wide].reshape(WIDTH, 512))
+            back = mm_t(g[rows, :TILE], wd[0, u].reshape(256, TILE))
+            for c in range(1, 4):
+                back += mm_t(g[rows, c * TILE : (c + 1) * TILE], wd[c, u].reshape(256, TILE))
+            gate, up = pair[:, :256], pair[:, 256:]
+            sig = 1.0 / (1.0 + jnp.exp(-gate))
+            silu = gate * sig
+            h1[rows, pl.ds(pl.multiple_of(u * 256, 256), 256)] = (silu * up).astype(BF)
+            x[rows, gate_cols] = (back * up * sig * (1.0 + gate * (1.0 - sig))).astype(BF)
+            x[rows, up_cols] = (back * silu).astype(BF)
+
+        for i, (src, dst) in enumerate(
+            [
+                (h2.at[rows], h2_o.at[rows]),
+                (x.at[rows, pl.ds(0, 2 * UNITS)], ggu_o.at[rows]),
+                (h1.at[rows, pl.ds(0, UNITS)], hid_o.at[rows]),
+            ]
+        ):
+            copy = pltpu.make_async_copy(src, dst, row_s.at[d, i])
+            copy.start()
+            row_saves.append(copy)
+
+    g_gather.finish()
+    keep_g.wait()
+    saves[9].start()
+    h2_gather.finish([4])
+    feed(0)
+    h2_gather.forward()
+    h2_gather.finish([5, 6])
+    feed(1)
     h2_gather.share()
-    h2_gather.finish()
-    saves[11].start()
+    feed(3)
+    h2_gather.finish([7, 8])
+    feed(2)
     for copy in gain_copies:
         copy.wait_send()
     for a in range(4):
@@ -653,11 +708,13 @@
             crossing(a, kk).wait_send()
     for spread in spreads:
         spread.drain()
-    x_gather.drain()
     g_gather.drain()
     h2_gather.drain()
     scatter.drain()
-    for copy in saves:
+    for i, copy in enumerate(saves):
+        if i not in (5, 11):
+            copy.wait()
+    for copy in weight_saves + row_saves:
         copy.wait()
 
 
@@ -675,15 +732,17 @@
         forward_kernel,
         out_shape=[
             out(wide), out(wide), out((4, 4, 4, 32, 512)), out((4, 4, 4, 16, TILE)), out((4, 4, 4, 32, 2 * UNITS)),
-            out((4, 4, 4, 48, TILE)), out((WIDTH, GROUP)), out((GROUP, 512)), out((2, GROUP, HEAD)), out((GROUP, HEAD)),
+            out((4, 3, 4, 4, 16, TILE)), out((WIDTH, GROUP)), out((GROUP, 512)), out((2, GROUP, HEAD)), out((GROUP, HEAD)),
             out((2, GROUP, HEAD)), out((2, GROUP, HEAD), F32), out((OWN, WIDTH), F32), out((4, 8, TILE), F32),
             out((OWN, WIDTH)), out((GROUP, HEAD), jnp.int32), out((GROUP, HEAD), F32), out((GROUP, HEAD), F32),
+            out((GROUP, 2 * UNITS)), out((GROUP, UNITS)),
         ],
         in_specs=[vmem] * 7 + [smem] * 3 + [hbm] * 4,
-        out_specs=[hbm] * 18,
+        out_specs=[hbm] * 20,
         scratch_shapes=[
             pltpu.VMEM(wide, BF), pltpu.VMEM(wide, BF), pltpu.VMEM((WIDTH, GROUP), BF), pltpu.VMEM(wide, BF),
             pltpu.VMEM(wide, BF), pltpu.VMEM((4, 4, 4, 32, 512), BF), pltpu.VMEM((4, 4, 4, 16, TILE), BF),
+            pltpu.VMEM((4, 4, 4, 32, 2 * UNITS), BF), pltpu.VMEM((4, 3, 4, 4, 16, TILE), BF),
             pltpu.VMEM((GROUP, 512), BF), pltpu.VMEM((2, GROUP, HEAD), BF), pltpu.VMEM((GROUP, HEAD), BF),
             pltpu.VMEM((2, GROUP, HEAD), BF), pltpu.VMEM((2, GROUP, HEAD), F32), pltpu.VMEM((OWN, WIDTH), F32),
             pltpu.VMEM((4, 8, TILE), F32), pltpu.VMEM((8, TILE), F32), pltpu.VMEM((GROUP, HEAD), jnp.int32),
@@ -694,135 +753,120 @@
         ]
         + GATHER_SEMS * 3
         + scatter_scratch()
-        + [dma((4, 2)), dma((4, 2)), dma((4,)), dma((4,)), dma((3,)), dma((4,)), dma((6,)), dma((16,)), dma((4,))]
+        + [dma((4, 2)), dma((4, 2)), dma((4,)), dma((4,)), dma((3,)), dma((4,)), dma((8,)), dma((16,)), dma((4,)), dma((4, 3))]
         + SPREAD_SEMS * 4,
         compiler_params=pltpu.CompilerParams(
             collective_id=1, has_side_effects=True, vmem_limit_bytes=VMEM_LIMIT
         ),
-        cost_estimate=pl.CostEstimate(flops=4_000_000_000, bytes_accessed=60_000_000, transcendentals=2_000_000),
+        cost_estimate=pl.CostEstimate(flops=14_000_000_000, bytes_accessed=60_000_000, transcendentals=2_000_000),
         name="forward",
     )(*args)
 
 
-def middle_kernel(h2, g, wg, wd, ggu, hid):
-    @pl.loop(0, GROUP // 256)
-    def _(i):
-        rows = pl.ds(pl.multiple_of(i * 256, 256), 256)
-        pair = mm(h2[rows], wg[...].reshape(WIDTH, 512))
-        back = mm_t(g[rows, :TILE], wd[0])
-        for c in range(1, 4):
-            back += mm_t(g[rows, c * TILE : (c + 1) * TILE], wd[c])
-        gate, up = pair[:, :256], pair[:, 256:]
-        sig = 1.0 / (1.0 + jnp.exp(-gate))
-        silu = gate * sig
-        hid[rows] = (silu * up).astype(BF)
-        ggu[rows, :256] = (back * up * sig * (1.0 + gate * (1.0 - sig))).astype(BF)
-        ggu[rows, 256:] = (back * silu).astype(BF)
-
-
-def middle_call(h2, g, wg, wd):
-    wide = pl.BlockSpec((GROUP, WIDTH), lambda u: (0, 0), pipeline_mode=pl.Buffered(1))
-    return pl.pallas_call(
-        middle_kernel,
-        grid=(3,),
-        out_shape=[
-            jax.ShapeDtypeStruct((GROUP, 2 * UNITS), BF),
-            jax.ShapeDtypeStruct((GROUP, UNITS), BF),
-        ],
-        in_specs=[
-            wide,
-            wide,
-            pl.BlockSpec((4, TILE, 512), lambda u: (0, 0, u)),
-            pl.BlockSpec((4, 256, TILE), lambda u: (0, u, 0)),
-        ],
-        out_specs=[
-            pl.BlockSpec((GROUP, 512), lambda u: (0, u)),
-            pl.BlockSpec((GROUP, 256), lambda u: (0, u)),
-        ],
-        compiler_params=pltpu.CompilerParams(vmem_limit_bytes=VMEM_LIMIT),
-        cost_estimate=pl.CostEstimate(flops=9_600_000_000, bytes_accessed=22_000_000, transcendentals=800_000),
-        name="feed_forward",
-    )(h2, g, wg, wd)
-
-
 class Collapse:
-    def __init__(self, which, src, got, sums, got2, done, send, recv, own):
-        px, py = dp_place()
-        here = (px, py)
-        self.which = which
-        self.got, self.sums, self.got2, self.done, self.here = got, sums, got2, done, here
-
-        def cut(axis, index, half):
-            pair = pl.ds(2 * half, 2)
-            return src.at[which, index, :, pair] if axis == 0 else src.at[which, :, index, pair]
-
-        self.keep, self.copies = [], {}
+    def __init__(self, which, data, near, full, done, send, recv):
+        here = dp_place()
+        self.which, self.data, self.near, self.full, self.done, self.here = which, data, near, full, done, here
+        self.copies = {}
         for half in range(2):
-            axis = half
-            self.keep.append(pltpu.make_async_copy(cut(axis, here[axis], half), sums.at[which, half], own.at[which, half]))
-            for o in range(1, 4):
-                there = (here[axis] + o) % 4
-                self.copies[half, 0, o] = remote(
-                    cut(axis, there, half), got.at[which, half, o - 1],
-                    send.at[which, half, 0, o - 1], recv.at[which, half, 0, o - 1], along(axis, o),
-                )
-                there = (here[1 - axis] + o) % 4
-                self.copies[half, 1, o] = remote(
-                    sums.at[which, half, there], got2.at[which, half, o - 1],
-                    send.at[which, half, 1, o - 1], recv.at[which, half, 1, o - 1], along(1 - axis, o),
-                )
-
-    def start(self):
+            for phase in range(2):
+                axis = half ^ phase
+
+                def copy(slot, src, dst, o):
+                    index = (which, half, phase, slot)
+                    return remote(src, dst, send.at[index], recv.at[index], along(axis, o))
+
+                self.copies[half, phase] = [
+                    copy(0, self.block(half, phase, 2, 0), near[phase].at[half, 0], 1),
+                    copy(1, self.block(half, phase, 2, 1), near[phase].at[half, 1], 3),
+                    copy(2, self.block(half, phase, 1), full[phase].at[half, 0], 1),
+                    copy(3, self.block(half, phase, 3), full[phase].at[half, 1], 3),
+                ]
+
+    def at(self, half, phase, o):
+        there = (self.here[half ^ phase] + o) % 4
+        if phase == 0:
+            return (there, slice(None)) if half == 0 else (slice(None), there)
+        return (self.here[0], there) if half == 0 else (there, self.here[1])
+
+    def block(self, half, phase, o, part=None):
+        which = pl.ds(2 * half, 2) if part is None else 2 * half + part
+        return self.data.at[(*self.at(half, phase, o), which)]
+
+    def cell(self, half, phase, o, a, c):
+        x, y = self.at(half, phase, o)
+        x, y = (a if isinstance(x, slice) else x), (a if isinstance(y, slice) else y)
+        return (x, y, 2 * half + c)
+
+    def start(self, phase=0):
         for half in range(2):
-            for o in range(1, 4):
-                self.copies[half, 0, o].start()
-            self.keep[half].start()
+            for slot in range(2):
+                self.copies[half, phase][slot].start()
+
+    def mid(self, phase=0):
+        for half in range(2):
+            for slot in range(2):
+                self.copies[half, phase][slot].wait_recv()
+
+                def add(a):
+                    index = self.cell(half, phase, (1, 3)[slot], a, slot)
+                    here = (half, slot, a) if phase == 0 else (half, slot)
+                    self.data[index] = (
+                        self.data[index].astype(F32) + self.near[phase][here].astype(F32)
+                    ).astype(BF)
+
+                if phase == 0:
+                    pl.loop(0, 4)(add)
+                else:
+                    add(0)
+                self.copies[half, phase][2 + slot].start()
 
     def first(self):
         for half in range(2):
-            self.keep[half].wait()
-            for o in range(1, 4):
-                self.copies[half, 0, o].wait_recv()
-
-            @pl.loop(0, 8)
-            def _(i):
-                a, c = i // 2, i % 2
-                total = self.sums[self.which, half, a, c].astype(F32)
-                for o in range(3):
-                    total += self.got[self.which, half, o, a, c].astype(F32)
-                self.sums[self.which, half, a, c] = total.astype(BF)
-
-            for o in range(1, 4):
-                self.copies[half, 1, o].start()
+            for slot in range(2):
+                self.copies[half, 0][2 + slot].wait_recv()
+
+            @pl.loop(0, 4)
+            def _(a):
+                for c in range(2):
+                    index = self.cell(half, 0, 0, a, c)
+                    total = self.data[index].astype(F32)
+                    for slot in range(2):
+                        total += self.full[0][half, slot, a, c].astype(F32)
+                    self.data[index] = total.astype(BF)
+
+        self.start(1)
 
     def second(self):
         for half in range(2):
-            for o in range(1, 4):
-                self.copies[half, 1, o].wait_recv()
+            for slot in range(2):
+                self.copies[half, 1][2 + slot].wait_recv()
             for c in range(2):
-                total = self.sums[self.which, half, self.here[1 - half], c].astype(F32)
-                for o in range(3):
-                    total += self.got2[self.which, half, o, c].astype(F32)
+                total = self.data[self.cell(half, 1, 0, 0, c)].astype(F32)
+                for slot in range(2):
+                    total += self.full[1][half, slot, c].astype(F32)
                 self.done[self.which, 2 * half + c] = total.astype(BF)
 
     def drain(self):
-        for copy in self.copies.values():
-            copy.wait_send()
-
-
-CHUNKS = 4
+        for copies in self.copies.values():
+            for copy in copies:
+                copy.wait_send()
+
+
+CHUNKS, BUFFERS = 4, 3
 
 
 def collapse_scratch():
     dma = pltpu.SemaphoreType.DMA
-    return [
-        pltpu.VMEM((CHUNKS, 2, 3, 4, 2, 48, 512), BF),
-        pltpu.VMEM((CHUNKS, 2, 4, 2, 48, 512), BF),
-        pltpu.VMEM((CHUNKS, 2, 3, 2, 48, 512), BF),
-        pltpu.VMEM((CHUNKS, 4, 48, 512), BF),
-        dma((CHUNKS, 2, 2, 3)), dma((CHUNKS, 2, 2, 3)), dma((CHUNKS, 2)),
-        dma((CHUNKS, 3)), dma((CHUNKS, 4)), dma((CHUNKS, 2, 2, 4)), dma((CHUNKS, 2, 2, 4)),
-    ]
+    return (
+        [pltpu.VMEM((4, 4, 4, 48, 512), BF)] * BUFFERS
+        + [pltpu.VMEM((2, 2, 4, 48, 512), BF)] * BUFFERS
+        + [pltpu.VMEM((2, 2, 48, 512), BF)] * BUFFERS
+        + [pltpu.VMEM((2, 2, 4, 2, 48, 512), BF)] * BUFFERS
+        + [pltpu.VMEM((2, 2, 2, 48, 512), BF)] * BUFFERS
+        + [pltpu.VMEM((CHUNKS, 4, 48, 512), BF), dma((CHUNKS, 2, 2, 4)), dma((CHUNKS, 2, 2, 4))]
+        + [dma((CHUNKS, 3)), dma((CHUNKS, 4)), dma((CHUNKS, 2, 2, 4)), dma((CHUNKS, 2, 2, 4))]
+    )
 
 
 class Trade:
@@ -870,12 +914,13 @@
 def backward_kernel(
     h2_i, ggu_i, hid_i, g_i, wg_i, wd_i, wo_i, wq_i, h1t_i, raw_i, q_i, k_i, att_i, lse_i, mid_i, gain_i, x_i,
     start_i, cos_i, sin_i, q_gain, k_gain,
-    result_o, stream_o, grads_o, local_o, sums_o,
-    m, gm, dqkv, stage, mid, gain, x_own, g_own, acc, head_acc, tile_f, tile_b, totals, heard,
+    result_o, stream_o, grads_o, sums_o,
+    m, gm, dqkv, mid, gain, x_own, g_own, acc, head_acc, tile_f, tile_b, totals, heard,
     ms, mr,
     parts, theirs, psums, near, full, rs_s, rs_r,
-    got, sums, got2, done, c_s, c_r, c_own, t_s, t_r, a_s, a_r,
-    fs, fr, ls, lr, as_, ar, in_s, stage_s, free,
+    data0, data1, data2, near0, near1, near2, next0, next1, next2, full0, full1, full2, last0, last1, last2,
+    done, c_s, c_r, t_s, t_r, a_s, a_r,
+    fs, fr, ls, lr, as_, ar, in_s, free,
 ):
     p, row, col, z, k = place()
     px, py = dp_place()
@@ -895,6 +940,8 @@
             copy.wait()
 
     collapses, trades, spreads = [], [], []
+    datas, nears, nexts = (data0, data1, data2), (near0, near1, near2), (next0, next1, next2)
+    fulls, lasts = (full0, full1, full2), (last0, last1, last2)
 
     def chunk(i):
         def at(half, x, y, part):
@@ -903,11 +950,8 @@
             which = pl.ds(2 * half, 2) if part is None else 2 * half + part
             return grads_o.at[i, xs, ys, which]
 
-        collapses.append(
-            Collapse(
-                i, local_o, got, sums, got2, done, c_s, c_r, c_own
-            )
-        )
+        b = i % BUFFERS
+        collapses.append(Collapse(i, datas[b], (nears[b], nexts[b]), (fulls[b], lasts[b]), done, c_s, c_r))
         trades.append(
             Trade(lambda c: done.at[i, c], lambda c: grads_o.at[i, px, py, c], t_s, t_r, (i,))
         )
@@ -941,18 +985,11 @@
         scatter.put(d)
 
     def weight_grads(i, first, second):
-        copies = [
-            pltpu.make_async_copy(stage.at[c % 2], local_o.at[i, :, :, c], stage_s.at[i, c]) for c in range(4)
-        ]
+        data = datas[i % BUFFERS]
         for c in range(4):
-            if c >= 2:
-                copies[c - 2].wait()
             cols = slice(c * TILE, (c + 1) * TILE)
-            stage[c % 2, :, :, :32] = first(cols).astype(BF).reshape(4, 4, 32, 512)
-            stage[c % 2, :, :, 32:] = second(cols).astype(BF).reshape(4, 4, 16, 512)
-            copies[c].start()
-        copies[2].wait()
-        copies[3].wait()
+            data[:, :, c, :32] = first(cols).astype(BF).reshape(4, 4, 32, 512)
+            data[:, :, c, 32:] = second(cols).astype(BF).reshape(4, 4, 16, 512)
         collapses[i].start()
 
     def gain_row(which):
@@ -961,11 +998,9 @@
     own_rows = pl.ds(pl.multiple_of(me * OWN, OWN), OWN)
 
     def stage_one(h2, g, ggu, hid, wg):
-        needed = [load(ggu_i, ggu), load(h2_i, h2), load(hid_i, hid), load(g_i, g)]
-        l_wg = load(wg_i, wg)
+        first_loads = [load(ggu_i, ggu), load(wg_i, wg)]
+        more_loads = [load(h2_i, h2), load(hid_i, hid), load(g_i, g)]
         meet(ring_friends() + [far] + xy_friends())
-        wait(needed)
-
         def grads(u):
             weight_grads(
                 u,
@@ -976,17 +1011,20 @@
         def product(rows, c, cols):
             return mm_t(ggu[rows], wg[c])
 
-        grads(0)
-        l_wg.wait()
+        wait(first_loads)
         project(2, product)
         project(1, product)
+        wait(more_loads)
+        grads(0)
         scatter.across()
         project(3, product)
         project(0, product)
-        grads(1)
+        collapses[0].mid()
         scatter.beside(0)
         scatter.beside(1)
+        grads(1)
         grads(2)
+        collapses[0].first()
 
     early = [load(mid_i, mid), load(gain_i, gain), load(x_i, x_own), load(g_i.at[own_rows], g_own)]
     pl.run_scoped(
@@ -1023,15 +1061,21 @@
         m_gather = Gather(rows_at(m), ms, mr)
         m_gather.start()
         release()
-        collapses[0].first()
+        collapses[1].mid()
+        collapses[2].mid()
+        collapses[0].mid(1)
         l_att.wait()
         for h in range(2):
             att_t[h * HEAD : (h + 1) * HEAD] = att[h].T
+        collapses[1].first()
         m_gather.forward()
         l_wo.wait()
         wait(l_heads)
         m_gather.share()
+        collapses[2].first()
         m_gather.finish()
+        collapses[0].second()
+        trades[0].start()
 
         @pl.loop(0, 4)
         def _(i):
@@ -1042,9 +1086,8 @@
             for h in range(2):
                 ga[h, rows] = back[:, h * HEAD : (h + 1) * HEAD].astype(BF)
 
-        collapses[1].first()
-        collapses[0].second()
-        trades[0].start()
+        collapses[1].mid(1)
+        collapses[2].mid(1)
         for block in range(GROUP // QROWS):
             first, keys = block * QROWS, (block + 1) * QROWS
             rows = pl.ds(first, QROWS)
@@ -1066,11 +1109,20 @@
                 dqkv[rows, cols] = back.astype(BF)
                 head_acc[0:1] += jnp.sum(gained, axis=0, keepdims=True)
 
-            if block == 1:
+            if block == 0:
                 trades[0].finish()
                 spreads[0].start(0)
+                collapses[1].second()
+                trades[1].start()
+            if block == 1:
+                spreads[0].pass_on(0)
+                collapses[2].second()
+                trades[2].start()
             if block == 2:
-                collapses[2].first()
+                spreads[0].wait(0)
+                spreads[0].start(1)
+                trades[1].finish()
+                spreads[1].start(0)
 
 
         @pl.loop(0, 4)
@@ -1082,7 +1134,11 @@
             dqkv[rows, 3 * HEAD :] = dv[rows].astype(BF)
             head_acc[1:2] += jnp.sum(gained, axis=0, keepdims=True)
 
+        trades[2].finish()
+        spreads[2].start(0)
         wait(l_last)
+        collapses[0].drain()
+        weight_grads(3, lambda cols: mm(h1t[cols], dqkv[...]), lambda cols: mm(att_t[...], m[:, cols]))
         pl.semaphore_wait(free, 3)
 
         def product(rows, c, cols):
@@ -1090,15 +1146,17 @@
 
         project(2, product)
         project(1, product)
-        weight_grads(3, lambda cols: mm(h1t[cols], dqkv[...]), lambda cols: mm(att_t[...], m[:, cols]))
-        spreads[0].pass_on(0)
+        spreads[0].pass_on(1)
+        spreads[1].pass_on(0)
         scatter.across()
         project(3, product)
         project(0, product)
-        collapses[1].second()
-        trades[1].start()
-        spreads[0].wait(0)
-        spreads[0].start(1)
+        spreads[2].pass_on(0)
+        collapses[3].mid()
+        scatter.beside(0)
+        scatter.beside(1)
+        spreads[1].wait(0)
+        spreads[1].start(1)
         m_gather.drain()
 
     pl.run_scoped(
@@ -1112,12 +1170,6 @@
 
     def stage_three(hid, wd):
         last = [load(hid_i, hid), load(wd_i, wd)]
-        scatter.beside(0)
-        scatter.beside(1)
-        collapses[2].second()
-        trades[2].start()
-        trades[1].finish()
-        spreads[1].start(0)
         gain_one = gain_row(0)
         scatter.arrive()
 
@@ -1152,10 +1204,8 @@
             totals[phase + 1] = total
 
         tell(0, [peer], [0])
-        trades[2].finish()
-        spreads[2].start(0)
         collapses[3].first()
-        spreads[1].pass_on(0)
+        spreads[2].wait(0)
         listen(0, [0])
         tell(1, [up, down, far], [1, 2, 3])
         wait(last)
@@ -1166,23 +1216,26 @@
 
         project(2, product)
         project(1, product)
-        spreads[0].pass_on(1)
-        spreads[1].wait(0)
-        spreads[1].start(1)
-        spreads[2].pass_on(0)
+        collapses[3].mid(1)
+        spreads[2].start(1)
         scatter.across()
         project(3, product)
         project(0, product)
+        spreads[1].pass_on(1)
+        collapses[3].second()
+        trades[3].start()
         listen(1, [1, 2, 3])
         tell(2, [along(0, o) for o in range(1, 4)], [4, 5, 6])
-        collapses[3].second()
-        trades[3].start()
         scatter.beside(0)
         scatter.beside(1)
-        spreads[2].wait(0)
-        spreads[2].start(1)
         trades[3].finish()
         spreads[3].start(0)
+        spreads[2].pass_on(1)
+        spreads[3].pass_on(0)
+        spreads[3].wait(0)
+        spreads[3].start(1)
+        listen(2, [4, 5, 6])
+        tell(3, [along(1, o) for o in range(1, 4)], [7, 8, 9])
         scatter.arrive()
 
         @pl.loop(0, OWN // 16)
@@ -1191,22 +1244,15 @@
             tile_b[rows] = (mid[rows] + scatter.total(pl.multiple_of(i * 16, 16), 16)).astype(BF)
 
         result_trade.start()
-        spreads[1].pass_on(1)
-        spreads[3].pass_on(0)
-        listen(2, [4, 5, 6])
-        tell(3, [along(1, o) for o in range(1, 4)], [7, 8, 9])
-        spreads[3].wait(0)
-        spreads[3].start(1)
-        spreads[2].pass_on(1)
+        spreads[3].pass_on(1)
+        listen(3, [7, 8, 9])
+        sums_o[...] = totals[4]
         stream_trade.finish()
         result_trade.finish()
-        listen(3, [7, 8, 9])
-        sums_o[...] = totals[4]
-        spreads[3].pass_on(1)
         for spread in spreads:
             spread.wait(1)
         scatter.drain()
-        for thing in collapses + trades + spreads + [stream_trade, result_trade]:
+        for thing in collapses[1:] + trades + spreads + [stream_trade, result_trade]:
             thing.drain()
         for copy in sent:
             copy.wait_send()
@@ -1222,12 +1268,12 @@
     grads = out((CHUNKS, 4, 4, 4, 48, 512), BF)
     return pl.pallas_call(
         backward_kernel,
-        out_shape=[out((TILE, TILE), BF), out((TILE, TILE), F32), grads, grads, out((8, WIDTH), F32)],
+        out_shape=[out((TILE, TILE), BF), out((TILE, TILE), F32), grads, out((8, WIDTH), F32)],
         in_specs=[hbm] * 20 + [vmem] * 2,
-        out_specs=[hbm] * 4 + [vmem],
+        out_specs=[hbm] * 3 + [vmem],
         scratch_shapes=[
             pltpu.VMEM((GROUP, WIDTH), BF), pltpu.VMEM((OWN, WIDTH), F32), pltpu.VMEM((GROUP, 512), BF),
-            pltpu.VMEM((2, 4, 4, 48, 512), BF), pltpu.VMEM((OWN, WIDTH), F32), pltpu.VMEM((4, 8, TILE), F32),
+            pltpu.VMEM((OWN, WIDTH), F32), pltpu.VMEM((4, 8, TILE), F32),
             pltpu.VMEM((OWN, WIDTH), BF), pltpu.VMEM((OWN, WIDTH), BF), pltpu.VMEM((2, 16, WIDTH), F32),
             pltpu.VMEM((8, HEAD), F32), pltpu.VMEM((OWN, WIDTH), F32), pltpu.VMEM((OWN, WIDTH), BF),
             pltpu.VMEM((5, 8, WIDTH), F32), pltpu.VMEM((10, 8, WIDTH), F32),
@@ -1236,8 +1282,7 @@
         + scatter_scratch()
         + collapse_scratch()
         + [
-            dma((3,)), dma((4,)), dma((3,)), dma((4,)), dma((10,)), dma((10,)), dma((24,)), dma((CHUNKS, 4)),
-            pltpu.SemaphoreType.REGULAR,
+            dma((3,)), dma((4,)), dma((3,)), dma((4,)), dma((10,)), dma((10,)), dma((24,)), pltpu.SemaphoreType.REGULAR,
         ],
         compiler_params=pltpu.CompilerParams(
             collective_id=2, has_side_effects=True, vmem_limit_bytes=VMEM_LIMIT
@@ -1247,11 +1292,19 @@
     )(*args)
 
 
-def place_big_kernel(grads, result, stream, totals, gate_up, down, result_o, stream_o, one, two, head):
-    value = grads[0, :, 0, :32].reshape(TILE, 512).astype(F32)
-    for g in range(2):
-        gate_up[:, g, :] = value[:, g * 256 : (g + 1) * 256]
-    down[...] = grads[0, :, 0, 32:].reshape(256, TILE).astype(F32)
+PLACE = 4
+
+
+def place_kernel(grads, result, stream, totals, gate_up, down, qkv, out, result_o, stream_o, one, two, head):
+    for c in range(4):
+        for u in range(3):
+            t = c * 3 + u
+            value = grads[u, :, c, :32].reshape(PLACE * 32, 512).astype(F32)
+            for g in range(2):
+                gate_up[:, g, t * 256 : (t + 1) * 256] = value[:, g * 256 : (g + 1) * 256]
+            down[t] = grads[u, :, c, 32:].astype(F32)
+        qkv[:, c, :] = grads[3, :, c, :32].reshape(PLACE * 32, 512).astype(F32)
+        out[c] = grads[3, :, c, 32:].astype(F32)
     result_o[...] = result[...]
     stream_o[...] = stream[...]
     one[...] = totals[0:1]
@@ -1259,82 +1312,59 @@
     head[...] = totals[2:3, : 2 * HEAD]
 
 
-def place_big(grads, result, stream, totals):
-    rows = pl.BlockSpec((OWN, TILE), lambda c, u: (c, 0))
+def place_grads(grads, result, stream, totals):
+    tile = pl.BlockSpec((32 * PLACE, TILE), lambda p: (p, 0))
 
     def whole(*shape):
-        return pl.BlockSpec(shape, lambda c, u: (0, 0))
+        return pl.BlockSpec(shape, lambda p: (0,) * len(shape))
 
     return pl.pallas_call(
-        place_big_kernel,
-        grid=(4, 3),
+        place_kernel,
+        grid=(DP // PLACE,),
         in_specs=[
-            pl.BlockSpec((1, DP, 1, 48, 512), lambda c, u: (u, 0, c, 0, 0)), rows, rows, whole(8, WIDTH),
+            pl.BlockSpec((CHUNKS, PLACE, 4, 48, 512), lambda p: (0, p, 0, 0, 0)), tile, tile, whole(8, WIDTH),
         ],
         out_specs=[
-            pl.BlockSpec((TILE, 2, 256), lambda c, u: (0, 0, c * 3 + u)),
-            pl.BlockSpec((256, TILE), lambda c, u: (c * 3 + u, 0)),
-            rows, rows, whole(1, WIDTH), whole(1, WIDTH), whole(1, 2 * HEAD),
+            pl.BlockSpec((32 * PLACE, 2, 4 * UNITS), lambda p: (p, 0, 0)),
+            pl.BlockSpec((12, PLACE, 16, TILE), lambda p: (0, p, 0, 0)),
+            pl.BlockSpec((32 * PLACE, 4, 512), lambda p: (p, 0, 0)),
+            pl.BlockSpec((4, PLACE, 16, TILE), lambda p: (0, p, 0, 0)),
+            tile, tile, whole(1, WIDTH), whole(1, WIDTH), whole(1, 2 * HEAD),
         ],
         out_shape=[
             jax.ShapeDtypeStruct((TILE, 2, 4 * UNITS), F32),
-            jax.ShapeDtypeStruct((4 * UNITS, TILE), F32),
+            jax.ShapeDtypeStruct((12, DP, 16, TILE), F32),
+            jax.ShapeDtypeStruct((TILE, 4, 512), F32),
+            jax.ShapeDtypeStruct((4, DP, 16, TILE), F32),
             jax.ShapeDtypeStruct((TILE, TILE), BF),
             jax.ShapeDtypeStruct((TILE, TILE), F32),
             jax.ShapeDtypeStruct((1, WIDTH), F32),
             jax.ShapeDtypeStruct((1, WIDTH), F32),
             jax.ShapeDtypeStruct((1, 2 * HEAD), F32),
         ],
-        compiler_params=pltpu.CompilerParams(vmem_limit_bytes=40 * 1024 * 1024),
-        cost_estimate=pl.CostEstimate(flops=0, bytes_accessed=32_000_000, transcendentals=0),
-        name="place_big",
+        compiler_params=pltpu.CompilerParams(vmem_limit_bytes=VMEM_LIMIT),
+        cost_estimate=pl.CostEstimate(flops=0, bytes_accessed=41_000_000, transcendentals=0),
+        name="place",
     )(grads, result, stream, totals)
-
-
-def place_small_kernel(grads, qkv, out):
-    for c in range(4):
-        qkv[:, c, :] = grads[0, :, c, :32].reshape(128, 512).astype(F32)
-        out[c] = grads[0, :, c, 32:].reshape(64, TILE).astype(F32)
-
-
-def place_small(grads):
-    return pl.pallas_call(
-        place_small_kernel,
-        grid=(4,),
-        in_specs=[pl.BlockSpec((1, 4, 4, 48, 512), lambda i: (3, i, 0, 0, 0))],
-        out_specs=[
-            pl.BlockSpec((128, 4, 512), lambda i: (i, 0, 0)),
-            pl.BlockSpec((4, 64, TILE), lambda i: (0, i, 0)),
-        ],
-        out_shape=[
-            jax.ShapeDtypeStruct((TILE, 4, 512), F32),
-            jax.ShapeDtypeStruct((4, 256, TILE), F32),
-        ],
-        compiler_params=pltpu.CompilerParams(vmem_limit_bytes=40 * 1024 * 1024),
-        cost_estimate=pl.CostEstimate(flops=0, bytes_accessed=9_000_000, transcendentals=0),
-        name="place_small",
-    )(grads)
 
 
 def body(
     tokens, norm1_gain, w_qkv, q_gain, k_gain, w_out, norm2_gain, w_gate_up, w_down, out_grad,
     seq_lengths, seq_group, seq_start,
 ):
-    (h2, g, wq, wo, wg, wd, h1t, raw, qs, ks, att, lse, middle, gain, x_own, start, cosine, sine) = forward_call(
+    (h2, g, wq, wo, wg, wd, h1t, raw, qs, ks, att, lse, middle, gain, x_own, start, cosine, sine, ggu, hid) = forward_call(
         tokens, out_grad, norm1_gain[None], norm2_gain[None], q_gain[None], k_gain[None], jnp.asarray(FREQ),
         seq_lengths, seq_group, seq_start, w_qkv, w_gate_up,
-        w_out.reshape(4, 4, 4, 16, TILE), w_down.reshape(4, 4, 4, 48, TILE),
+        w_out.reshape(4, 4, 4, 16, TILE), w_down.reshape(4, 3, 4, 4, 16, TILE),
     )
     wg = wg.reshape(4, TILE, 2 * UNITS)
     wd = wd.reshape(4, UNITS, TILE)
-    ggu, hid = middle_call(h2, g, wg, wd)
-    result, stream, grads, _, totals = backward_call(
+    result, stream, grads, totals = backward_call(
         h2, ggu, hid, g, wg, wd, wo.reshape(4, 256, TILE), wq.reshape(4, TILE, 512), h1t, raw, qs, ks, att, lse,
         middle, gain, x_own, start, cosine, sine, q_gain[None], k_gain[None],
     )
     grads = grads.reshape(CHUNKS, DP, 4, 48, 512)
-    g_gate_up, g_down, result, stream, one, two, head = place_big(grads, result, stream, totals)
-    g_qkv, g_out = place_small(grads)
+    g_gate_up, g_down, g_qkv, g_out, result, stream, one, two, head = place_grads(grads, result, stream, totals)
     return (
         result,
         stream,
@@ -1345,7 +1375,7 @@
         g_out.reshape(w_out.shape),
         two.reshape(WIDTH),
         g_gate_up,
-        g_down,
+        g_down.reshape(w_down.shape),
     )
 
 

time: 338 us -> 301 us (0.89)
  Pallas kernels: 327 us -> 296 us
  local copies, waits for them, and re-layouts: 9.67 us -> 1.12 us
    pallas_call x1, Pallas kernels: 191 us -> 175 us  [backward_call(): pl.pallas_call(backward_kernel, out_shape=[out((TILE, TILE), BF), out((TI...]
    pallas_call x3 -> x1, Pallas kernels: 30.7 us -> 15.6 us  [place_grads(): pl.pallas_call(place_kernel, grid=(DP // PLACE,), in_specs=[pl.BlockSpec(...]
    unnamed x10 -> x0, local copies, waits for them, and re-layouts: 9.15 us -> none
where the time goes in v4:
time: 301 us; the launch traced here: 298 us
  Pallas kernels  296 us (98%)
    pallas_call x1, Pallas kernels, backward_call(): pl.pallas_call(backward_kernel, out_shape=[out((TILE, TILE), BF), out((TI...  175 us
    pallas_call x1, Pallas kernels, forward_call(): pl.pallas_call(forward_kernel, out_shape=[out(wide), out(wide), out((4, 4...  105 us
    pallas_call x1, Pallas kernels, place_grads(): pl.pallas_call(place_kernel, grid=(DP // PLACE,), in_specs=[pl.BlockSpec(...  15.6 us

profile of v4, /device:TPU:0, one launch (start us, length us, event | category | flops | bytes accessed | tf_op | source)
XLA Modules:
  0.0 297.6 jit_solution(1543447253605006358)
XLA Ops:
  0.6 104.7 %forward.1 = (bf16[1024,2048]{1,0:T(8,128)(2,1)}, bf16[1024,2048]{1,0:T(8,128)(2,1)}, bf16[4,4,4,32,512]{4,3,2,1,0:T(8,128)(2,1)}, bf16[4,4,4,16,512]{4,3,2,1,0:...) custom-call(bf16[512,512]{1,0:T(8,128)(2,1)} %tok.1, ...), custom_call_target="tpu_custom_call" | custom-call | flops 14000000000 | bytes 60000000 | tf_op jit(solution)/shard_map/forward/pallas_call | solution.py:731
  105.4 175.3 %backward.1 = (bf16[512,512]{1,0:T(8,128)(2,1)}, f32[512,512]{1,0:T(8,128)}, bf16[4,4,4,4,48,512]{5,4,3,2,1,0:T(8,128)(2,1)}, f32[8,2048]{1,0:T(8,128)}) custom-call(bf16[1024,2048]{1,0:T(8,128)(2,1)} %get-tuple-element.43.h2_i, bf16[1024,1536]{1,0:T(8,128)(2,1)} %get-tuple-element.44.ggu_i, bf16[1024,768]{1,0:T(8,128)(2,1)} %get-tuple-element.45.hid_i, ...), custom_call_target="tpu_custom_call" | custom-call | flops 24999999488 | bytes 100000000 | tf_op jit(solution)/shard_map/backward/pallas_call | solution.py:1269
  280.6 15.6 %place.1 = (f32[512,2,3072]{2,1,0:T(2,128)}, f32[12,16,16,512]{3,2,1,0:T(8,128)}, f32[512,4,512]{2,1,0:T(4,128)}, f32[4,16,16,512]{3,2,1,0:T(8,128)}, bf16[512,5...) custom-call(bf16[4,16,4,48,512]{4,3,2,1,0:T(8,128)(2,1)} %bitcast.19, ...), custom_call_target="tpu_custom_call" | custom-call | bytes 41000000 | tf_op jit(solution)/shard_map/place/pallas_call | solution.py:1321
  296.3 1.1 slice_bitcast_fusion
